TPU v7x, 32 devices: a whole 2x2x4 slice. The times are simulated.
32 devices in a mesh: slab: 4 (over x, core), seq: 8 (over z, y).
Axes of the slice: x: 2, y: 2, z: 4, core: 2. Of those that a mesh axis runs over, the one named last changes fastest.
Arguments:
- stream: bfloat16 [4, 384, 1536], P('slab', 'seq'), may hold values from -40 to 40
- latents: float32 [4, 384, 64], P('slab', 'seq'), may hold values from -6 to 6
- time_mod: float32 [4, 3, 1536], P('slab'), may hold values from -4 to 4
- block_mod: float32 [3, 1536], replicated, may hold values from -4 to 4
- w_qkv: bfloat16 [1536, 3072], P(None, 'seq'), may hold values from -0.15625 to 0.15625
- qk_gain: float32 [2, 1024], replicated, may hold values from 0.5 to 9
- w_out: bfloat16 [1024, 1536], replicated, may hold values from -0.1875 to 0.1875
- head_mod: float32 [4, 2, 1536], P('slab'), may hold values from -4 to 4
- w_head: bfloat16 [1536, 64], replicated, may hold values from -0.15625 to 0.15625
- noise_level: int32 [4], P('slab'), may hold values from 1 to 32, as said below
Outputs:
- new_stream: bfloat16 [4, 384, 1536], P('slab', 'seq')
- next_latents: float32 [4, 384, 64], P('slab', 'seq')
Inputs may be any that keep to these rules, and one draw needn't show every extreme that they name: noise_level rises strictly along the groups; the first group has level 1 and the last has level 32.
All inputs are finite; a program needn't handle non-finite values.
Results may differ from a plain program's by a relative error of at most 0.0056.
The roundings to bfloat16 on the way count: a program that leaves them out, or rounds other values in their place, can miss the bound.
Values may be sent and summed in bfloat16 or wider, within the bound.
No kernel may reach another device: no remote copies, remote signals or barrier semaphores. Data moves between devices by JAX's collectives and lax.ppermute only.
A program may use at most 128 MiB of HBM per device.

v0:
```python
import jax
import jax.numpy as jnp
from jax import lax
from jax.sharding import PartitionSpec as P

HEADS = 8
HEAD_DIM = 128
LEVELS = 32
TOK_DEV = 48
ATT = 1024


def from_behind(value, axis, steps):
    count = lax.axis_size(axis)
    pairs = [(source, (source + steps) % count) for source in range(count)]
    return lax.ppermute(value, axis, pairs)


def layer_norm(values):
    center = values - jnp.mean(values, axis=-1, keepdims=True)
    spread = jnp.mean(center * center, axis=-1, keepdims=True)
    return center * lax.rsqrt(spread + 1e-06)


def sigma_table():
    fraction = jnp.arange(LEVELS + 1).astype(jnp.float32) / LEVELS
    return 5.0 * fraction / (1.0 + 4.0 * fraction)


def norm_rope(values, gain_row, position):
    row_count = values.shape[0]
    floats = values.astype(jnp.float32)
    scaled = (
        floats * lax.rsqrt(jnp.mean(floats * floats, axis=-1, keepdims=True) + 1e-06) * gain_row
    )
    halves = HEAD_DIM // 2
    scaled = scaled.reshape(row_count, HEADS, HEAD_DIM)
    frequency = jnp.power(10000.0, -jnp.arange(halves).astype(jnp.float32) / halves)
    angles = position[:, None, None] * frequency[None, None, :]
    cosines = jnp.cos(angles)
    sines = jnp.sin(angles)
    front_half = scaled[..., :halves]
    back_half = scaled[..., halves:]
    turned = jnp.concatenate(
        [front_half * cosines - back_half * sines, front_half * sines + back_half * cosines],
        axis=-1,
    )
    return turned.reshape(row_count, ATT).astype(jnp.bfloat16)


def group_parts(queries, key_rows, value_rows):
    row_count = queries.shape[0]
    key_count = key_rows.shape[0]
    query_heads = queries.reshape(row_count, HEADS, HEAD_DIM).transpose(1, 0, 2)
    key_heads = key_rows.reshape(key_count, HEADS, HEAD_DIM).transpose(1, 0, 2)
    value_heads = value_rows.reshape(key_count, HEADS, HEAD_DIM).transpose(1, 0, 2)

    def one_head(operands):
        query_part, key_part, value_part = operands
        scores = jnp.einsum(
            "rd,kd->rk", query_part, key_part, preferred_element_type=jnp.float32
        ) * HEAD_DIM ** (-0.5)
        maxima = jnp.max(scores, axis=-1)
        weights = jnp.exp(scores - maxima[:, None]).astype(jnp.bfloat16)
        totals = jnp.sum(weights.astype(jnp.float32), axis=-1)
        output = jnp.dot(weights, value_part, preferred_element_type=jnp.float32)
        return (output, maxima, totals)

    output, maxima, totals = lax.map(one_head, (query_heads, key_heads, value_heads))
    return (output.transpose(1, 0, 2).reshape(row_count, ATT), maxima.T, totals.T)


def local(
    stream, latents, time_mod, block_mod, w_qkv, qk_gain, w_out, head_mod, w_head, noise_level
):
    slab_count = lax.axis_size("slab")
    seq_count = lax.axis_size("seq")
    slab_index = lax.axis_index("slab")
    seq_index = lax.axis_index("seq")
    group_rows = TOK_DEV * seq_count
    hidden = stream[0].astype(jnp.float32)
    modulation = block_mod + time_mod[0]
    modded = (layer_norm(hidden) * (1.0 + modulation[1]) + modulation[0]).astype(jnp.bfloat16)
    columns = jnp.dot(
        lax.all_gather(modded, "seq", axis=0, tiled=True), w_qkv, preferred_element_type=jnp.float32
    ).astype(jnp.bfloat16)
    own_position = (slab_index * group_rows + seq_index * TOK_DEV + jnp.arange(TOK_DEV)).astype(
        jnp.float32
    )
    full_mixed = lax.all_gather(columns, "seq", axis=1, tiled=True)
    own_mixed = lax.dynamic_slice_in_dim(full_mixed, seq_index * TOK_DEV, TOK_DEV, 0)
    own_queries = norm_rope(own_mixed[:, :ATT], qk_gain[0], own_position)
    group_position = (slab_index * group_rows + jnp.arange(group_rows)).astype(jnp.float32)
    group_keys = norm_rope(full_mixed[:, ATT : 2 * ATT], qk_gain[1], group_position)
    group_values = full_mixed[:, 2 * ATT :]
    all_queries = lax.all_gather(own_queries[None], "slab", axis=0, tiled=True)
    slab_ids = jnp.arange(slab_count)
    output, maxima, totals = group_parts(
        all_queries.reshape(slab_count * TOK_DEV, ATT), group_keys, group_values
    )
    usable = (slab_ids >= slab_index)[:, None, None]
    output = jnp.where(usable, output.reshape(slab_count, TOK_DEV, ATT), 0.0)
    maxima = jnp.where(usable, maxima.reshape(slab_count, TOK_DEV, HEADS), -1e30)
    totals = jnp.where(usable, totals.reshape(slab_count, TOK_DEV, HEADS), 0.0)
    recv_out, recv_max, recv_sum = (
        lax.all_to_all(output, "slab", split_axis=0, concat_axis=0, tiled=True),
        lax.all_to_all(maxima, "slab", split_axis=0, concat_axis=0, tiled=True),
        lax.all_to_all(totals, "slab", split_axis=0, concat_axis=0, tiled=True),
    )
    highest = jnp.max(recv_max, axis=0)
    weights = jnp.exp(recv_max - highest)
    total_sum = jnp.sum(recv_sum * weights, axis=0)
    accum = jnp.sum(
        recv_out.reshape(slab_count, TOK_DEV, HEADS, HEAD_DIM) * weights[..., None], axis=0
    )
    attended = (accum / total_sum[..., None]).reshape(TOK_DEV, ATT).astype(jnp.bfloat16)
    projected = jnp.dot(attended, w_out, preferred_element_type=jnp.float32)
    updated = hidden + modulation[2] * projected
    head_in = (layer_norm(updated) * (1.0 + head_mod[0, 1]) + head_mod[0, 0]).astype(jnp.bfloat16)
    velocity = jnp.dot(head_in, w_head, preferred_element_type=jnp.float32)
    table = sigma_table()
    level_ids = jnp.arange(LEVELS + 1)
    current_level = noise_level[0]
    sigma_now = jnp.sum(jnp.where(level_ids == current_level, table, 0.0))
    sigma_next = jnp.sum(jnp.where(level_ids == current_level - 1, table, 0.0))
    stepped = latents[0] + (sigma_next - sigma_now) * velocity
    moved = from_behind(stepped[None], "slab", -1)
    return (updated.astype(jnp.bfloat16)[None], moved)


def solution(mesh):
    in_specs = (
        P("slab", "seq", None),
        P("slab", "seq", None),
        P("slab", None, None),
        P(),
        P(None, "seq"),
        P(),
        P(),
        P("slab", None, None),
        P(),
        P("slab"),
    )
    out_specs = (P("slab", "seq", None), P("slab", "seq", None))
    return jax.shard_map(local, mesh=mesh, in_specs=in_specs, out_specs=out_specs, check_vma=False)
```

profile of v0, /device:TPU:1, one launch (start us, length us, event | category | flops | bytes accessed | tf_op | source)
XLA Modules:
  0.0 204.6 jit_solution(3559094238035976868)
XLA Ops:
  10.4 1.7 fusion.21
  12.2 42.0 %all-gather.3.cloned.1.call-done = bf16[384,1536]{1,0:T(8,128)(2,1)} async-done(((bf16[48,1536]{1,0:T(8,128)(2,1)}), bf16[384,1536]{1,0:T(8,128)(2,1)}) %all-gather.3.cloned.1.call-update) | async-done | bytes 1179664 | tf_op jit(solution)/shard_map/all_gather | solution.py:85
  54.1 3.1 %convolution_convert_fusion = bf16[384,384]{1,0:T(8,128)(2,1)} fusion(bf16[384,1536]{1,0:T(8,128)(2,1)} %all-gather.3.cloned.1.call-done, bf16[1536,384]{1,0:T(8,128)(2,1)} %param.16), kind=kOutput, calls=%fused_computation.22 | convolution fusion | flops 453132288 | bytes 2654208 | tf_op jit(solution)/shard_map/dot_general | solution.py:84
  59.5 51.3 %all-gather.5.cloned.1.call-done = bf16[384,3072]{1,0:T(8,128)(2,1)} async-done(((bf16[384,384]{1,0:T(8,128)(2,1)}), bf16[384,3072]{1,0:T(8,128)(2,1)}) %all-gather.5.cloned.1.call-update) | async-done | bytes 2359312 | tf_op jit(solution)/shard_map/all_gather | solution.py:90
  111.8 1.4 fusion.10
  115.7 1.6 convert_element_type.82
  117.3 7.6 %all_gather.11 = bf16[4,48,1024]{2,1,0:T(8,128)(2,1)S(1)} all-gather(bf16[1,48,1024]{2,1,0:T(8,128)(2,1)} %convert_element_type.82), channel_id=1, replica_groups=mesh['slab'=4,'seq'=8] {'slab'}, dimensions={0}, use_global_device_ids=true | all-gather | bytes 491520 | tf_op jit(solution)/shard_map/all_gather | solution.py:96
  125.8 1.4 fusion.12
  128.6 1.3 maximum_bitcast_fusion
  129.9 2.2 %bitcast_bitcast_fusion = bf16[8,384,128]{2,1,0:T(8,128)(2,1)} fusion(bf16[384,3072]{1,0:T(8,128)(2,1)} %all-gather.5.cloned.1.call-done), kind=kLoop, calls=%fused_computation.26 | loop fusion | bytes 1572864 | tf_op jit(solution)/shard_map/transpose | solution.py:56
  132.1 26.5 %while.14 = (s32[]{:T(128)}, f32[8,192,128]{2,1,0:T(8,128)}, f32[8,192]{1,0:T(8,128)S(1)}, f32[8,192]{1,0:T(8,128)S(1)}, bf16[8,192,128]{2,1,0:T(8,128)(2,1)}, /...) while((s32[]{:T(128)}, f32[8,192,128]{2,1,0:T(8,128)}, ...), condition=%wide.region_7.8_spmd, body=%wide.region_4.7_spmd.sunk | while | flops 38338176 | bytes 1237101 | solution.py:69
  132.1 1.2 fusion.46
  133.6 1.8 fusion.47
  135.4 1.2 fusion.46
  137.0 1.8 fusion.47
  140.3 1.8 fusion.47
  142.1 1.2 fusion.46
  143.6 1.8 fusion.47
  146.9 1.8 fusion.47
  150.2 1.8 fusion.47
  153.5 1.8 fusion.47
  156.8 1.8 fusion.47
  159.5 3.4 %all-to-all-start.1 = ((f32[4,1,384]{2,1,0:T(1,128)}), f32[4,1,384]{2,1,0:T(1,128)S(1)}, u32[]{:S(2)}, u32[]{:S(2)}) async-start(f32[4,1,384]{2,1,0:T(1,128)} %reshape.240), calls=%async_computation.1 | async-start | bytes 12288 | tf_op jit(solution)/shard_map/all_to_all | solution.py:107
  162.9 2.5 %copy.34 = f32[192,8,128]{2,1,0:T(8,128)} copy(f32[192,8,128]{2,0,1:T(8,128)} %bitcast.119) | data formatting | bytes 1572864 | tf_op jit(solution)/shard_map/transpose | solution.py:70
  165.4 2.1 %reshape_reshape.7 = f32[4,48,1024]{2,1,0:T(8,128)} reshape(f32[192,8,128]{2,1,0:T(8,128)} %copy.34) | data formatting | bytes 1572864 | tf_op jit(solution)/shard_map/reshape;reshape | solution.py:102
  168.2 3.3 %all-to-all-start.2 = ((f32[4,1,384]{2,1,0:T(1,128)}), f32[4,1,384]{2,1,0:T(1,128)S(1)}, u32[]{:S(2)}, u32[]{:S(2)}) async-start(f32[4,1,384]{2,1,0:T(1,128)} %reshape.242), calls=%async_computation.2 | async-start | bytes 12288 | tf_op jit(solution)/shard_map/all_to_all | solution.py:108
  171.5 2.2 %broadcast_select_fusion = f32[4,48,1024]{2,1,0:T(8,128)} fusion(f32[4,48,1024]{2,1,0:T(8,128)} %reshape_reshape.7, pred[4]{0:T(512)(128)(4,1)S(1)} %copy-done.11), kind=kLoop, calls=%fused_computation.30 | loop fusion | flops 196608 | bytes 1572868 | tf_op jit(solution)/shard_map/jit(_where)/select_n | solution.py:102
  174.6 4.8 %all-to-all-start = ((f32[4,48,1024]{2,1,0:T(8,128)}), f32[4,48,1024]{2,1,0:T(8,128)}, u32[]{:S(2)}, u32[]{:S(2)}) async-start(f32[4,48,1024]{2,1,0:T(8,128)} %broadcast_select_fusion), calls=%async_computation | async-start | bytes 1572864 | tf_op jit(solution)/shard_map/all_to_all | solution.py:106
  185.5 2.2 %mul.278 = f32[4,48,1024]{2,1,0:T(8,128)} reshape(f32[4,48,8,128]{3,2,1,0:T(8,128)} %mul.277) | data formatting | bytes 1572864 | tf_op jit(solution)/shard_map/mul | solution.py:114
  187.7 2.6 %all-to-all-done = f32[4,48,1024]{2,1,0:T(8,128)} async-done(((f32[4,48,1024]{2,1,0:T(8,128)}), f32[4,48,1024]{2,1,0:T(8,128)}, u32[]{:S(2)}, u32[]{:S(2)}) %all-to-all-start) | async-done | bytes 786464 | tf_op jit(solution)/shard_map/all_to_all | solution.py:106
  190.4 1.5 multiply_reduce_fusion
  194.7 2.4 %collective-permute-done = f32[1,48,64]{2,1,0:T(8,128)S(1)} collective-permute-done((f32[1,48,64]{2,1,0:T(8,128)S(1)}, f32[1,48,64]{2,1,0:T(8,128)S(1)}, u32[]{:S(2)}, u32[]{:S(2)}) %collective-permute-start) | collective-permute-done | bytes 12320 | tf_op jit(solution)/shard_map/ppermute | solution.py:16
  (114 shorter events, 29.7 us)
Async XLA Ops:
  7.2 184.8 %copy-start = (bf16[1024,1536]{1,0:T(8,128)(2,1)S(1)}, bf16[1024,1536]{1,0:T(8,128)(2,1)}, u32[]{:S(2)}) copy-start(bf16[1024,1536]{1,0:T(8,128)(2,1)} %param.18) | copy-start | bytes 9437188
  7.2 47.0 %all-gather.3.cloned.1.call-start = ((), (), s32[]{:S(2)}) async-start(), calls=%async_computation.3 | async-start | bytes 1327104 | tf_op jit(solution)/shard_map/all_gather | solution.py:85
  12.1 45.8 %copy-start.9 = (f32[2,1024]{1,0:T(2,128)S(1)}, f32[2,1024]{1,0:T(2,128)}, u32[]{:S(2)}) copy-start(f32[2,1024]{1,0:T(2,128)} %param.17) | copy-start | bytes 24580
  12.1 98.7 %all-gather.5.cloned.1.call-start = ((), (), s32[]{:S(2)}) async-start(), calls=%async_computation.4 | async-start | bytes 2654208 | tf_op jit(solution)/shard_map/all_gather | solution.py:90
  110.8 4.0 %copy-start.3 = (f32[48,64]{1,0:T(8,128)S(1)}, f32[48,64]{1,0:T(8,128)}, u32[]{:S(2)}) copy-start(f32[48,64]{1,0:T(8,128)} %get-tuple-element.100) | copy-start | bytes 36868
  110.8 4.0 %copy-start.4 = (f32[48,64]{1,0:T(8,128)S(1)}, f32[48,64]{1,0:T(8,128)}, u32[]{:S(2)}) copy-start(f32[48,64]{1,0:T(8,128)} %get-tuple-element.101) | copy-start | bytes 36868
  114.9 10.9 %copy-start.10 = (f32[384]{0:T(512)S(1)}, f32[384]{0:T(512)}, u32[]{:S(2)}) copy-start(f32[384]{0:T(512)} %add_rsqrt_fusion) | copy-start | bytes 4612
  128.6 3.5 %copy-start.7 = (f32[8,192]{1,0:T(8,128)S(1)}, f32[8,192]{1,0:T(8,128)}, u32[]{:S(2)}) copy-start(f32[8,192]{1,0:T(8,128)} %custom-call.2) | copy-start | bytes 18436
  128.6 3.5 %copy-start.8 = (f32[8,192]{1,0:T(8,128)S(1)}, f32[8,192]{1,0:T(8,128)}, u32[]{:S(2)}) copy-start(f32[8,192]{1,0:T(8,128)} %custom-call.1) | copy-start | bytes 18436
  132.1 26.7 %copy-start.11 = (pred[4]{0:T(512)(128)(4,1)S(1)}, pred[4]{0:T(512)(128)(4,1)}, u32[]{:S(2)}) copy-start(pred[4]{0:T(512)(128)(4,1)} %iota_compare_fusion) | copy-start | bytes 16
  159.5 8.7 %all-to-all-start.1 = ((f32[4,1,384]{2,1,0:T(1,128)}), f32[4,1,384]{2,1,0:T(1,128)S(1)}, u32[]{:S(2)}, u32[]{:S(2)}) async-start(f32[4,1,384]{2,1,0:T(1,128)} %reshape.240), calls=%async_computation.1 | async-start | bytes 12288 | tf_op jit(solution)/shard_map/all_to_all | solution.py:107
  168.2 6.4 %all-to-all-start.2 = ((f32[4,1,384]{2,1,0:T(1,128)}), f32[4,1,384]{2,1,0:T(1,128)S(1)}, u32[]{:S(2)}, u32[]{:S(2)}) async-start(f32[4,1,384]{2,1,0:T(1,128)} %reshape.242), calls=%async_computation.2 | async-start | bytes 12288 | tf_op jit(solution)/shard_map/all_to_all | solution.py:108
  171.5 10.6 %copy-start.6 = (f32[1,2,1536]{2,1,0:T(2,128)S(1)}, f32[1,2,1536]{2,1,0:T(2,128)}, u32[]{:S(2)}) copy-start(f32[1,2,1536]{2,1,0:T(2,128)} %param.19) | copy-start | bytes 36868
  174.6 15.7 %all-to-all-start = ((f32[4,48,1024]{2,1,0:T(8,128)}), f32[4,48,1024]{2,1,0:T(8,128)}, u32[]{:S(2)}, u32[]{:S(2)}) async-start(f32[4,48,1024]{2,1,0:T(8,128)} %broadcast_select_fusion), calls=%async_computation | async-start | bytes 1572864 | tf_op jit(solution)/shard_map/all_to_all | solution.py:106
  185.5 6.5 %copy-start.1 = (bf16[1,48,1536]{2,1,0:T(8,128)(2,1)S(1)}, bf16[1,48,1536]{2,1,0:T(8,128)(2,1)}, u32[]{:S(2)}) copy-start(bf16[1,48,1536]{2,1,0:T(8,128)(2,1)} %param.12) | copy-start | bytes 442372
  192.0 1.6 copy-start.2
  192.0 1.6 copy-start.5
  193.8 3.3 %collective-permute-start = (f32[1,48,64]{2,1,0:T(8,128)S(1)}, f32[1,48,64]{2,1,0:T(8,128)S(1)}, u32[]{:S(2)}, u32[]{:S(2)}) collective-permute-start(f32[1,48,64]{2,1,0:T(8,128)S(1)} %fusion.14), channel_id=1, source_target_pairs={{0,24},{8,0},{16,8},{24,16},{1,25},{9,1},{17,9},{25,17},{2,26},{10... | collective-permute-start | bytes 36872 | tf_op jit(solution)/shard_map/ppermute | solution.py:16
Sparse Core Ops, SparseCore 0:
  12.2 41.8 all-gather.2
  57.4 53.3 all-gather.4
where the time goes:
time: 206 us; the launch traced here: 205 us
  waiting for transfers between devices  99.2 us (48%)
  matrix products  28.1 us (14%)
  other arithmetic  23.4 us (11%)
  local copies, waits for them, and re-layouts  17.3 us (8%)
  between operations  16.3 us (8%)
  starting transfers between devices  12.5 us (6%)
  blocking collectives  7.55 us (4%)
    all_gather x1, waiting for transfers between devices, local(): full_mixed = lax.all_gather(columns, 'seq', axis=1, tiled=True)  51.3 us
    all_gather x1, waiting for transfers between devices, local(): lax.all_gather(modded, 'seq', axis=0, tiled=True)  42 us
    dot_general x8, matrix products, one_head(): output = jnp.dot(weights, value_part, preferred_element_type=jnp.float32)  14.3 us
    dot_general x8, matrix products, one_head(): jnp.einsum('rd,kd->rk', query_part, key_part, preferred_element_type=jnp....  9.77 us
    all_gather x1, blocking collectives, local(): all_queries = lax.all_gather(own_queries[None], 'slab', axis=0, tiled=True)  7.55 us
    all_to_all x1, starting transfers between devices, local(): lax.all_to_all(output, 'slab', split_axis=0, concat_axis=0, tiled=True)  4.85 us
  transfers between devices with their start and end apart: 6, of which 5 were waited for; matrix products, arithmetic and copies ran while one was open for 8% of the time, Pallas kernels for 0%

commit v1 on v0

--- a/solution.py
+++ b/solution.py
@@ -1,6 +1,10 @@
+import functools
+
 import jax
 import jax.numpy as jnp
 from jax import lax
+from jax.experimental import pallas as pl
+from jax.experimental.pallas import tpu as pltpu
 from jax.sharding import PartitionSpec as P
 
 HEADS = 8
@@ -8,6 +12,14 @@
 LEVELS = 32
 TOK_DEV = 48
 ATT = 1024
+D = 1536
+CHAN = 64
+PAIR = 2 * HEAD_DIM
+LINE = 4
+ROWS = LINE * TOK_DEV
+BF16 = jnp.bfloat16
+F32 = jnp.float32
+VMEM_LIMIT = 40 * 1024 * 1024
 
 
 def from_behind(value, axis, steps):
@@ -70,7 +82,7 @@
     return (output.transpose(1, 0, 2).reshape(row_count, ATT), maxima.T, totals.T)
 
 
-def local(
+def general(
     stream, latents, time_mod, block_mod, w_qkv, qk_gain, w_out, head_mod, w_head, noise_level
 ):
     slab_count = lax.axis_size("slab")
@@ -128,6 +140,242 @@
     return (updated.astype(jnp.bfloat16)[None], moved)
 
 
+def vmem_call(kernel, outs, name, flops, scratch=()):
+    whole = pl.BlockSpec(memory_space=pltpu.VMEM)
+
+    def call(scalars, *operands):
+        return pl.pallas_call(
+            kernel,
+            out_shape=[jax.ShapeDtypeStruct(shape, dtype) for shape, dtype in outs],
+            in_specs=[pl.BlockSpec(memory_space=pltpu.SMEM)] + [whole] * len(operands),
+            out_specs=[whole] * len(outs),
+            scratch_shapes=list(scratch),
+            compiler_params=pltpu.CompilerParams(vmem_limit_bytes=VMEM_LIMIT),
+            cost_estimate=pl.CostEstimate(flops=flops, bytes_accessed=1 << 20, transcendentals=0),
+            name=name,
+        )(scalars, *operands)
+
+    return call
+
+
+def dot_rows(left, right):
+    return lax.dot_general(left, right, (((1,), (1,)), ((), ())), preferred_element_type=F32)
+
+
+def project_kernel(
+    place, x0, x1, x2, x3, time_mod, block_mod, w_own, w_first, w_second,
+    near_out, far_out, keep_out, sums_out, modded, mixed,
+):
+    line, side, core = place[0], place[1], place[2]
+    modulation = block_mod[...] + time_mod[...]
+    shift, scale = modulation[0:1], 1.0 + modulation[1:2]
+    for step, rows in enumerate((x0, x1, x2, x3)):
+        normal = layer_norm(rows[...].astype(F32))
+        at = pl.multiple_of(jnp.bitwise_xor(line, step) * TOK_DEV, 16)
+        modded[pl.ds(at, TOK_DEV), :] = (normal * scale + shift).astype(BF16)
+    half = D // 2
+    width = w_own.shape[1]
+    own = jnp.dot(modded[...], w_own[...], preferred_element_type=F32)
+    other = jnp.dot(
+        modded[:, pl.ds(pl.multiple_of(core * half, half), half)], w_first[...],
+        preferred_element_type=F32,
+    )
+    other += jnp.dot(
+        modded[:, pl.ds(pl.multiple_of((1 - core) * half, half), half)], w_second[...],
+        preferred_element_type=F32,
+    )
+    mixed[:, pl.ds(pl.multiple_of(side * width, width), width)] = own.astype(BF16)
+    mixed[:, pl.ds(pl.multiple_of((1 - side) * width, width), width)] = other.astype(BF16)
+    ones = jnp.ones((16, PAIR), BF16)
+    row_id = lax.broadcasted_iota(jnp.int32, (16, ROWS), 0)
+    picked = jnp.zeros((16, ROWS), F32)
+    for unit in range(3):
+        values = mixed[:, unit * PAIR : (unit + 1) * PAIR].astype(F32)
+        squares = values * values
+        high = squares.astype(BF16)
+        low = (squares - high.astype(F32)).astype(BF16)
+        total = dot_rows(ones, high) + dot_rows(ones, low)
+        kind = (line * 3 + unit) // LINE
+        picked += jnp.where(row_id // 3 == kind, total, 0.0)
+    picked = jnp.where(row_id < 6, picked, 0.0)
+    first = picked.astype(BF16).astype(F32)
+    second = (picked - first).astype(BF16).astype(F32)
+    third = picked - first - second
+    part = row_id % 3
+    packed = jnp.where(part == 0, first, jnp.where(part == 1, second, third)).astype(BF16)
+    padded = jnp.concatenate([packed, jnp.zeros((16, PAIR - ROWS), BF16)], axis=1)
+    sums_out[...] = padded
+    near_out[:ROWS, :] = mixed[:, PAIR : 2 * PAIR]
+    near_out[ROWS:, :] = padded
+    odd = line % 2
+    at = pl.multiple_of((1 - odd) * 2 * PAIR, PAIR)
+    far_out[:ROWS, :] = mixed[:, pl.ds(at, PAIR)]
+    far_out[ROWS:, :] = padded
+    at = pl.multiple_of(odd * 2 * PAIR, PAIR)
+    keep_out[...] = mixed[:, pl.ds(at, PAIR)]
+
+
+def rope_kernel(
+    place, keep, near, far, own_sums, last_sums, gains, cosines, sines, q_out, kv_out, units
+):
+    line = place[0]
+    units[0] = keep[...]
+    units[1] = near[:ROWS, :]
+    units[2] = far[:ROWS, :]
+    pieces = [
+        own_sums[...].astype(F32), near[ROWS:, :].astype(F32),
+        far[ROWS:, :].astype(F32), last_sums[...].astype(F32),
+    ]
+    row_id = lax.broadcasted_iota(jnp.int32, (16, 1), 0)
+    cos, sin = cosines[...], sines[...]
+    for kind in range(2):
+        wanted = row_id // 3 == kind
+        total = jnp.zeros((1, PAIR), F32)
+        for piece in pieces:
+            total += jnp.sum(jnp.where(wanted, piece, 0.0), axis=0, keepdims=True)
+        scale = lax.rsqrt(total * (1.0 / ATT) + 1e-06)
+        scale = jnp.transpose(jnp.broadcast_to(scale, (HEAD_DIM, PAIR)))[:ROWS]
+        values = units[place[3 + kind]].astype(F32)
+        for head in range(2):
+            columns = slice(head * HEAD_DIM, (head + 1) * HEAD_DIM)
+            at = pl.multiple_of(line * PAIR + head * HEAD_DIM, HEAD_DIM)
+            scaled = values[:, columns] * scale * gains[kind : kind + 1, pl.ds(at, HEAD_DIM)]
+            turned = scaled * cos + pltpu.roll(scaled, HEAD_DIM // 2, axis=1) * sin
+            (kv_out if kind else q_out)[:, columns] = turned.astype(BF16)
+    kv_out[:, PAIR:] = units[place[5]]
+
+
+def attend_kernel(
+    place, queries, a0, a1, b0, b1, c0, c1, d0, d1, o0, o1, o2, o3, result, accum, highest, sums
+):
+    line = place[0]
+    accum[...] = jnp.zeros_like(accum)
+    sums[...] = jnp.zeros_like(sums)
+    highest[...] = jnp.full_like(highest, -1e30)
+
+    def group(one, two):
+        for head in range(2):
+            columns = slice(head * HEAD_DIM, (head + 1) * HEAD_DIM)
+            value_columns = slice(PAIR + head * HEAD_DIM, PAIR + (head + 1) * HEAD_DIM)
+            keys = jnp.concatenate([one[:, columns], two[:, columns]], axis=0)
+            values = jnp.concatenate([one[:, value_columns], two[:, value_columns]], axis=0)
+            scores = dot_rows(queries[:, columns], keys) * HEAD_DIM ** (-0.5)
+            maxima = jnp.max(scores, axis=-1, keepdims=True)
+            weights = jnp.exp(scores - maxima).astype(BF16)
+            totals = jnp.sum(weights.astype(F32), axis=-1, keepdims=True)
+            output = jnp.dot(weights, values, preferred_element_type=F32)
+            old = highest[head]
+            new = jnp.maximum(old, maxima)
+            keep_old, keep_new = jnp.exp(old - new), jnp.exp(maxima - new)
+            highest[head] = new
+            sums[head] = sums[head] * keep_old + totals * keep_new
+            accum[head] = accum[head] * keep_old + output * keep_new
+
+    group(a0, a1)
+    pl.when(place[2] == 1)(lambda: group(b0, b1))
+    pl.when(place[6] == 1)(lambda: group(c0, c1))
+    pl.when(place[6] == 1)(lambda: group(d0, d1))
+    for head in range(2):
+        columns = slice(head * HEAD_DIM, (head + 1) * HEAD_DIM)
+        result[:, columns] = (accum[head] / sums[head]).astype(BF16)
+    for step, out in enumerate((o0, o1, o2, o3)):
+        at = pl.multiple_of(jnp.bitwise_xor(line, step) * TOK_DEV, 16)
+        out[...] = result[pl.ds(at, TOK_DEV), :]
+
+
+def finish_kernel(
+    place, r0, r1, r2, r3, w_out, stream, time_mod, block_mod, head_mod, w_head, latents,
+    stream_out, latents_out,
+):
+    line = place[0]
+    projected = jnp.zeros((TOK_DEV, D), F32)
+    for step, rows in enumerate((r0, r1, r2, r3)):
+        at = pl.multiple_of(jnp.bitwise_xor(line, step) * PAIR, PAIR)
+        projected += jnp.dot(rows[...], w_out[pl.ds(at, PAIR), :], preferred_element_type=F32)
+    gate = block_mod[2:3] + time_mod[2:3]
+    updated = stream[...].astype(F32) + gate * projected
+    stream_out[...] = updated.astype(BF16)
+    head_in = (layer_norm(updated) * (1.0 + head_mod[1:2]) + head_mod[0:1]).astype(BF16)
+    velocity = jnp.dot(head_in, w_head[...], preferred_element_type=F32)
+
+    def sigma(level):
+        fraction = jnp.full((1, CHAN), level, jnp.int32).astype(F32) / LEVELS
+        return 5.0 * fraction / (1.0 + 4.0 * fraction)
+
+    latents_out[...] = latents[...] + (sigma(place[7] - 1) - sigma(place[7])) * velocity
+
+
+def lines(
+    stream, latents, time_mod, block_mod, w_qkv, qk_gain, w_out, head_mod, w_head, noise_level
+):
+    slab, seq = lax.axis_index("slab"), lax.axis_index("seq")
+    line, side, core = seq // 2, seq % 2, slab % 2
+    slots = jnp.array([[0, 1, 2], [1, 0, 2], [2, 0, 1], [2, 1, 0]], jnp.int32)[line]
+    place = jnp.concatenate(
+        [jnp.stack([line, side, core]), slots, (slab // 2)[None], noise_level]
+    ).astype(jnp.int32)
+
+    def along(step, value):
+        return lax.ppermute(value, "seq", [(i, i ^ (2 * step)) for i in range(2 * LINE)])
+
+    def across(value):
+        return lax.ppermute(value, "seq", [(i, i ^ 1) for i in range(2 * LINE)])
+
+    def cores(value):
+        return lax.ppermute(value, "slab", [(i, i ^ 1) for i in range(4)])
+
+    def chips(value, flip):
+        count = 2 * LINE
+        pairs = [(s * count + i, (s + 2) * count + (i ^ flip)) for s in range(2) for i in range(count)]
+        return lax.ppermute(value, ("slab", "seq"), pairs)
+
+    rows = stream[0]
+    w_first = across(lax.dynamic_slice_in_dim(w_qkv, core * (D // 2), D // 2, 0))
+    x3, x2, x1 = along(3, rows), along(2, rows), along(1, rows)
+    w_second = cores(w_first)
+
+    at = (jnp.arange(LINE)[:, None] * 2 + side) * TOK_DEV + jnp.arange(TOK_DEV)[None]
+    position = (slab * (2 * LINE * TOK_DEV) + at.reshape(ROWS)).astype(F32)
+    halves = HEAD_DIM // 2
+    frequency = jnp.power(10000.0, -jnp.arange(halves).astype(F32) / halves)
+    angles = position[:, None] * frequency[None]
+    cosines, sines = jnp.cos(angles), jnp.sin(angles)
+    cosines = jnp.concatenate([cosines, cosines], axis=1)
+    sines = jnp.concatenate([-sines, sines], axis=1)
+
+    message = (ROWS + 16, PAIR)
+    near, far, keep, sums = vmem_call(
+        project_kernel,
+        [(message, BF16), (message, BF16), ((ROWS, PAIR), BF16), ((16, PAIR), BF16)],
+        "project", 2 * ROWS * D * 3 * PAIR,
+        [pltpu.VMEM((ROWS, D), BF16), pltpu.VMEM((ROWS, 3 * PAIR), BF16)],
+    )(place, rows, x1, x2, x3, time_mod[0], block_mod, w_qkv, w_first, w_second)
+    far, near, last_sums = along(2, far), along(1, near), along(3, sums)
+    queries, pairs = vmem_call(
+        rope_kernel,
+        [((ROWS, PAIR), BF16), ((ROWS, 2 * PAIR), BF16)],
+        "rope", 1 << 22, [pltpu.VMEM((3, ROWS, PAIR), BF16)],
+    )(place, keep, near, far, sums, last_sums, qk_gain, cosines, sines)
+    core_pairs = cores(pairs)
+    side_pairs = across(pairs)
+    chip_pairs = chips(pairs, 0)
+    both_pairs = chips(pairs, 1)
+    shape, dtype = (TOK_DEV, PAIR), BF16
+    state = pltpu.VMEM((2, ROWS, 1), F32)
+    parts = vmem_call(
+        attend_kernel, [(shape, dtype)] * 4, "attend", 1 << 28,
+        [pltpu.VMEM((ROWS, PAIR), BF16), pltpu.VMEM((2, ROWS, HEAD_DIM), F32), state, state],
+    )(
+        place, queries, pairs, side_pairs, core_pairs, cores(side_pairs),
+        chip_pairs, both_pairs, cores(chip_pairs), cores(both_pairs),
+    )
+    taken = [parts[0]] + [along(step, parts[step]) for step in (1, 2, 3)]
+    new_stream, stepped = vmem_call(
+        finish_kernel, [((TOK_DEV, D), BF16), ((TOK_DEV, CHAN), F32)], "finish", 1 << 28
+    )(place, *taken, w_out, rows, time_mod[0], block_mod, head_mod[0], w_head, latents[0])
+    return (new_stream[None], from_behind(stepped[None], "slab", -1))
+
+
 def solution(mesh):
     in_specs = (
         P("slab", "seq", None),
@@ -142,4 +390,5 @@
         P("slab"),
     )
     out_specs = (P("slab", "seq", None), P("slab", "seq", None))
+    local = lines if tuple(mesh.shape.values()) == (4, 2 * LINE) else general
     return jax.shard_map(local, mesh=mesh, in_specs=in_specs, out_specs=out_specs, check_vma=False)

time: 206 us -> 72.8 us (0.35)
  waiting for transfers between devices: 99.2 us -> 22.9 us
  matrix products: 28.1 us -> 0 us
  other arithmetic: 23.4 us -> 0.64 us
  starting transfers between devices: 12.5 us -> 29 us
  between operations: 16.3 us -> 1.5 us
  Pallas kernels: 0 us -> 9.08 us
  local copies, waits for them, and re-layouts: 17.3 us -> 9.05 us
  blocking collectives: 7.55 us -> 0 us
    all_gather x2 -> x0, waiting for transfers between devices: 93.3 us -> none  [the longest x1 51.3 us: local(): full_mixed = lax.all_gather(columns, 'seq', axis=1, tiled=True)]
    ppermute x0 -> x18, starting transfers between devices: none -> 28.4 us  [the longest x9 11 us: along(): lax.ppermute(value, 'seq', [(i, i ^ 2 * step) for i in range(2 * LINE)])]
    dot_general x19 -> x0, matrix products: 28.1 us -> none  [the longest x8 14.3 us: one_head(): output = jnp.dot(weights, value_part, preferred_element_type=jnp.float32)]
    ppermute x0 -> x18, waiting for transfers between devices: none -> 16.8 us  [the longest x2 8.04 us: across(): return lax.ppermute(value, 'seq', [(i, i ^ 1) for i in range(2 * LINE)])]
    all_to_all x3 -> x0, starting transfers between devices: 11.5 us -> none  [the longest x1 4.85 us: local(): lax.all_to_all(output, 'slab', split_axis=0, concat_axis=0, tiled=True)]
    reduce_sum x16 -> x0, other arithmetic: 9.36 us -> none  [the longest x2 2.4 us: norm_rope(): jnp.mean(floats * floats, axis=-1, keepdims=True) + 1e-06]
    pallas_call x0 -> x4, Pallas kernels: none -> 9.08 us  [call(): pl.pallas_call(kernel, out_shape=[jax.ShapeDtypeStruct(shape, dtype) for...]
    all_gather x1 -> x0, blocking collectives: 7.55 us -> none  [local(): all_queries = lax.all_gather(own_queries[None], 'slab', axis=0, tiled=True)]
  transfers between devices with their start and end apart: 6 -> 19, of which waited for: 5 -> 6; matrix products, arithmetic and copies ran while one was open for 8% -> 5% of each run, Pallas kernels for 0% -> 0%
where the time goes in v1:
time: 72.8 us; the launch traced here: 72.1 us
  starting transfers between devices  29 us (40%)
  waiting for transfers between devices  22.9 us (31%)
  Pallas kernels  9.08 us (12%)
  local copies, waits for them, and re-layouts  9.05 us (12%)
  between operations  1.5 us (2%)
    ppermute x9, starting transfers between devices, along(): lax.ppermute(value, 'seq', [(i, i ^ 2 * step) for i in range(2 * LINE)])  11 us
    ppermute x5, starting transfers between devices, cores(): return lax.ppermute(value, 'slab', [(i, i ^ 1) for i in range(4)])  9.21 us
    pallas_call x4, Pallas kernels, call(): pl.pallas_call(kernel, out_shape=[jax.ShapeDtypeStruct(shape, dtype) for...  9.08 us
    ppermute x2, waiting for transfers between devices, across(): return lax.ppermute(value, 'seq', [(i, i ^ 1) for i in range(2 * LINE)])  8.04 us
    ppermute x9, waiting for transfers between devices, along(): lax.ppermute(value, 'seq', [(i, i ^ 2 * step) for i in range(2 * LINE)])  7.48 us
    unnamed x29, local copies, waits for them, and re-layouts  6.98 us
    ppermute x1, waiting for transfers between devices, from_behind(): return lax.ppermute(value, axis, pairs)  6.08 us
    ppermute x2, starting transfers between devices, chips(): return lax.ppermute(value, ('slab', 'seq'), pairs)  4.42 us
  transfers between devices with their start and end apart: 19, of which 6 were waited for; matrix products, arithmetic and copies ran while one was open for 5% of the time, Pallas kernels for 0%

profile of v1, /device:TPU:1, one launch (start us, length us, event | category | flops | bytes accessed | tf_op | source)
XLA Modules:
  0.0 72.1 jit_solution(18089786950772612875)
XLA Ops:
  0.7 1.2 %constant_dynamic-slice_fusion = bf16[768,384]{1,0:T(8,128)(2,1)S(1)} fusion(bf16[1536,384]{1,0:T(8,128)(2,1)} %w_own.1, s32[]{:T(128)S(6)} %select_n.29), kind=kLoop, calls=%fused_computation.10 | loop fusion | bytes 1179652 | tf_op jit(solution)/shard_map/dynamic_slice | solution.py:333
  1.9 2.1 %collective-permute-start.3 = (bf16[768,384]{1,0:T(8,128)(2,1)S(1)}, bf16[768,384]{1,0:T(8,128)(2,1)S(1)}, u32[]{:S(2)}, u32[]{:S(2)}) collective-permute-start(bf16[768,384]{1,0:T(8,128)(2,1)S(1)} %constant_dynamic-slice_fusion), channel_id=1, source_target_pairs={{0,1},{1,0},{2,3},{3,2},{4,5},{5,4},{6,7},{7,6},{8,9},{9,8},{10,11... | collective-permute-start | bytes 1769480 | tf_op jit(solution)/shard_map/ppermute | solution.py:322
  4.0 1.3 %collective-permute-start = (bf16[48,1536]{1,0:T(8,128)(2,1)}, bf16[48,1536]{1,0:T(8,128)(2,1)S(1)}, u32[]{:S(2)}, u32[]{:S(2)}) collective-permute-start(bf16[48,1536]{1,0:T(8,128)(2,1)} %bitcast.14), channel_id=1, source_target_pairs={{0,2},{1,3},{2,0},{3,1},{4,6},{5,7},{6,4},{7,5},{8,10},{9,11},{10,... | collective-permute-start | bytes 442376 | tf_op jit(solution)/shard_map/ppermute | solution.py:319
  5.3 2.3 %collective-permute-start.1 = (bf16[48,1536]{1,0:T(8,128)(2,1)}, bf16[48,1536]{1,0:T(8,128)(2,1)S(1)}, u32[]{:S(2)}, u32[]{:S(2)}) collective-permute-start(bf16[48,1536]{1,0:T(8,128)(2,1)} %bitcast.15), channel_id=1, source_target_pairs={{0,4},{1,5},{2,6},{3,7},{4,0},{5,1},{6,2},{7,3},{8,12},{9,13},{10,... | collective-permute-start | bytes 442376 | tf_op jit(solution)/shard_map/ppermute | solution.py:319
  8.3 0.7 %copy.16 = f32[1,3,1536]{2,1,0:T(4,128)S(1)} copy(f32[1,3,1536]{2,0,1:T(1,128)} %param.13) | data formatting | bytes 36864
  9.1 8.0 %collective-permute-done.3.w_first = bf16[768,384]{1,0:T(8,128)(2,1)S(1)} collective-permute-done((bf16[768,384]{1,0:T(8,128)(2,1)S(1)}, bf16[768,384]{1,0:T(8,128)(2,1)S(1)}, u32[]{:S(2)}, u32[]{:S(2)}) %collective-permute-start.3) | collective-permute-done | bytes 589856 | tf_op jit(solution)/shard_map/ppermute | solution.py:322
  17.1 1.2 %collective-permute-start.4 = (bf16[768,384]{1,0:T(8,128)(2,1)S(1)}, bf16[768,384]{1,0:T(8,128)(2,1)S(1)}, u32[]{:S(2)}, u32[]{:S(2)}) collective-permute-start(bf16[768,384]{1,0:T(8,128)(2,1)S(1)} %collective-permute-done.3.w_first), channel_id=1, source_target_pairs={{0,8},{8,0},{16,24},{24,16},{1,9},{9,1},{17,25},{25,17},{2,10},{10... | collective-permute-start | bytes 1769480 | tf_op jit(solution)/shard_map/ppermute | solution.py:325
  18.5 0.7 dynamic-slice_bitcast_fusion
  20.0 2.2 %project.1 = (bf16[208,256]{1,0:T(8,128)(2,1)S(1)}, bf16[208,256]{1,0:T(8,128)(2,1)S(1)}, bf16[192,256]{1,0:T(8,128)(2,1)S(1)}, bf16[16,256]{1,0:T(8,128)(2,1)S(1)}) custom-call(s32[8]{0:T(128)S(1)} %concatenate.9.place, bf16[48,1536]{1,0:T(8,128)(2,1)S(1)} %bitcast.17, bf16[48,1536]{1,0:T(8,128)(2,1)S(1)} %collective-permute-done.x1, ...), custom_call_target="tpu_custom_call" | custom-call | flops 452984832 | bytes 1048576 | tf_op jit(solution)/shard_map/project/pallas_call | solution.py:147
  22.2 1.6 %collective-permute-start.5 = (bf16[208,256]{1,0:T(8,128)(2,1)S(1)}, bf16[208,256]{1,0:T(8,128)(2,1)S(1)}, u32[]{:S(2)}, u32[]{:S(2)}) collective-permute-start(bf16[208,256]{1,0:T(8,128)(2,1)S(1)} %get-tuple-element.15), channel_id=1, source_target_pairs={{0,2},{1,3},{2,0},{3,1},{4,6},{5,7},{6,4},{7,5},{8,10},{9,11},{10,... | collective-permute-start | bytes 319496 | tf_op jit(solution)/shard_map/ppermute | solution.py:319
  23.8 2.3 %collective-permute-start.6 = (bf16[208,256]{1,0:T(8,128)(2,1)S(1)}, bf16[208,256]{1,0:T(8,128)(2,1)S(1)}, u32[]{:S(2)}, u32[]{:S(2)}) collective-permute-start(bf16[208,256]{1,0:T(8,128)(2,1)S(1)} %get-tuple-element.16), channel_id=1, source_target_pairs={{0,4},{1,5},{2,6},{3,7},{4,0},{5,1},{6,2},{7,3},{8,12},{9,13},{10,... | collective-permute-start | bytes 319496 | tf_op jit(solution)/shard_map/ppermute | solution.py:319
  26.2 4.4 %collective-permute-done.7.last_sums = bf16[16,256]{1,0:T(8,128)(2,1)S(1)} collective-permute-done((bf16[16,256]{1,0:T(8,128)(2,1)S(1)}, bf16[16,256]{1,0:T(8,128)(2,1)S(1)}, u32[]{:S(2)}, u32[]{:S(2)}) %collective-permute-start.7) | collective-permute-done | bytes 8224 | tf_op jit(solution)/shard_map/ppermute | solution.py:319
  30.7 0.8 %rope.1 = (bf16[192,256]{1,0:T(8,128)(2,1)S(1)}, bf16[192,512]{1,0:T(8,128)(2,1)S(1)}) custom-call(s32[8]{0:T(128)S(1)} %concatenate.9.place, bf16[192,256]{1,0:T(8,128)(2,1)S(1)} %get-tuple-element.14.keep, bf16[208,256]{1,0:T(8,128)(2,1)S(1)} %collective-permute-done.5.near, bf16[208,256]{1,0:T(8,128)(2,1)S(1)} %collective-permute-done.6.far, ...), custom_call_target="tpu_custom_call" | custom-call | flops 4194304 | bytes 1048576 | tf_op jit(solution)/shard_map/rope/pallas_call | solution.py:147
  31.5 1.6 %collective-permute-start.8 = (bf16[192,512]{1,0:T(8,128)(2,1)S(1)}, bf16[192,512]{1,0:T(8,128)(2,1)S(1)}, u32[]{:S(2)}, u32[]{:S(2)}) collective-permute-start(bf16[192,512]{1,0:T(8,128)(2,1)S(1)} %get-tuple-element.19.a0), channel_id=1, source_target_pairs={{0,1},{1,0},{2,3},{3,2},{4,5},{5,4},{6,7},{7,6},{8,9},{9,8},{10,11... | collective-permute-start | bytes 589832 | tf_op jit(solution)/shard_map/ppermute | solution.py:322
  33.1 3.1 %collective-permute-start.11 = (bf16[192,512]{1,0:T(8,128)(2,1)S(1)}, bf16[192,512]{1,0:T(8,128)(2,1)S(1)}, u32[]{:S(2)}, u32[]{:S(2)}) collective-permute-start(bf16[192,512]{1,0:T(8,128)(2,1)S(1)} %get-tuple-element.19.a0), channel_id=1, source_target_pairs={{0,16},{1,17},{2,18},{3,19},{4,20},{5,21},{6,22},{7,23},{8,24},{9,... | collective-permute-start | bytes 589832 | tf_op jit(solution)/shard_map/ppermute | solution.py:330
  36.2 1.3 %collective-permute-start.12 = (bf16[192,512]{1,0:T(8,128)(2,1)S(1)}, bf16[192,512]{1,0:T(8,128)(2,1)S(1)}, u32[]{:S(2)}, u32[]{:S(2)}) collective-permute-start(bf16[192,512]{1,0:T(8,128)(2,1)S(1)} %get-tuple-element.19.a0), channel_id=1, source_target_pairs={{0,17},{1,16},{2,19},{3,18},{4,21},{5,20},{6,23},{7,22},{8,25},{9,... | collective-permute-start | bytes 589832 | tf_op jit(solution)/shard_map/ppermute | solution.py:330
  37.6 2.3 %collective-permute-start.9 = (bf16[192,512]{1,0:T(8,128)(2,1)S(1)}, bf16[192,512]{1,0:T(8,128)(2,1)S(1)}, u32[]{:S(2)}, u32[]{:S(2)}) collective-permute-start(bf16[192,512]{1,0:T(8,128)(2,1)S(1)} %get-tuple-element.19.a0), channel_id=1, source_target_pairs={{0,8},{8,0},{16,24},{24,16},{1,9},{9,1},{17,25},{25,17},{2,10},{10... | collective-permute-start | bytes 589832 | tf_op jit(solution)/shard_map/ppermute | solution.py:325
  40.0 3.5 %collective-permute-start.13 = (bf16[192,512]{1,0:T(8,128)(2,1)S(1)}, bf16[192,512]{1,0:T(8,128)(2,1)S(1)}, u32[]{:S(2)}, u32[]{:S(2)}) collective-permute-start(bf16[192,512]{1,0:T(8,128)(2,1)S(1)} %collective-permute-done.11.c0), channel_id=1, source_target_pairs={{0,8},{8,0},{16,24},{24,16},{1,9},{9,1},{17,25},{25,17},{2,10},{10... | collective-permute-start | bytes 589832 | tf_op jit(solution)/shard_map/ppermute | solution.py:325
  43.4 2.1 %collective-permute-start.14 = (bf16[192,512]{1,0:T(8,128)(2,1)S(1)}, bf16[192,512]{1,0:T(8,128)(2,1)S(1)}, u32[]{:S(2)}, u32[]{:S(2)}) collective-permute-start(bf16[192,512]{1,0:T(8,128)(2,1)S(1)} %collective-permute-done.12.c1), channel_id=1, source_target_pairs={{0,8},{8,0},{16,24},{24,16},{1,9},{9,1},{17,25},{25,17},{2,10},{10... | collective-permute-start | bytes 589832 | tf_op jit(solution)/shard_map/ppermute | solution.py:325
  45.6 1.1 %collective-permute-done.14.d1 = bf16[192,512]{1,0:T(8,128)(2,1)S(1)} collective-permute-done((bf16[192,512]{1,0:T(8,128)(2,1)S(1)}, bf16[192,512]{1,0:T(8,128)(2,1)S(1)}, u32[]{:S(2)}, u32[]{:S(2)}) %collective-permute-start.14) | collective-permute-done | bytes 196640 | tf_op jit(solution)/shard_map/ppermute | solution.py:325
  46.6 3.7 %attend.1 = (bf16[48,256]{1,0:T(8,128)(2,1)S(1)}, bf16[48,256]{1,0:T(8,128)(2,1)}, bf16[48,256]{1,0:T(8,128)(2,1)}, bf16[48,256]{1,0:T(8,128)(2,1)}) custom-call(s32[8]{0:T(128)S(1)} %concatenate.9.place, bf16[192,256]{1,0:T(8,128)(2,1)S(1)} %get-tuple-element.18.queries, bf16[192,512]{1,0:T(8,128)(2,1)S(1)} %get-tuple-element.19.a0, ...), custom_call_target="tpu_custom_call" | custom-call | flops 268435456 | bytes 1048576 | tf_op jit(solution)/shard_map/attend/pallas_call | solution.py:147
  51.2 2.3 %collective-permute-start.16 = (bf16[48,256]{1,0:T(8,128)(2,1)}, bf16[48,256]{1,0:T(8,128)(2,1)}, u32[]{:S(2)}, u32[]{:S(2)}) collective-permute-start(bf16[48,256]{1,0:T(8,128)(2,1)} %get-tuple-element.22), channel_id=1, source_target_pairs={{0,4},{1,5},{2,6},{3,7},{4,0},{5,1},{6,2},{7,3},{8,12},{9,13},{10,... | collective-permute-start | bytes 73736 | tf_op jit(solution)/shard_map/ppermute | solution.py:319
  53.5 0.9 %collective-permute-start.17 = (bf16[48,256]{1,0:T(8,128)(2,1)}, bf16[48,256]{1,0:T(8,128)(2,1)}, u32[]{:S(2)}, u32[]{:S(2)}) collective-permute-start(bf16[48,256]{1,0:T(8,128)(2,1)} %get-tuple-element.23), channel_id=1, source_target_pairs={{0,6},{1,7},{2,4},{3,5},{4,2},{5,3},{6,0},{7,1},{8,14},{9,15},{10,... | collective-permute-start | bytes 73736 | tf_op jit(solution)/shard_map/ppermute | solution.py:319
  54.5 1.1 %copy.13.w_head = bf16[1536,64]{1,0:T(8,128)(2,1)S(1)} copy(bf16[1536,64]{0,1:T(8,128)(2,1)} %param.19) | data formatting | bytes 393216 | tf_op args[8]
  55.6 3.0 %collective-permute-done.17.r3 = bf16[48,256]{1,0:T(8,128)(2,1)} collective-permute-done((bf16[48,256]{1,0:T(8,128)(2,1)}, bf16[48,256]{1,0:T(8,128)(2,1)}, u32[]{:S(2)}, u32[]{:S(2)}) %collective-permute-start.17) | collective-permute-done | bytes 24608 | tf_op jit(solution)/shard_map/ppermute | solution.py:319
  58.7 0.9 %copy-done.3 = bf16[1,48,1536]{2,1,0:T(8,128)(2,1)S(1)} copy-done((bf16[1,48,1536]{2,1,0:T(8,128)(2,1)S(1)}, bf16[1,48,1536]{2,1,0:T(8,128)(2,1)}, u32[]{:S(2)}) %copy-start.3) | copy-done | bytes 147480
  59.6 0.7 %copy-done.5 = f32[1,3,1536]{2,1,0:T(4,128)S(1)} copy-done((f32[1,3,1536]{2,1,0:T(4,128)S(1)}, f32[1,3,1536]{2,1,0:T(4,128)}, u32[]{:S(2)}) %copy-start.5) | copy-done | bytes 18456
  60.3 0.7 %copy-done.7 = f32[3,1536]{1,0:T(4,128)S(1)} copy-done((f32[3,1536]{1,0:T(4,128)S(1)}, f32[3,1536]{1,0:T(4,128)}, u32[]{:S(2)}) %copy-start.7) | copy-done | bytes 18456
  61.1 0.7 %copy-done.8 = f32[1,48,64]{2,1,0:T(8,128)S(1)} copy-done((f32[1,48,64]{2,1,0:T(8,128)S(1)}, f32[1,48,64]{2,1,0:T(8,128)}, u32[]{:S(2)}) %copy-start.8) | copy-done | bytes 12312
  61.8 0.7 %copy-done.10 = bf16[48,256]{1,0:T(8,128)(2,1)S(1)} copy-done((bf16[48,256]{1,0:T(8,128)(2,1)S(1)}, bf16[48,256]{1,0:T(8,128)(2,1)}, u32[]{:S(2)}) %copy-start.10) | copy-done | bytes 24600
  62.5 2.3 %finish.1 = (bf16[48,1536]{1,0:T(8,128)(2,1)}, f32[48,64]{1,0:T(8,128)S(1)}) custom-call(s32[8]{0:T(128)S(1)} %concatenate.9.place, bf16[48,256]{1,0:T(8,128)(2,1)S(1)} %copy-done.10, bf16[48,256]{1,0:T(8,128)(2,1)} %collective-permute-done.15.r1, bf16[48,256]{1,0:T(8,128)(2,1)} %collective-permute-done.16.r2, bf16[48,256]{1,0:T(8,128)(2,1)} %collective-permute-done.17.r3, ...), custom_call_target="tpu_custom_call" | custom-call | flops 268435456 | bytes 1048576 | tf_op jit(solution)/shard_map/finish/pallas_call | solution.py:147
  65.5 6.1 %collective-permute-done.18 = f32[1,48,64]{2,1,0:T(8,128)S(1)} collective-permute-done((f32[1,48,64]{2,1,0:T(8,128)S(1)}, f32[1,48,64]{2,1,0:T(8,128)S(1)}, u32[]{:S(2)}, u32[]{:S(2)}) %collective-permute-start.18) | collective-permute-done | bytes 12320 | tf_op jit(solution)/shard_map/ppermute | solution.py:28
  (48 shorter events, 3.3 us)
Async XLA Ops:
  0.6 19.3 %copy-start.1 = (bf16[1536,384]{1,0:T(8,128)(2,1)S(1)}, bf16[1536,384]{1,0:T(8,128)(2,1)}, u32[]{:S(2)}) copy-start(bf16[1536,384]{1,0:T(8,128)(2,1)} %w_own.1) | copy-start | bytes 3538948
  0.6 19.3 %copy-start.2 = (bf16[1,48,1536]{2,1,0:T(8,128)(2,1)S(1)}, bf16[1,48,1536]{2,1,0:T(8,128)(2,1)}, u32[]{:S(2)}) copy-start(bf16[1,48,1536]{2,1,0:T(8,128)(2,1)} %param.11) | copy-start | bytes 442372
  0.7 19.3 %copy-start.6 = (f32[3,1536]{1,0:T(4,128)S(1)}, f32[3,1536]{1,0:T(4,128)}, u32[]{:S(2)}) copy-start(f32[3,1536]{1,0:T(4,128)} %block_mod.3) | copy-start | bytes 55300
  1.9 15.2 %collective-permute-start.3 = (bf16[768,384]{1,0:T(8,128)(2,1)S(1)}, bf16[768,384]{1,0:T(8,128)(2,1)S(1)}, u32[]{:S(2)}, u32[]{:S(2)}) collective-permute-start(bf16[768,384]{1,0:T(8,128)(2,1)S(1)} %constant_dynamic-slice_fusion), channel_id=1, source_target_pairs={{0,1},{1,0},{2,3},{3,2},{4,5},{5,4},{6,7},{7,6},{8,9},{9,8},{10,11... | collective-permute-start | bytes 1769480 | tf_op jit(solution)/shard_map/ppermute | solution.py:322
  4.0 15.7 %collective-permute-start = (bf16[48,1536]{1,0:T(8,128)(2,1)}, bf16[48,1536]{1,0:T(8,128)(2,1)S(1)}, u32[]{:S(2)}, u32[]{:S(2)}) collective-permute-start(bf16[48,1536]{1,0:T(8,128)(2,1)} %bitcast.14), channel_id=1, source_target_pairs={{0,2},{1,3},{2,0},{3,1},{4,6},{5,7},{6,4},{7,5},{8,10},{9,11},{10,... | collective-permute-start | bytes 442376 | tf_op jit(solution)/shard_map/ppermute | solution.py:319
  5.3 14.4 %collective-permute-start.1 = (bf16[48,1536]{1,0:T(8,128)(2,1)}, bf16[48,1536]{1,0:T(8,128)(2,1)S(1)}, u32[]{:S(2)}, u32[]{:S(2)}) collective-permute-start(bf16[48,1536]{1,0:T(8,128)(2,1)} %bitcast.15), channel_id=1, source_target_pairs={{0,4},{1,5},{2,6},{3,7},{4,0},{5,1},{6,2},{7,3},{8,12},{9,13},{10,... | collective-permute-start | bytes 442376 | tf_op jit(solution)/shard_map/ppermute | solution.py:319
  7.7 12.1 %collective-permute-start.2 = (bf16[48,1536]{1,0:T(8,128)(2,1)}, bf16[48,1536]{1,0:T(8,128)(2,1)S(1)}, u32[]{:S(2)}, u32[]{:S(2)}) collective-permute-start(bf16[48,1536]{1,0:T(8,128)(2,1)} %bitcast.16), channel_id=1, source_target_pairs={{0,6},{1,7},{2,4},{3,5},{4,2},{5,3},{6,0},{7,1},{8,14},{9,15},{10,... | collective-permute-start | bytes 442376 | tf_op jit(solution)/shard_map/ppermute | solution.py:319
  9.0 13.2 %copy-start.4 = (f32[1,3,1536]{2,1,0:T(4,128)}, f32[1,3,1536]{2,1,0:T(4,128)S(1)}, u32[]{:S(2)}) copy-start(f32[1,3,1536]{2,1,0:T(4,128)S(1)} %copy.16) | copy-start | bytes 55300
  17.1 2.9 %collective-permute-start.4 = (bf16[768,384]{1,0:T(8,128)(2,1)S(1)}, bf16[768,384]{1,0:T(8,128)(2,1)S(1)}, u32[]{:S(2)}, u32[]{:S(2)}) collective-permute-start(bf16[768,384]{1,0:T(8,128)(2,1)S(1)} %collective-permute-done.3.w_first), channel_id=1, source_target_pairs={{0,8},{8,0},{16,24},{24,16},{1,9},{9,1},{17,25},{25,17},{2,10},{10... | collective-permute-start | bytes 1769480 | tf_op jit(solution)/shard_map/ppermute | solution.py:325
  20.0 10.7 %copy-start.12 = (f32[2,1024]{1,0:T(2,128)S(1)}, f32[2,1024]{1,0:T(2,128)}, u32[]{:S(2)}) copy-start(f32[2,1024]{1,0:T(2,128)} %gains.1) | copy-start | bytes 24580
  22.2 8.4 %collective-permute-start.5 = (bf16[208,256]{1,0:T(8,128)(2,1)S(1)}, bf16[208,256]{1,0:T(8,128)(2,1)S(1)}, u32[]{:S(2)}, u32[]{:S(2)}) collective-permute-start(bf16[208,256]{1,0:T(8,128)(2,1)S(1)} %get-tuple-element.15), channel_id=1, source_target_pairs={{0,2},{1,3},{2,0},{3,1},{4,6},{5,7},{6,4},{7,5},{8,10},{9,11},{10,... | collective-permute-start | bytes 319496 | tf_op jit(solution)/shard_map/ppermute | solution.py:319
  23.8 6.9 %collective-permute-start.6 = (bf16[208,256]{1,0:T(8,128)(2,1)S(1)}, bf16[208,256]{1,0:T(8,128)(2,1)S(1)}, u32[]{:S(2)}, u32[]{:S(2)}) collective-permute-start(bf16[208,256]{1,0:T(8,128)(2,1)S(1)} %get-tuple-element.16), channel_id=1, source_target_pairs={{0,4},{1,5},{2,6},{3,7},{4,0},{5,1},{6,2},{7,3},{8,12},{9,13},{10,... | collective-permute-start | bytes 319496 | tf_op jit(solution)/shard_map/ppermute | solution.py:319
  26.1 4.6 %collective-permute-start.7 = (bf16[16,256]{1,0:T(8,128)(2,1)S(1)}, bf16[16,256]{1,0:T(8,128)(2,1)S(1)}, u32[]{:S(2)}, u32[]{:S(2)}) collective-permute-start(bf16[16,256]{1,0:T(8,128)(2,1)S(1)} %get-tuple-element.17.own_sums), channel_id=1, source_target_pairs={{0,6},{1,7},{2,4},{3,5},{4,2},{5,3},{6,0},{7,1},{8,14},{9,15},{10,... | collective-permute-start | bytes 24584 | tf_op jit(solution)/shard_map/ppermute | solution.py:319
  26.1 32.6 %copy-start = (bf16[1024,1536]{1,0:T(8,128)(2,1)S(1)}, bf16[1024,1536]{1,0:T(8,128)(2,1)}, u32[]{:S(2)}) copy-start(bf16[1024,1536]{1,0:T(8,128)(2,1)} %w_out.1) | copy-start | bytes 9437188
  31.5 27.2 %copy-start.11 = (f32[1,2,1536]{2,1,0:T(2,128)S(1)}, f32[1,2,1536]{2,1,0:T(2,128)}, u32[]{:S(2)}) copy-start(f32[1,2,1536]{2,1,0:T(2,128)} %param.18) | copy-start | bytes 36868
  31.5 8.4 %collective-permute-start.8 = (bf16[192,512]{1,0:T(8,128)(2,1)S(1)}, bf16[192,512]{1,0:T(8,128)(2,1)S(1)}, u32[]{:S(2)}, u32[]{:S(2)}) collective-permute-start(bf16[192,512]{1,0:T(8,128)(2,1)S(1)} %get-tuple-element.19.a0), channel_id=1, source_target_pairs={{0,1},{1,0},{2,3},{3,2},{4,5},{5,4},{6,7},{7,6},{8,9},{9,8},{10,11... | collective-permute-start | bytes 589832 | tf_op jit(solution)/shard_map/ppermute | solution.py:322
  33.1 6.8 %collective-permute-start.11 = (bf16[192,512]{1,0:T(8,128)(2,1)S(1)}, bf16[192,512]{1,0:T(8,128)(2,1)S(1)}, u32[]{:S(2)}, u32[]{:S(2)}) collective-permute-start(bf16[192,512]{1,0:T(8,128)(2,1)S(1)} %get-tuple-element.19.a0), channel_id=1, source_target_pairs={{0,16},{1,17},{2,18},{3,19},{4,20},{5,21},{6,22},{7,23},{8,24},{9,... | collective-permute-start | bytes 589832 | tf_op jit(solution)/shard_map/ppermute | solution.py:330
  36.2 7.2 %collective-permute-start.12 = (bf16[192,512]{1,0:T(8,128)(2,1)S(1)}, bf16[192,512]{1,0:T(8,128)(2,1)S(1)}, u32[]{:S(2)}, u32[]{:S(2)}) collective-permute-start(bf16[192,512]{1,0:T(8,128)(2,1)S(1)} %get-tuple-element.19.a0), channel_id=1, source_target_pairs={{0,17},{1,16},{2,19},{3,18},{4,21},{5,20},{6,23},{7,22},{8,25},{9,... | collective-permute-start | bytes 589832 | tf_op jit(solution)/shard_map/ppermute | solution.py:330
  37.6 8.0 %collective-permute-start.9 = (bf16[192,512]{1,0:T(8,128)(2,1)S(1)}, bf16[192,512]{1,0:T(8,128)(2,1)S(1)}, u32[]{:S(2)}, u32[]{:S(2)}) collective-permute-start(bf16[192,512]{1,0:T(8,128)(2,1)S(1)} %get-tuple-element.19.a0), channel_id=1, source_target_pairs={{0,8},{8,0},{16,24},{24,16},{1,9},{9,1},{17,25},{25,17},{2,10},{10... | collective-permute-start | bytes 589832 | tf_op jit(solution)/shard_map/ppermute | solution.py:325
  39.9 5.7 %collective-permute-start.10 = (bf16[192,512]{1,0:T(8,128)(2,1)S(1)}, bf16[192,512]{1,0:T(8,128)(2,1)S(1)}, u32[]{:S(2)}, u32[]{:S(2)}) collective-permute-start(bf16[192,512]{1,0:T(8,128)(2,1)S(1)} %collective-permute-done.8.a1), channel_id=1, source_target_pairs={{0,8},{8,0},{16,24},{24,16},{1,9},{9,1},{17,25},{25,17},{2,10},{10... | collective-permute-start | bytes 589832 | tf_op jit(solution)/shard_map/ppermute | solution.py:325
  40.0 5.6 %collective-permute-start.13 = (bf16[192,512]{1,0:T(8,128)(2,1)S(1)}, bf16[192,512]{1,0:T(8,128)(2,1)S(1)}, u32[]{:S(2)}, u32[]{:S(2)}) collective-permute-start(bf16[192,512]{1,0:T(8,128)(2,1)S(1)} %collective-permute-done.11.c0), channel_id=1, source_target_pairs={{0,8},{8,0},{16,24},{24,16},{1,9},{9,1},{17,25},{25,17},{2,10},{10... | collective-permute-start | bytes 589832 | tf_op jit(solution)/shard_map/ppermute | solution.py:325
  43.4 3.2 %collective-permute-start.14 = (bf16[192,512]{1,0:T(8,128)(2,1)S(1)}, bf16[192,512]{1,0:T(8,128)(2,1)S(1)}, u32[]{:S(2)}, u32[]{:S(2)}) collective-permute-start(bf16[192,512]{1,0:T(8,128)(2,1)S(1)} %collective-permute-done.12.c1), channel_id=1, source_target_pairs={{0,8},{8,0},{16,24},{24,16},{1,9},{9,1},{17,25},{25,17},{2,10},{10... | collective-permute-start | bytes 589832 | tf_op jit(solution)/shard_map/ppermute | solution.py:325
  50.3 0.6 copy-start.9
  50.9 4.7 %collective-permute-start.15 = (bf16[48,256]{1,0:T(8,128)(2,1)}, bf16[48,256]{1,0:T(8,128)(2,1)}, u32[]{:S(2)}, u32[]{:S(2)}) collective-permute-start(bf16[48,256]{1,0:T(8,128)(2,1)} %get-tuple-element.21), channel_id=1, source_target_pairs={{0,2},{1,3},{2,0},{3,1},{4,6},{5,7},{6,4},{7,5},{8,10},{9,11},{10,... | collective-permute-start | bytes 73736 | tf_op jit(solution)/shard_map/ppermute | solution.py:319
  51.2 4.4 %collective-permute-start.16 = (bf16[48,256]{1,0:T(8,128)(2,1)}, bf16[48,256]{1,0:T(8,128)(2,1)}, u32[]{:S(2)}, u32[]{:S(2)}) collective-permute-start(bf16[48,256]{1,0:T(8,128)(2,1)} %get-tuple-element.22), channel_id=1, source_target_pairs={{0,4},{1,5},{2,6},{3,7},{4,0},{5,1},{6,2},{7,3},{8,12},{9,13},{10,... | collective-permute-start | bytes 73736 | tf_op jit(solution)/shard_map/ppermute | solution.py:319
  53.5 5.2 %collective-permute-start.17 = (bf16[48,256]{1,0:T(8,128)(2,1)}, bf16[48,256]{1,0:T(8,128)(2,1)}, u32[]{:S(2)}, u32[]{:S(2)}) collective-permute-start(bf16[48,256]{1,0:T(8,128)(2,1)} %get-tuple-element.23), channel_id=1, source_target_pairs={{0,6},{1,7},{2,4},{3,5},{4,2},{5,3},{6,0},{7,1},{8,14},{9,15},{10,... | collective-permute-start | bytes 73736 | tf_op jit(solution)/shard_map/ppermute | solution.py:319
  58.7 0.9 %copy-start.3 = (bf16[1,48,1536]{2,1,0:T(8,128)(2,1)S(1)}, bf16[1,48,1536]{2,1,0:T(8,128)(2,1)}, u32[]{:S(2)}) copy-start(bf16[1,48,1536]{2,1,0:T(8,128)(2,1)} %param.11) | copy-start | bytes 442372
  59.6 0.7 %copy-start.5 = (f32[1,3,1536]{2,1,0:T(4,128)S(1)}, f32[1,3,1536]{2,1,0:T(4,128)}, u32[]{:S(2)}) copy-start(f32[1,3,1536]{2,1,0:T(4,128)} %copy-done.4) | copy-start | bytes 55300
  60.3 0.7 %copy-start.7 = (f32[3,1536]{1,0:T(4,128)S(1)}, f32[3,1536]{1,0:T(4,128)}, u32[]{:S(2)}) copy-start(f32[3,1536]{1,0:T(4,128)} %block_mod.3) | copy-start | bytes 55300
  61.1 0.7 %copy-start.8 = (f32[1,48,64]{2,1,0:T(8,128)S(1)}, f32[1,48,64]{2,1,0:T(8,128)}, u32[]{:S(2)}) copy-start(f32[1,48,64]{2,1,0:T(8,128)} %param.12) | copy-start | bytes 36868
  61.8 0.7 %copy-start.10 = (bf16[48,256]{1,0:T(8,128)(2,1)S(1)}, bf16[48,256]{1,0:T(8,128)(2,1)}, u32[]{:S(2)}) copy-start(bf16[48,256]{1,0:T(8,128)(2,1)} %copy-done.9) | copy-start | bytes 73732
  64.9 6.7 %collective-permute-start.18 = (f32[1,48,64]{2,1,0:T(8,128)S(1)}, f32[1,48,64]{2,1,0:T(8,128)S(1)}, u32[]{:S(2)}, u32[]{:S(2)}) collective-permute-start(f32[1,48,64]{2,1,0:T(8,128)S(1)} %bitcast.23), channel_id=1, source_target_pairs={{0,24},{8,0},{16,8},{24,16},{1,25},{9,1},{17,9},{25,17},{2,26},{10... | collective-permute-start | bytes 36872 | tf_op jit(solution)/shard_map/ppermute | solution.py:28

commit v2 on v1

--- a/solution.py
+++ b/solution.py
@@ -140,42 +140,57 @@
     return (updated.astype(jnp.bfloat16)[None], moved)
 
 
-def vmem_call(kernel, outs, name, flops, scratch=()):
+def vmem_call(kernel, outs, name, flops, scratch=(), placed=0):
     whole = pl.BlockSpec(memory_space=pltpu.VMEM)
-
-    def call(scalars, *operands):
+    stay = pl.BlockSpec(memory_space=pltpu.HBM)
+
+    def call(*operands):
         return pl.pallas_call(
             kernel,
             out_shape=[jax.ShapeDtypeStruct(shape, dtype) for shape, dtype in outs],
-            in_specs=[pl.BlockSpec(memory_space=pltpu.SMEM)] + [whole] * len(operands),
+            in_specs=[whole] * (len(operands) - placed) + [stay] * placed,
             out_specs=[whole] * len(outs),
             scratch_shapes=list(scratch),
             compiler_params=pltpu.CompilerParams(vmem_limit_bytes=VMEM_LIMIT),
             cost_estimate=pl.CostEstimate(flops=flops, bytes_accessed=1 << 20, transcendentals=0),
             name=name,
-        )(scalars, *operands)
+        )(*operands)
 
     return call
+
+
+def here():
+    slab, seq = lax.axis_index("slab"), lax.axis_index("seq")
+    return seq // 2, seq % 2, slab % 2, slab // 2
 
 
 def dot_rows(left, right):
     return lax.dot_general(left, right, (((1,), (1,)), ((), ())), preferred_element_type=F32)
 
 
+def modulated(rows, time_mod, block_mod):
+    shift = block_mod[0:1] + time_mod[0]
+    scale = 1.0 + (block_mod[1:2] + time_mod[1])
+    return (layer_norm(rows[...].astype(F32)) * scale + shift).astype(BF16)
+
+
+def own_kernel(x1, x2, time_mod, block_mod, w_own, modded, own):
+    for step, rows in enumerate((x1, x2)):
+        modded[step * TOK_DEV : (step + 1) * TOK_DEV, :] = modulated(rows, time_mod, block_mod)
+    own[...] = jnp.dot(modded[...], w_own[...], preferred_element_type=F32).astype(BF16)
+
+
 def project_kernel(
-    place, x0, x1, x2, x3, time_mod, block_mod, w_own, w_first, w_second,
-    near_out, far_out, keep_out, sums_out, modded, mixed,
-):
-    line, side, core = place[0], place[1], place[2]
-    modulation = block_mod[...] + time_mod[...]
-    shift, scale = modulation[0:1], 1.0 + modulation[1:2]
-    for step, rows in enumerate((x0, x1, x2, x3)):
-        normal = layer_norm(rows[...].astype(F32))
-        at = pl.multiple_of(jnp.bitwise_xor(line, step) * TOK_DEV, 16)
-        modded[pl.ds(at, TOK_DEV), :] = (normal * scale + shift).astype(BF16)
+    x3, x0, time_mod, block_mod, w_own, w_first, w_second, modded_in, own_in,
+    far_out, near_out, keep_out, sums_out, modded, mixed,
+):
+    line, side, core, _ = here()
     half = D // 2
     width = w_own.shape[1]
-    own = jnp.dot(modded[...], w_own[...], preferred_element_type=F32)
+    modded[:TOK_DEV, :] = modulated(x0, time_mod, block_mod)
+    modded[TOK_DEV : 2 * TOK_DEV, :] = modulated(x3, time_mod, block_mod)
+    modded[2 * TOK_DEV :, :] = modded_in[...]
+    late = jnp.dot(modded[: 2 * TOK_DEV, :], w_own[...], preferred_element_type=F32).astype(BF16)
     other = jnp.dot(
         modded[:, pl.ds(pl.multiple_of(core * half, half), half)], w_first[...],
         preferred_element_type=F32,
@@ -184,8 +199,18 @@
         modded[:, pl.ds(pl.multiple_of((1 - core) * half, half), half)], w_second[...],
         preferred_element_type=F32,
     )
-    mixed[:, pl.ds(pl.multiple_of(side * width, width), width)] = own.astype(BF16)
-    mixed[:, pl.ds(pl.multiple_of((1 - side) * width, width), width)] = other.astype(BF16)
+    other = other.astype(BF16)
+    mine = pl.multiple_of(side * width, width)
+    there = pl.multiple_of((1 - side) * width, width)
+    for place, step in enumerate((0, 3, 1, 2)):
+        at = pl.multiple_of(jnp.bitwise_xor(line, step) * TOK_DEV, 16)
+        rows = slice(place * TOK_DEV, (place + 1) * TOK_DEV)
+        if place < 2:
+            mixed[pl.ds(at, TOK_DEV), pl.ds(mine, width)] = late[rows]
+        else:
+            behind = slice((place - 2) * TOK_DEV, (place - 1) * TOK_DEV)
+            mixed[pl.ds(at, TOK_DEV), pl.ds(mine, width)] = own_in[behind, :]
+        mixed[pl.ds(at, TOK_DEV), pl.ds(there, width)] = other[rows]
     ones = jnp.ones((16, PAIR), BF16)
     row_id = lax.broadcasted_iota(jnp.int32, (16, ROWS), 0)
     picked = jnp.zeros((16, ROWS), F32)
@@ -216,9 +241,15 @@
 
 
 def rope_kernel(
-    place, keep, near, far, own_sums, last_sums, gains, cosines, sines, q_out, kv_out, units
-):
-    line = place[0]
+    far, last_sums, near, keep, own_sums, gains, cosines, sines, q_out, kv_out, units
+):
+    line, _, _, _ = here()
+    upper, odd = line // 2, line % 2
+    slots = (
+        jnp.where(upper == 1, 2, odd),
+        jnp.where((line == 0) | (line == 3), 1, 0),
+        jnp.where(upper == 0, 2, 1 - odd),
+    )
     units[0] = keep[...]
     units[1] = near[:ROWS, :]
     units[2] = far[:ROWS, :]
@@ -235,85 +266,123 @@
             total += jnp.sum(jnp.where(wanted, piece, 0.0), axis=0, keepdims=True)
         scale = lax.rsqrt(total * (1.0 / ATT) + 1e-06)
         scale = jnp.transpose(jnp.broadcast_to(scale, (HEAD_DIM, PAIR)))[:ROWS]
-        values = units[place[3 + kind]].astype(F32)
+        values = units[slots[kind]].astype(F32)
         for head in range(2):
             columns = slice(head * HEAD_DIM, (head + 1) * HEAD_DIM)
             at = pl.multiple_of(line * PAIR + head * HEAD_DIM, HEAD_DIM)
             scaled = values[:, columns] * scale * gains[kind : kind + 1, pl.ds(at, HEAD_DIM)]
             turned = scaled * cos + pltpu.roll(scaled, HEAD_DIM // 2, axis=1) * sin
             (kv_out if kind else q_out)[:, columns] = turned.astype(BF16)
-    kv_out[:, PAIR:] = units[place[5]]
-
-
-def attend_kernel(
-    place, queries, a0, a1, b0, b1, c0, c1, d0, d1, o0, o1, o2, o3, result, accum, highest, sums
-):
-    line = place[0]
-    accum[...] = jnp.zeros_like(accum)
-    sums[...] = jnp.zeros_like(sums)
-    highest[...] = jnp.full_like(highest, -1e30)
-
-    def group(one, two):
-        for head in range(2):
-            columns = slice(head * HEAD_DIM, (head + 1) * HEAD_DIM)
-            value_columns = slice(PAIR + head * HEAD_DIM, PAIR + (head + 1) * HEAD_DIM)
-            keys = jnp.concatenate([one[:, columns], two[:, columns]], axis=0)
-            values = jnp.concatenate([one[:, value_columns], two[:, value_columns]], axis=0)
-            scores = dot_rows(queries[:, columns], keys) * HEAD_DIM ** (-0.5)
-            maxima = jnp.max(scores, axis=-1, keepdims=True)
-            weights = jnp.exp(scores - maxima).astype(BF16)
-            totals = jnp.sum(weights.astype(F32), axis=-1, keepdims=True)
-            output = jnp.dot(weights, values, preferred_element_type=F32)
-            old = highest[head]
-            new = jnp.maximum(old, maxima)
-            keep_old, keep_new = jnp.exp(old - new), jnp.exp(maxima - new)
-            highest[head] = new
-            sums[head] = sums[head] * keep_old + totals * keep_new
-            accum[head] = accum[head] * keep_old + output * keep_new
-
-    group(a0, a1)
-    pl.when(place[2] == 1)(lambda: group(b0, b1))
-    pl.when(place[6] == 1)(lambda: group(c0, c1))
-    pl.when(place[6] == 1)(lambda: group(d0, d1))
+    kv_out[:, PAIR:] = units[slots[2]]
+
+
+def attend_group(queries, one, two, state):
+    total, highest = state
+    ones = jnp.ones((2 * ROWS, HEAD_DIM), BF16)
     for head in range(2):
         columns = slice(head * HEAD_DIM, (head + 1) * HEAD_DIM)
-        result[:, columns] = (accum[head] / sums[head]).astype(BF16)
+        value_columns = slice(PAIR + head * HEAD_DIM, PAIR + (head + 1) * HEAD_DIM)
+        keys = jnp.concatenate([one[:, columns], two[:, columns]], axis=0)
+        values = jnp.concatenate([one[:, value_columns], two[:, value_columns]], axis=0)
+        scores = dot_rows(queries[:, columns], keys) * HEAD_DIM ** (-0.5)
+        maxima = jnp.max(scores, axis=-1, keepdims=True)
+        weights = jnp.exp(scores - maxima).astype(BF16)
+        output = jnp.dot(
+            weights, jnp.concatenate([values, ones], axis=1), preferred_element_type=F32
+        )
+        old = highest[head]
+        new = jnp.maximum(old, maxima)
+        keep_old, keep_new = jnp.exp(old - new), jnp.exp(maxima - new)
+        highest[head] = new
+        for part in range(2):
+            lanes = slice(part * HEAD_DIM, (part + 1) * HEAD_DIM)
+            total[head, :, lanes] = total[head, :, lanes] * keep_old + output[:, lanes] * keep_new
+
+
+def own_attend_kernel(queries, a0, a1, total, highest):
+    total[...] = jnp.zeros_like(total)
+    highest[...] = jnp.full_like(highest, -1e30)
+    attend_group(queries, a0, a1, (total, highest))
+
+
+def next_attend_kernel(which, queries, one, two, total_in, highest_in, total, highest):
+    total[...] = total_in[...]
+    highest[...] = highest_in[...]
+    pl.when(here()[which] == 1)(lambda: attend_group(queries, one, two, (total, highest)))
+
+
+def last_attend_kernel(
+    queries, d0, d1, total_in, highest_in, o3, o2, o1, o0, total, highest, result
+):
+    line, _, _, chip = here()
+    total[...] = total_in[...]
+    highest[...] = highest_in[...]
+    pl.when(chip == 1)(lambda: attend_group(queries, d0, d1, (total, highest)))
+    for head in range(2):
+        columns = slice(head * HEAD_DIM, (head + 1) * HEAD_DIM)
+        result[:, columns] = (total[head, :, :HEAD_DIM] / total[head, :, HEAD_DIM:]).astype(BF16)
     for step, out in enumerate((o0, o1, o2, o3)):
         at = pl.multiple_of(jnp.bitwise_xor(line, step) * TOK_DEV, 16)
         out[...] = result[pl.ds(at, TOK_DEV), :]
 
 
+def load(sources, held, arrived):
+    copies = [
+        pltpu.make_async_copy(source, target, arrived.at[i])
+        for i, (source, target) in enumerate(zip(sources, held))
+    ]
+    for copy in copies:
+        copy.start()
+    return copies
+
+
+def times_w_out(rows, w_out, step):
+    at = pl.multiple_of(jnp.bitwise_xor(here()[0], step) * PAIR, PAIR)
+    return jnp.dot(rows[...], w_out[pl.ds(at, PAIR), :], preferred_element_type=F32)
+
+
+def begin_kernel(
+    r0, w_out, stream_in, time_in, block_in, head_in, base, vectors,
+    stream, time_mod, block_mod, head_mod, arrived,
+):
+    copies = load(
+        (stream_in, time_in, block_in, head_in), (stream, time_mod, block_mod, head_mod), arrived
+    )
+    projected = times_w_out(r0, w_out, 0)
+    for copy in copies:
+        copy.wait()
+    gate = block_mod[2:3] + time_mod[2]
+    base[...] = stream[...].astype(F32) + gate * projected
+    vectors[0:1] = gate
+    vectors[1:2] = 1.0 + head_mod[1:2]
+    vectors[2:3] = head_mod[0:1]
+
+
 def finish_kernel(
-    place, r0, r1, r2, r3, w_out, stream, time_mod, block_mod, head_mod, w_head, latents,
-    stream_out, latents_out,
-):
-    line = place[0]
-    projected = jnp.zeros((TOK_DEV, D), F32)
-    for step, rows in enumerate((r0, r1, r2, r3)):
-        at = pl.multiple_of(jnp.bitwise_xor(line, step) * PAIR, PAIR)
-        projected += jnp.dot(rows[...], w_out[pl.ds(at, PAIR), :], preferred_element_type=F32)
-    gate = block_mod[2:3] + time_mod[2:3]
-    updated = stream[...].astype(F32) + gate * projected
+    r3, r2, r1, w_out, base, vectors, w_head, levels, latents_in, stream_out, latents_out,
+    latents, arrived,
+):
+    copies = load((latents_in,), (latents,), arrived)
+    projected = times_w_out(r3, w_out, 3) + times_w_out(r2, w_out, 2) + times_w_out(r1, w_out, 1)
+    updated = base[...] + vectors[0:1] * projected
     stream_out[...] = updated.astype(BF16)
-    head_in = (layer_norm(updated) * (1.0 + head_mod[1:2]) + head_mod[0:1]).astype(BF16)
-    velocity = jnp.dot(head_in, w_head[...], preferred_element_type=F32)
+    head_in = (layer_norm(updated) * vectors[1:2] + vectors[2:3]).astype(BF16)
+    velocity = dot_rows(head_in, w_head[...])
 
     def sigma(level):
-        fraction = jnp.full((1, CHAN), level, jnp.int32).astype(F32) / LEVELS
+        fraction = level.astype(F32) / LEVELS
         return 5.0 * fraction / (1.0 + 4.0 * fraction)
 
-    latents_out[...] = latents[...] + (sigma(place[7] - 1) - sigma(place[7])) * velocity
+    level = levels[...]
+    copies[0].wait()
+    latents_out[...] = latents[...] + (sigma(level - 1) - sigma(level)) * velocity
 
 
 def lines(
     stream, latents, time_mod, block_mod, w_qkv, qk_gain, w_out, head_mod, w_head, noise_level
 ):
     slab, seq = lax.axis_index("slab"), lax.axis_index("seq")
-    line, side, core = seq // 2, seq % 2, slab % 2
-    slots = jnp.array([[0, 1, 2], [1, 0, 2], [2, 0, 1], [2, 1, 0]], jnp.int32)[line]
-    place = jnp.concatenate(
-        [jnp.stack([line, side, core]), slots, (slab // 2)[None], noise_level]
-    ).astype(jnp.int32)
+    side, core = seq % 2, slab % 2
 
     def along(step, value):
         return lax.ppermute(value, "seq", [(i, i ^ (2 * step)) for i in range(2 * LINE)])
@@ -330,10 +399,9 @@
         return lax.ppermute(value, ("slab", "seq"), pairs)
 
     rows = stream[0]
+    time_rows = time_mod.transpose(1, 0, 2)
     w_first = across(lax.dynamic_slice_in_dim(w_qkv, core * (D // 2), D // 2, 0))
     x3, x2, x1 = along(3, rows), along(2, rows), along(1, rows)
-    w_second = cores(w_first)
-
     at = (jnp.arange(LINE)[:, None] * 2 + side) * TOK_DEV + jnp.arange(TOK_DEV)[None]
     position = (slab * (2 * LINE * TOK_DEV) + at.reshape(ROWS)).astype(F32)
     halves = HEAD_DIM // 2
@@ -343,36 +411,55 @@
     cosines = jnp.concatenate([cosines, cosines], axis=1)
     sines = jnp.concatenate([-sines, sines], axis=1)
 
+    width = w_qkv.shape[1]
+    modded, own = vmem_call(
+        own_kernel, [((2 * TOK_DEV, D), BF16), ((2 * TOK_DEV, width), BF16)], "own", 1 << 28
+    )(x1, x2, time_rows, block_mod, w_qkv)
+    w_second = cores(w_first)
     message = (ROWS + 16, PAIR)
-    near, far, keep, sums = vmem_call(
+    far, near, keep, sums = vmem_call(
         project_kernel,
         [(message, BF16), (message, BF16), ((ROWS, PAIR), BF16), ((16, PAIR), BF16)],
-        "project", 2 * ROWS * D * 3 * PAIR,
+        "project", 1 << 28,
         [pltpu.VMEM((ROWS, D), BF16), pltpu.VMEM((ROWS, 3 * PAIR), BF16)],
-    )(place, rows, x1, x2, x3, time_mod[0], block_mod, w_qkv, w_first, w_second)
-    far, near, last_sums = along(2, far), along(1, near), along(3, sums)
+    )(x3, rows, time_rows, block_mod, w_qkv, w_first, w_second, modded, own)
+    far, last_sums, near = along(2, far), along(3, sums), along(1, near)
     queries, pairs = vmem_call(
         rope_kernel,
         [((ROWS, PAIR), BF16), ((ROWS, 2 * PAIR), BF16)],
         "rope", 1 << 22, [pltpu.VMEM((3, ROWS, PAIR), BF16)],
-    )(place, keep, near, far, sums, last_sums, qk_gain, cosines, sines)
-    core_pairs = cores(pairs)
-    side_pairs = across(pairs)
-    chip_pairs = chips(pairs, 0)
-    both_pairs = chips(pairs, 1)
-    shape, dtype = (TOK_DEV, PAIR), BF16
-    state = pltpu.VMEM((2, ROWS, 1), F32)
-    parts = vmem_call(
-        attend_kernel, [(shape, dtype)] * 4, "attend", 1 << 28,
-        [pltpu.VMEM((ROWS, PAIR), BF16), pltpu.VMEM((2, ROWS, HEAD_DIM), F32), state, state],
-    )(
-        place, queries, pairs, side_pairs, core_pairs, cores(side_pairs),
-        chip_pairs, both_pairs, cores(chip_pairs), cores(both_pairs),
-    )
-    taken = [parts[0]] + [along(step, parts[step]) for step in (1, 2, 3)]
+    )(far, last_sums, near, keep, sums, qk_gain, cosines, sines)
+    chip_pairs, both_pairs = chips(pairs, 0), chips(pairs, 1)
+    side_pairs, core_pairs = across(pairs), cores(pairs)
+    state = [((2, ROWS, PAIR), F32), ((2, ROWS, HEAD_DIM), F32)]
+    held = [pltpu.VMEM(shape, dtype) for shape, dtype in state]
+    now = vmem_call(own_attend_kernel, state, "attend_own", 1 << 27)(queries, pairs, side_pairs)
+    now, chip_pairs, both_pairs, side_pairs = lax.optimization_barrier(
+        (now, chip_pairs, both_pairs, side_pairs)
+    )
+    core_side, core_chip, core_both = cores(side_pairs), cores(chip_pairs), cores(both_pairs)
+    for name, which, blocks in (
+        ("attend_core", 2, (core_pairs, core_side)),
+        ("attend_chip", 3, (chip_pairs, both_pairs)),
+    ):
+        kernel = functools.partial(next_attend_kernel, which)
+        now = vmem_call(kernel, state, name, 1 << 27)(queries, *blocks, *now)
+    part3, part2, part1, part0 = vmem_call(
+        last_attend_kernel, [((TOK_DEV, PAIR), BF16)] * 4, "attend_last", 1 << 27,
+        held + [pltpu.VMEM((ROWS, PAIR), BF16)],
+    )(queries, core_chip, core_both, *now)
+    late = [along(3, part3), along(2, part2), along(1, part1)]
+    loaded = (rows, time_rows, block_mod, head_mod[0])
+    base, vectors = vmem_call(
+        begin_kernel, [((TOK_DEV, D), F32), ((8, D), F32)], "begin", 1 << 28,
+        [pltpu.VMEM(v.shape, v.dtype) for v in loaded] + [pltpu.SemaphoreType.DMA((len(loaded),))],
+        placed=len(loaded),
+    )(part0, w_out, *loaded)
+    level = jnp.broadcast_to(noise_level[:, None], (1, CHAN))
     new_stream, stepped = vmem_call(
-        finish_kernel, [((TOK_DEV, D), BF16), ((TOK_DEV, CHAN), F32)], "finish", 1 << 28
-    )(place, *taken, w_out, rows, time_mod[0], block_mod, head_mod[0], w_head, latents[0])
+        finish_kernel, [((TOK_DEV, D), BF16), ((TOK_DEV, CHAN), F32)], "finish", 1 << 28,
+        [pltpu.VMEM((TOK_DEV, CHAN), F32), pltpu.SemaphoreType.DMA((1,))], placed=1,
+    )(*late, w_out, base, vectors, w_head.T, level, latents[0])
     return (new_stream[None], from_behind(stepped[None], "slab", -1))
 
 

time: 72.8 us -> 61 us (0.84)
  local copies, waits for them, and re-layouts: 9.05 us -> 1.95 us
  Pallas kernels: 9.08 us -> 5.77 us
  starting transfers between devices: 29 us -> 27.7 us
    unnamed x29 -> x19, local copies, waits for them, and re-layouts: 6.98 us -> 0.65 us
    pallas_call x4 -> x9, Pallas kernels: 9.08 us -> 5.77 us  [call(): pl.pallas_call(kernel, out_shape=[jax.ShapeDtypeStruct(shape, dtype) for...]
    ppermute x5, starting transfers between devices: 9.21 us -> 7.14 us  [cores(): return lax.ppermute(value, 'slab', [(i, i ^ 1) for i in range(4)])]
    ppermute x2, waiting for transfers between devices: 0.01 us -> 1.78 us  [chips(): return lax.ppermute(value, ('slab', 'seq'), pairs)]
    ppermute x1, waiting for transfers between devices: 6.08 us -> 4.34 us  [from_behind(): return lax.ppermute(value, axis, pairs)]
    ppermute x2, waiting for transfers between devices: 8.04 us -> 9.44 us  [across(): return lax.ppermute(value, 'seq', [(i, i ^ 1) for i in range(2 * LINE)])]
    ppermute x5, waiting for transfers between devices: 1.29 us -> 0.41 us  [cores(): return lax.ppermute(value, 'slab', [(i, i ^ 1) for i in range(4)])]
  transfers between devices with their start and end apart: 19 -> 19, of which waited for: 6 -> 7; matrix products, arithmetic and copies ran while one was open for 5% -> 1% of each run, Pallas kernels for 0% -> 4%
where the time goes in v2:
time: 61 us; the launch traced here: 60.8 us
  starting transfers between devices  27.7 us (45%)
  waiting for transfers between devices  23.2 us (38%)
  Pallas kernels  5.77 us (9%)
  local copies, waits for them, and re-layouts  1.95 us (3%)
  between operations  1.57 us (3%)
  other arithmetic  0.63 us (1%)
    ppermute x9, starting transfers between devices, along(): lax.ppermute(value, 'seq', [(i, i ^ 2 * step) for i in range(2 * LINE)])  11.2 us
    ppermute x2, waiting for transfers between devices, across(): return lax.ppermute(value, 'seq', [(i, i ^ 1) for i in range(2 * LINE)])  9.44 us
    ppermute x9, waiting for transfers between devices, along(): lax.ppermute(value, 'seq', [(i, i ^ 2 * step) for i in range(2 * LINE)])  7.22 us
    ppermute x5, starting transfers between devices, cores(): return lax.ppermute(value, 'slab', [(i, i ^ 1) for i in range(4)])  7.14 us
    pallas_call x9, Pallas kernels, call(): pl.pallas_call(kernel, out_shape=[jax.ShapeDtypeStruct(shape, dtype) for...  5.77 us
    ppermute x2, starting transfers between devices, chips(): return lax.ppermute(value, ('slab', 'seq'), pairs)  4.38 us
    ppermute x1, waiting for transfers between devices, from_behind(): return lax.ppermute(value, axis, pairs)  4.34 us
    ppermute x2, starting transfers between devices, across(): return lax.ppermute(value, 'seq', [(i, i ^ 1) for i in range(2 * LINE)])  3.68 us
  transfers between devices with their start and end apart: 19, of which 7 were waited for; matrix products, arithmetic and copies ran while one was open for 1% of the time, Pallas kernels for 4%

profile of v2, /device:TPU:1, one launch (start us, length us, event | category | flops | bytes accessed | tf_op | source)
XLA Modules:
  0.0 60.8 jit_solution(1236479244691827591)
XLA Ops:
  0.7 1.2 %constant_dynamic-slice_fusion = bf16[768,384]{1,0:T(8,128)(2,1)S(1)} fusion(bf16[1536,384]{1,0:T(8,128)(2,1)} %w_own.3, s32[]{:T(128)S(6)} %select_n.15), kind=kLoop, calls=%fused_computation.8 | loop fusion | bytes 1179652 | tf_op jit(solution)/shard_map/dynamic_slice | solution.py:403
  1.9 2.1 %collective-permute-start.1 = (bf16[768,384]{1,0:T(8,128)(2,1)S(1)}, bf16[768,384]{1,0:T(8,128)(2,1)S(1)}, u32[]{:S(2)}, u32[]{:S(2)}) collective-permute-start(bf16[768,384]{1,0:T(8,128)(2,1)S(1)} %constant_dynamic-slice_fusion), channel_id=1, source_target_pairs={{0,1},{1,0},{2,3},{3,2},{4,5},{5,4},{6,7},{7,6},{8,9},{9,8},{10,11... | collective-permute-start | bytes 1769480 | tf_op jit(solution)/shard_map/ppermute | solution.py:391
  4.0 1.3 %collective-permute-start.3 = (bf16[48,1536]{1,0:T(8,128)(2,1)}, bf16[48,1536]{1,0:T(8,128)(2,1)S(1)}, u32[]{:S(2)}, u32[]{:S(2)}) collective-permute-start(bf16[48,1536]{1,0:T(8,128)(2,1)} %bitcast.9), channel_id=1, source_target_pairs={{0,2},{1,3},{2,0},{3,1},{4,6},{5,7},{6,4},{7,5},{8,10},{9,11},{10,... | collective-permute-start | bytes 442376 | tf_op jit(solution)/shard_map/ppermute | solution.py:388
  5.3 2.3 %collective-permute-start.4 = (bf16[48,1536]{1,0:T(8,128)(2,1)}, bf16[48,1536]{1,0:T(8,128)(2,1)S(1)}, u32[]{:S(2)}, u32[]{:S(2)}) collective-permute-start(bf16[48,1536]{1,0:T(8,128)(2,1)} %bitcast.10), channel_id=1, source_target_pairs={{0,4},{1,5},{2,6},{3,7},{4,0},{5,1},{6,2},{7,3},{8,12},{9,13},{10,... | collective-permute-start | bytes 442376 | tf_op jit(solution)/shard_map/ppermute | solution.py:388
  7.7 9.4 %collective-permute-done.1.w_first = bf16[768,384]{1,0:T(8,128)(2,1)S(1)} collective-permute-done((bf16[768,384]{1,0:T(8,128)(2,1)S(1)}, bf16[768,384]{1,0:T(8,128)(2,1)S(1)}, u32[]{:S(2)}, u32[]{:S(2)}) %collective-permute-start.1) | collective-permute-done | bytes 589856 | tf_op jit(solution)/shard_map/ppermute | solution.py:391
  17.1 1.2 %collective-permute-start.2 = (bf16[768,384]{1,0:T(8,128)(2,1)S(1)}, bf16[768,384]{1,0:T(8,128)(2,1)S(1)}, u32[]{:S(2)}, u32[]{:S(2)}) collective-permute-start(bf16[768,384]{1,0:T(8,128)(2,1)S(1)} %collective-permute-done.1.w_first), channel_id=1, source_target_pairs={{0,8},{8,0},{16,24},{24,16},{1,9},{9,1},{17,25},{25,17},{2,10},{10... | collective-permute-start | bytes 1769480 | tf_op jit(solution)/shard_map/ppermute | solution.py:394
  18.5 0.4 fusion
  19.0 0.6 own.1
  19.6 0.4 collective-permute-done.2.w_second
  20.0 1.3 %project.1 = (bf16[208,256]{1,0:T(8,128)(2,1)S(1)}, bf16[208,256]{1,0:T(8,128)(2,1)S(1)}, bf16[192,256]{1,0:T(8,128)(2,1)S(1)}, bf16[16,256]{1,0:T(8,128)(2,1)S(1)}) custom-call(bf16[48,1536]{1,0:T(8,128)(2,1)S(1)} %collective-permute-done.x3, bf16[48,1536]{1,0:T(8,128)(2,1)S(1)} %bitcast.12, f32[3,1,1536]{2,1,0:T(1,128)S(1)} %bitcast.16, ...), custom_call_target="tpu_custom_call" | custom-call | flops 268435456 | bytes 1048576 | tf_op jit(solution)/shard_map/project/pallas_call | solution.py:148
  21.3 2.6 %collective-permute-start.5 = (bf16[208,256]{1,0:T(8,128)(2,1)S(1)}, bf16[208,256]{1,0:T(8,128)(2,1)S(1)}, u32[]{:S(2)}, u32[]{:S(2)}) collective-permute-start(bf16[208,256]{1,0:T(8,128)(2,1)S(1)} %get-tuple-element.31), channel_id=1, source_target_pairs={{0,4},{1,5},{2,6},{3,7},{4,0},{5,1},{6,2},{7,3},{8,12},{9,13},{10,... | collective-permute-start | bytes 319496 | tf_op jit(solution)/shard_map/ppermute | solution.py:388
  23.9 1.3 %collective-permute-start.7 = (bf16[208,256]{1,0:T(8,128)(2,1)S(1)}, bf16[208,256]{1,0:T(8,128)(2,1)S(1)}, u32[]{:S(2)}, u32[]{:S(2)}) collective-permute-start(bf16[208,256]{1,0:T(8,128)(2,1)S(1)} %get-tuple-element.33), channel_id=1, source_target_pairs={{0,2},{1,3},{2,0},{3,1},{4,6},{5,7},{6,4},{7,5},{8,10},{9,11},{10,... | collective-permute-start | bytes 319496 | tf_op jit(solution)/shard_map/ppermute | solution.py:388
  25.3 4.3 %collective-permute-done.6.last_sums = bf16[16,256]{1,0:T(8,128)(2,1)S(1)} collective-permute-done((bf16[16,256]{1,0:T(8,128)(2,1)S(1)}, bf16[16,256]{1,0:T(8,128)(2,1)S(1)}, u32[]{:S(2)}, u32[]{:S(2)}) %collective-permute-start.6) | collective-permute-done | bytes 8224 | tf_op jit(solution)/shard_map/ppermute | solution.py:388
  29.6 0.3 rope.1
  29.9 1.6 %collective-permute-start.8 = (bf16[192,512]{1,0:T(8,128)(2,1)S(1)}, bf16[192,512]{1,0:T(8,128)(2,1)S(1)}, u32[]{:S(2)}, u32[]{:S(2)}) collective-permute-start(bf16[192,512]{1,0:T(8,128)(2,1)S(1)} %get-tuple-element.36.a0), channel_id=1, source_target_pairs={{0,1},{1,0},{2,3},{3,2},{4,5},{5,4},{6,7},{7,6},{8,9},{9,8},{10,11... | collective-permute-start | bytes 589832 | tf_op jit(solution)/shard_map/ppermute | solution.py:391
  31.5 2.8 %collective-permute-start.10 = (bf16[192,512]{1,0:T(8,128)(2,1)S(1)}, bf16[192,512]{1,0:T(8,128)(2,1)S(1)}, u32[]{:S(2)}, u32[]{:S(2)}) collective-permute-start(bf16[192,512]{1,0:T(8,128)(2,1)S(1)} %get-tuple-element.36.a0), channel_id=1, source_target_pairs={{0,17},{1,16},{2,19},{3,18},{4,21},{5,20},{6,23},{7,22},{8,25},{9,... | collective-permute-start | bytes 589832 | tf_op jit(solution)/shard_map/ppermute | solution.py:399
  34.3 1.6 %collective-permute-start.9 = (bf16[192,512]{1,0:T(8,128)(2,1)S(1)}, bf16[192,512]{1,0:T(8,128)(2,1)S(1)}, u32[]{:S(2)}, u32[]{:S(2)}) collective-permute-start(bf16[192,512]{1,0:T(8,128)(2,1)S(1)} %get-tuple-element.36.a0), channel_id=1, source_target_pairs={{0,16},{1,17},{2,18},{3,19},{4,20},{5,21},{6,22},{7,23},{8,24},{9,... | collective-permute-start | bytes 589832 | tf_op jit(solution)/shard_map/ppermute | solution.py:399
  35.9 2.3 %collective-permute-start.13 = (bf16[192,512]{1,0:T(8,128)(2,1)S(1)}, bf16[192,512]{1,0:T(8,128)(2,1)S(1)}, u32[]{:S(2)}, u32[]{:S(2)}) collective-permute-start(bf16[192,512]{1,0:T(8,128)(2,1)S(1)} %get-tuple-element.36.a0), channel_id=1, source_target_pairs={{0,8},{8,0},{16,24},{24,16},{1,9},{9,1},{17,25},{25,17},{2,10},{10... | collective-permute-start | bytes 589832 | tf_op jit(solution)/shard_map/ppermute | solution.py:394
  38.2 0.6 attend_own.1
  38.8 1.8 %collective-permute-done.9.one = bf16[192,512]{1,0:T(8,128)(2,1)S(1)} collective-permute-done((bf16[192,512]{1,0:T(8,128)(2,1)S(1)}, bf16[192,512]{1,0:T(8,128)(2,1)S(1)}, u32[]{:S(2)}, u32[]{:S(2)}) %collective-permute-start.9) | collective-permute-done | bytes 196640 | tf_op jit(solution)/shard_map/ppermute | solution.py:399
  40.6 3.1 %collective-permute-start.14 = (bf16[192,512]{1,0:T(8,128)(2,1)S(1)}, bf16[192,512]{1,0:T(8,128)(2,1)S(1)}, u32[]{:S(2)}, u32[]{:S(2)}) collective-permute-start(bf16[192,512]{1,0:T(8,128)(2,1)S(1)} %collective-permute-done.8.a1), channel_id=1, source_target_pairs={{0,8},{8,0},{16,24},{24,16},{1,9},{9,1},{17,25},{25,17},{2,10},{10... | collective-permute-start | bytes 589832 | tf_op jit(solution)/shard_map/ppermute | solution.py:394
  43.7 0.5 collective-permute-start.12
  44.9 0.6 %attend_core.1 = (f32[2,192,256]{2,1,0:T(8,128)S(1)}, f32[2,192,128]{2,1,0:T(8,128)S(1)}) custom-call(bf16[192,256]{1,0:T(8,128)(2,1)S(1)} %get-tuple-element.35.queries, bf16[192,512]{1,0:T(8,128)(2,1)S(1)} %collective-permute-done.13.one, bf16[192,512]{1,0:T(8,128)(2,1)S(1)} %collective-permute-done.14.two, f32[2,192,256]{2,1,0:T(8,128)S(1)} %get-tuple-element.42.total_in, ...), custom_call_target="tpu_custom_call" | custom-call | flops 134217728 | bytes 1048576 | tf_op jit(solution)/shard_map/attend_core/pallas_call | solution.py:148
  45.7 3.4 %collective-permute-start.15 = (bf16[48,256]{1,0:T(8,128)(2,1)S(1)}, bf16[48,256]{1,0:T(8,128)(2,1)S(1)}, u32[]{:S(2)}, u32[]{:S(2)}) collective-permute-start(bf16[48,256]{1,0:T(8,128)(2,1)S(1)} %get-tuple-element.48), channel_id=1, source_target_pairs={{0,6},{1,7},{2,4},{3,5},{4,2},{5,3},{6,0},{7,1},{8,14},{9,15},{10,... | collective-permute-start | bytes 73736 | tf_op jit(solution)/shard_map/ppermute | solution.py:388
  49.1 0.3 collective-permute-start.17
  49.4 0.6 begin.1
  50.0 0.2 collective-permute-done.15.r3
  50.3 2.6 %collective-permute-done.16.r2 = bf16[48,256]{1,0:T(8,128)(2,1)S(1)} collective-permute-done((bf16[48,256]{1,0:T(8,128)(2,1)S(1)}, bf16[48,256]{1,0:T(8,128)(2,1)S(1)}, u32[]{:S(2)}, u32[]{:S(2)}) %collective-permute-start.16) | collective-permute-done | bytes 24608 | tf_op jit(solution)/shard_map/ppermute | solution.py:388
  52.9 1.7 %finish.1 = (bf16[48,1536]{1,0:T(8,128)(2,1)}, f32[48,64]{1,0:T(8,128)S(1)}) custom-call(bf16[48,256]{1,0:T(8,128)(2,1)S(1)} %collective-permute-done.15.r3, bf16[48,256]{1,0:T(8,128)(2,1)S(1)} %collective-permute-done.16.r2, bf16[48,256]{1,0:T(8,128)(2,1)S(1)} %collective-permute-done.17.r1, bf16[1024,1536]{1,0:T(8,128)(2,1)S(1)} %copy-done, ...), custom_call_target="tpu_custom_call" | custom-call | flops 268435456 | bytes 1048576 | tf_op jit(solution)/shard_map/finish/pallas_call | solution.py:148
  54.6 1.3 %collective-permute-start.18 = (f32[1,48,64]{2,1,0:T(8,128)S(1)}, f32[1,48,64]{2,1,0:T(8,128)S(1)}, u32[]{:S(2)}, u32[]{:S(2)}) collective-permute-start(f32[1,48,64]{2,1,0:T(8,128)S(1)} %bitcast.20), channel_id=1, source_target_pairs={{0,24},{8,0},{16,8},{24,16},{1,25},{9,1},{17,9},{25,17},{2,26},{10... | collective-permute-start | bytes 36872 | tf_op jit(solution)/shard_map/ppermute | solution.py:28
  55.9 4.3 %collective-permute-done.18 = f32[1,48,64]{2,1,0:T(8,128)S(1)} collective-permute-done((f32[1,48,64]{2,1,0:T(8,128)S(1)}, f32[1,48,64]{2,1,0:T(8,128)S(1)}, u32[]{:S(2)}, u32[]{:S(2)}) %collective-permute-start.18) | collective-permute-done | bytes 12320 | tf_op jit(solution)/shard_map/ppermute | solution.py:28
  60.2 0.6 copy.14
  (42 shorter events, 0.5 us)
Async XLA Ops:
  0.6 18.3 %copy-start.1 = (bf16[1536,384]{1,0:T(8,128)(2,1)S(1)}, bf16[1536,384]{1,0:T(8,128)(2,1)}, u32[]{:S(2)}) copy-start(bf16[1536,384]{1,0:T(8,128)(2,1)} %w_own.3) | copy-start | bytes 3538948
  0.6 18.3 %copy-start.5 = (f32[1,3,1536]{2,0,1:T(1,128)S(1)}, f32[1,3,1536]{2,0,1:T(1,128)}, u32[]{:S(2)}) copy-start(f32[1,3,1536]{2,0,1:T(1,128)} %param.12) | copy-start | bytes 55300
  0.7 18.3 %copy-start.3 = (f32[3,1536]{1,0:T(4,128)S(1)}, f32[3,1536]{1,0:T(4,128)}, u32[]{:S(2)}) copy-start(f32[3,1536]{1,0:T(4,128)} %block_in.1) | copy-start | bytes 55300
  1.9 18.1 %copy-start.2 = (bf16[1,48,1536]{2,1,0:T(8,128)(2,1)S(1)}, bf16[1,48,1536]{2,1,0:T(8,128)(2,1)}, u32[]{:S(2)}) copy-start(bf16[1,48,1536]{2,1,0:T(8,128)(2,1)} %param.10) | copy-start | bytes 442372
  1.9 15.2 %collective-permute-start.1 = (bf16[768,384]{1,0:T(8,128)(2,1)S(1)}, bf16[768,384]{1,0:T(8,128)(2,1)S(1)}, u32[]{:S(2)}, u32[]{:S(2)}) collective-permute-start(bf16[768,384]{1,0:T(8,128)(2,1)S(1)} %constant_dynamic-slice_fusion), channel_id=1, source_target_pairs={{0,1},{1,0},{2,3},{3,2},{4,5},{5,4},{6,7},{7,6},{8,9},{9,8},{10,11... | collective-permute-start | bytes 1769480 | tf_op jit(solution)/shard_map/ppermute | solution.py:391
  4.0 14.9 %collective-permute-start.3 = (bf16[48,1536]{1,0:T(8,128)(2,1)}, bf16[48,1536]{1,0:T(8,128)(2,1)S(1)}, u32[]{:S(2)}, u32[]{:S(2)}) collective-permute-start(bf16[48,1536]{1,0:T(8,128)(2,1)} %bitcast.9), channel_id=1, source_target_pairs={{0,2},{1,3},{2,0},{3,1},{4,6},{5,7},{6,4},{7,5},{8,10},{9,11},{10,... | collective-permute-start | bytes 442376 | tf_op jit(solution)/shard_map/ppermute | solution.py:388
  5.3 13.6 %collective-permute-start.4 = (bf16[48,1536]{1,0:T(8,128)(2,1)}, bf16[48,1536]{1,0:T(8,128)(2,1)S(1)}, u32[]{:S(2)}, u32[]{:S(2)}) collective-permute-start(bf16[48,1536]{1,0:T(8,128)(2,1)} %bitcast.10), channel_id=1, source_target_pairs={{0,4},{1,5},{2,6},{3,7},{4,0},{5,1},{6,2},{7,3},{8,12},{9,13},{10,... | collective-permute-start | bytes 442376 | tf_op jit(solution)/shard_map/ppermute | solution.py:388
  7.6 11.9 %collective-permute-start = (bf16[48,1536]{1,0:T(8,128)(2,1)}, bf16[48,1536]{1,0:T(8,128)(2,1)S(1)}, u32[]{:S(2)}, u32[]{:S(2)}) collective-permute-start(bf16[48,1536]{1,0:T(8,128)(2,1)} %bitcast.11), channel_id=1, source_target_pairs={{0,6},{1,7},{2,4},{3,5},{4,2},{5,3},{6,0},{7,1},{8,14},{9,15},{10,... | collective-permute-start | bytes 442376 | tf_op jit(solution)/shard_map/ppermute | solution.py:388
  17.1 2.9 %collective-permute-start.2 = (bf16[768,384]{1,0:T(8,128)(2,1)S(1)}, bf16[768,384]{1,0:T(8,128)(2,1)S(1)}, u32[]{:S(2)}, u32[]{:S(2)}) collective-permute-start(bf16[768,384]{1,0:T(8,128)(2,1)S(1)} %collective-permute-done.1.w_first), channel_id=1, source_target_pairs={{0,8},{8,0},{16,24},{24,16},{1,9},{9,1},{17,25},{25,17},{2,10},{10... | collective-permute-start | bytes 1769480 | tf_op jit(solution)/shard_map/ppermute | solution.py:394
  20.0 9.7 %copy-start.8 = (f32[2,1024]{1,0:T(2,128)S(1)}, f32[2,1024]{1,0:T(2,128)}, u32[]{:S(2)}) copy-start(f32[2,1024]{1,0:T(2,128)} %gains.1) | copy-start | bytes 24580
  21.3 8.3 %collective-permute-start.5 = (bf16[208,256]{1,0:T(8,128)(2,1)S(1)}, bf16[208,256]{1,0:T(8,128)(2,1)S(1)}, u32[]{:S(2)}, u32[]{:S(2)}) collective-permute-start(bf16[208,256]{1,0:T(8,128)(2,1)S(1)} %get-tuple-element.31), channel_id=1, source_target_pairs={{0,4},{1,5},{2,6},{3,7},{4,0},{5,1},{6,2},{7,3},{8,12},{9,13},{10,... | collective-permute-start | bytes 319496 | tf_op jit(solution)/shard_map/ppermute | solution.py:388
  23.9 5.8 %collective-permute-start.7 = (bf16[208,256]{1,0:T(8,128)(2,1)S(1)}, bf16[208,256]{1,0:T(8,128)(2,1)S(1)}, u32[]{:S(2)}, u32[]{:S(2)}) collective-permute-start(bf16[208,256]{1,0:T(8,128)(2,1)S(1)} %get-tuple-element.33), channel_id=1, source_target_pairs={{0,2},{1,3},{2,0},{3,1},{4,6},{5,7},{6,4},{7,5},{8,10},{9,11},{10,... | collective-permute-start | bytes 319496 | tf_op jit(solution)/shard_map/ppermute | solution.py:388
  25.2 4.5 %collective-permute-start.6 = (bf16[16,256]{1,0:T(8,128)(2,1)S(1)}, bf16[16,256]{1,0:T(8,128)(2,1)S(1)}, u32[]{:S(2)}, u32[]{:S(2)}) collective-permute-start(bf16[16,256]{1,0:T(8,128)(2,1)S(1)} %get-tuple-element.32.own_sums), channel_id=1, source_target_pairs={{0,6},{1,7},{2,4},{3,5},{4,2},{5,3},{6,0},{7,1},{8,14},{9,15},{10,... | collective-permute-start | bytes 24584 | tf_op jit(solution)/shard_map/ppermute | solution.py:388
  29.9 8.3 %collective-permute-start.8 = (bf16[192,512]{1,0:T(8,128)(2,1)S(1)}, bf16[192,512]{1,0:T(8,128)(2,1)S(1)}, u32[]{:S(2)}, u32[]{:S(2)}) collective-permute-start(bf16[192,512]{1,0:T(8,128)(2,1)S(1)} %get-tuple-element.36.a0), channel_id=1, source_target_pairs={{0,1},{1,0},{2,3},{3,2},{4,5},{5,4},{6,7},{7,6},{8,9},{9,8},{10,11... | collective-permute-start | bytes 589832 | tf_op jit(solution)/shard_map/ppermute | solution.py:391
  31.5 7.3 %collective-permute-start.10 = (bf16[192,512]{1,0:T(8,128)(2,1)S(1)}, bf16[192,512]{1,0:T(8,128)(2,1)S(1)}, u32[]{:S(2)}, u32[]{:S(2)}) collective-permute-start(bf16[192,512]{1,0:T(8,128)(2,1)S(1)} %get-tuple-element.36.a0), channel_id=1, source_target_pairs={{0,17},{1,16},{2,19},{3,18},{4,21},{5,20},{6,23},{7,22},{8,25},{9,... | collective-permute-start | bytes 589832 | tf_op jit(solution)/shard_map/ppermute | solution.py:399
  34.3 6.3 %collective-permute-start.9 = (bf16[192,512]{1,0:T(8,128)(2,1)S(1)}, bf16[192,512]{1,0:T(8,128)(2,1)S(1)}, u32[]{:S(2)}, u32[]{:S(2)}) collective-permute-start(bf16[192,512]{1,0:T(8,128)(2,1)S(1)} %get-tuple-element.36.a0), channel_id=1, source_target_pairs={{0,16},{1,17},{2,18},{3,19},{4,20},{5,21},{6,22},{7,23},{8,24},{9,... | collective-permute-start | bytes 589832 | tf_op jit(solution)/shard_map/ppermute | solution.py:399
  35.9 9.0 %collective-permute-start.13 = (bf16[192,512]{1,0:T(8,128)(2,1)S(1)}, bf16[192,512]{1,0:T(8,128)(2,1)S(1)}, u32[]{:S(2)}, u32[]{:S(2)}) collective-permute-start(bf16[192,512]{1,0:T(8,128)(2,1)S(1)} %get-tuple-element.36.a0), channel_id=1, source_target_pairs={{0,8},{8,0},{16,24},{24,16},{1,9},{9,1},{17,25},{25,17},{2,10},{10... | collective-permute-start | bytes 589832 | tf_op jit(solution)/shard_map/ppermute | solution.py:394
  40.6 4.2 %collective-permute-start.14 = (bf16[192,512]{1,0:T(8,128)(2,1)S(1)}, bf16[192,512]{1,0:T(8,128)(2,1)S(1)}, u32[]{:S(2)}, u32[]{:S(2)}) collective-permute-start(bf16[192,512]{1,0:T(8,128)(2,1)S(1)} %collective-permute-done.8.a1), channel_id=1, source_target_pairs={{0,8},{8,0},{16,24},{24,16},{1,9},{9,1},{17,25},{25,17},{2,10},{10... | collective-permute-start | bytes 589832 | tf_op jit(solution)/shard_map/ppermute | solution.py:394
  43.7 1.9 %collective-permute-start.11 = (bf16[192,512]{1,0:T(8,128)(2,1)S(1)}, bf16[192,512]{1,0:T(8,128)(2,1)S(1)}, u32[]{:S(2)}, u32[]{:S(2)}) collective-permute-start(bf16[192,512]{1,0:T(8,128)(2,1)S(1)} %collective-permute-done.9.one), channel_id=1, source_target_pairs={{0,8},{8,0},{16,24},{24,16},{1,9},{9,1},{17,25},{25,17},{2,10},{10... | collective-permute-start | bytes 589832 | tf_op jit(solution)/shard_map/ppermute | solution.py:394
  43.7 1.9 %collective-permute-start.12 = (bf16[192,512]{1,0:T(8,128)(2,1)S(1)}, bf16[192,512]{1,0:T(8,128)(2,1)S(1)}, u32[]{:S(2)}, u32[]{:S(2)}) collective-permute-start(bf16[192,512]{1,0:T(8,128)(2,1)S(1)} %collective-permute-done.10.two), channel_id=1, source_target_pairs={{0,8},{8,0},{16,24},{24,16},{1,9},{9,1},{17,25},{25,17},{2,10},{10... | collective-permute-start | bytes 589832 | tf_op jit(solution)/shard_map/ppermute | solution.py:394
  44.9 4.6 %copy-start = (bf16[1024,1536]{1,0:T(8,128)(2,1)S(1)}, bf16[1024,1536]{1,0:T(8,128)(2,1)}, u32[]{:S(2)}) copy-start(bf16[1024,1536]{1,0:T(8,128)(2,1)} %w_out.3) | copy-start | bytes 9437188
  45.5 3.9 %copy-start.7 = (f32[1,2,1536]{2,1,0:T(2,128)S(1)}, f32[1,2,1536]{2,1,0:T(2,128)}, u32[]{:S(2)}) copy-start(f32[1,2,1536]{2,1,0:T(2,128)} %param.17) | copy-start | bytes 36868
  45.7 4.6 %collective-permute-start.15 = (bf16[48,256]{1,0:T(8,128)(2,1)S(1)}, bf16[48,256]{1,0:T(8,128)(2,1)S(1)}, u32[]{:S(2)}, u32[]{:S(2)}) collective-permute-start(bf16[48,256]{1,0:T(8,128)(2,1)S(1)} %get-tuple-element.48), channel_id=1, source_target_pairs={{0,6},{1,7},{2,4},{3,5},{4,2},{5,3},{6,0},{7,1},{8,14},{9,15},{10,... | collective-permute-start | bytes 73736 | tf_op jit(solution)/shard_map/ppermute | solution.py:388
  49.1 3.8 %collective-permute-start.16 = (bf16[48,256]{1,0:T(8,128)(2,1)S(1)}, bf16[48,256]{1,0:T(8,128)(2,1)S(1)}, u32[]{:S(2)}, u32[]{:S(2)}) collective-permute-start(bf16[48,256]{1,0:T(8,128)(2,1)S(1)} %get-tuple-element.49), channel_id=1, source_target_pairs={{0,4},{1,5},{2,6},{3,7},{4,0},{5,1},{6,2},{7,3},{8,12},{9,13},{10,... | collective-permute-start | bytes 73736 | tf_op jit(solution)/shard_map/ppermute | solution.py:388
  49.1 3.8 %collective-permute-start.17 = (bf16[48,256]{1,0:T(8,128)(2,1)S(1)}, bf16[48,256]{1,0:T(8,128)(2,1)S(1)}, u32[]{:S(2)}, u32[]{:S(2)}) collective-permute-start(bf16[48,256]{1,0:T(8,128)(2,1)S(1)} %get-tuple-element.50), channel_id=1, source_target_pairs={{0,2},{1,3},{2,0},{3,1},{4,6},{5,7},{6,4},{7,5},{8,10},{9,11},{10,... | collective-permute-start | bytes 73736 | tf_op jit(solution)/shard_map/ppermute | solution.py:388
  49.4 3.5 %copy-start.4 = (bf16[1536,64]{0,1:T(8,128)(2,1)S(1)}, bf16[1536,64]{0,1:T(8,128)(2,1)}, u32[]{:S(2)}) copy-start(bf16[1536,64]{0,1:T(8,128)(2,1)} %param.18) | copy-start | bytes 589828
  49.4 3.5 %copy-start.6 = (f32[1,48,64]{2,1,0:T(8,128)S(1)}, f32[1,48,64]{2,1,0:T(8,128)}, u32[]{:S(2)}) copy-start(f32[1,48,64]{2,1,0:T(8,128)} %param.11) | copy-start | bytes 36868
  54.6 5.6 %collective-permute-start.18 = (f32[1,48,64]{2,1,0:T(8,128)S(1)}, f32[1,48,64]{2,1,0:T(8,128)S(1)}, u32[]{:S(2)}, u32[]{:S(2)}) collective-permute-start(f32[1,48,64]{2,1,0:T(8,128)S(1)} %bitcast.20), channel_id=1, source_target_pairs={{0,24},{8,0},{16,8},{24,16},{1,25},{9,1},{17,9},{25,17},{2,26},{10... | collective-permute-start | bytes 36872 | tf_op jit(solution)/shard_map/ppermute | solution.py:28

commit v3 on v2

--- a/solution.py
+++ b/solution.py
@@ -174,42 +174,32 @@
     return (layer_norm(rows[...].astype(F32)) * scale + shift).astype(BF16)
 
 
-def own_kernel(x1, x2, time_mod, block_mod, w_own, modded, own):
-    for step, rows in enumerate((x1, x2)):
-        modded[step * TOK_DEV : (step + 1) * TOK_DEV, :] = modulated(rows, time_mod, block_mod)
+def first_kernel(
+    x2, x1, x3, x0, time_mod, block_mod, w_own, w_first, modded, own, other
+):
+    for place, rows in enumerate((x2, x1, x3, x0)):
+        modded[place * TOK_DEV : (place + 1) * TOK_DEV, :] = modulated(rows, time_mod, block_mod)
+    half = D // 2
+    at = pl.multiple_of(here()[2] * half, half)
     own[...] = jnp.dot(modded[...], w_own[...], preferred_element_type=F32).astype(BF16)
+    other[...] = jnp.dot(modded[:, pl.ds(at, half)], w_first[...], preferred_element_type=F32)
 
 
 def project_kernel(
-    x3, x0, time_mod, block_mod, w_own, w_first, w_second, modded_in, own_in,
-    far_out, near_out, keep_out, sums_out, modded, mixed,
+    w_second, modded, own_in, other_in, far_out, near_out, keep_out, sums_out, mixed
 ):
     line, side, core, _ = here()
     half = D // 2
-    width = w_own.shape[1]
-    modded[:TOK_DEV, :] = modulated(x0, time_mod, block_mod)
-    modded[TOK_DEV : 2 * TOK_DEV, :] = modulated(x3, time_mod, block_mod)
-    modded[2 * TOK_DEV :, :] = modded_in[...]
-    late = jnp.dot(modded[: 2 * TOK_DEV, :], w_own[...], preferred_element_type=F32).astype(BF16)
-    other = jnp.dot(
-        modded[:, pl.ds(pl.multiple_of(core * half, half), half)], w_first[...],
-        preferred_element_type=F32,
-    )
-    other += jnp.dot(
-        modded[:, pl.ds(pl.multiple_of((1 - core) * half, half), half)], w_second[...],
-        preferred_element_type=F32,
-    )
-    other = other.astype(BF16)
+    width = w_second.shape[1]
+    at = pl.multiple_of((1 - core) * half, half)
+    other = jnp.dot(modded[:, pl.ds(at, half)], w_second[...], preferred_element_type=F32)
+    other = (other + other_in[...]).astype(BF16)
     mine = pl.multiple_of(side * width, width)
     there = pl.multiple_of((1 - side) * width, width)
-    for place, step in enumerate((0, 3, 1, 2)):
+    for place, step in enumerate((2, 1, 3, 0)):
         at = pl.multiple_of(jnp.bitwise_xor(line, step) * TOK_DEV, 16)
         rows = slice(place * TOK_DEV, (place + 1) * TOK_DEV)
-        if place < 2:
-            mixed[pl.ds(at, TOK_DEV), pl.ds(mine, width)] = late[rows]
-        else:
-            behind = slice((place - 2) * TOK_DEV, (place - 1) * TOK_DEV)
-            mixed[pl.ds(at, TOK_DEV), pl.ds(mine, width)] = own_in[behind, :]
+        mixed[pl.ds(at, TOK_DEV), pl.ds(mine, width)] = own_in[rows, :]
         mixed[pl.ds(at, TOK_DEV), pl.ds(there, width)] = other[rows]
     ones = jnp.ones((16, PAIR), BF16)
     row_id = lax.broadcasted_iota(jnp.int32, (16, ROWS), 0)
@@ -240,8 +230,18 @@
     keep_out[...] = mixed[:, pl.ds(at, PAIR)]
 
 
+def step_size(levels):
+    level = jnp.broadcast_to(levels[...], (1, HEAD_DIM))
+
+    def sigma(level):
+        fraction = level.astype(F32) / LEVELS
+        return 5.0 * fraction / (1.0 + 4.0 * fraction)
+
+    return sigma(level - 1) - sigma(level)
+
+
 def rope_kernel(
-    far, last_sums, near, keep, own_sums, gains, cosines, sines, q_out, kv_out, units
+    far, last_sums, near, keep, own_sums, gains, cosines, sines, levels, q_out, kv_out, size, units
 ):
     line, _, _, _ = here()
     upper, odd = line // 2, line % 2
@@ -274,53 +274,50 @@
             turned = scaled * cos + pltpu.roll(scaled, HEAD_DIM // 2, axis=1) * sin
             (kv_out if kind else q_out)[:, columns] = turned.astype(BF16)
     kv_out[:, PAIR:] = units[slots[2]]
-
-
-def attend_group(queries, one, two, state):
-    total, highest = state
+    size[...] = step_size(levels)
+
+
+def attend_group(queries, one, two, head, counts=None):
+    columns = slice(head * HEAD_DIM, (head + 1) * HEAD_DIM)
+    value_columns = slice(PAIR + head * HEAD_DIM, PAIR + (head + 1) * HEAD_DIM)
+    keys = jnp.concatenate([one[:, columns], two[:, columns]], axis=0)
+    values = jnp.concatenate([one[:, value_columns], two[:, value_columns]], axis=0)
     ones = jnp.ones((2 * ROWS, HEAD_DIM), BF16)
+    scores = dot_rows(queries[:, columns], keys) * HEAD_DIM ** (-0.5)
+    maxima = jnp.max(scores, axis=-1, keepdims=True)
+    weights = jnp.exp(scores - maxima).astype(BF16)
+    output = jnp.dot(weights, jnp.concatenate([values, ones], axis=1), preferred_element_type=F32)
+    if counts is not None:
+        maxima = jnp.where(counts, maxima, -1e30)
+    return output, maxima
+
+
+def merged(parts):
+    highest = functools.reduce(jnp.maximum, [maxima for _, maxima in parts])
+    total = sum(output * jnp.exp(maxima - highest) for output, maxima in parts)
+    return total, highest
+
+
+def first_attend_kernel(queries, c0, c1, a0, a1, total_out, highest_out):
+    chip = here()[3]
     for head in range(2):
+        own = attend_group(queries, a0, a1, head)
+        far = attend_group(queries, c0, c1, head, chip == 1)
+        total, highest = merged([own, far])
+        total_out[head] = total
+        highest_out[head] = jnp.broadcast_to(highest, (ROWS, HEAD_DIM))
+
+
+def last_attend_kernel(
+    queries, b0, b1, d0, d1, total_in, highest_in, o3, o2, o1, o0, result
+):
+    line, _, core, chip = here()
+    for head in range(2):
+        near = attend_group(queries, b0, b1, head, core == 1)
+        far = attend_group(queries, d0, d1, head, chip == 1)
+        total, _ = merged([(total_in[head], highest_in[head, :, :1]), near, far])
         columns = slice(head * HEAD_DIM, (head + 1) * HEAD_DIM)
-        value_columns = slice(PAIR + head * HEAD_DIM, PAIR + (head + 1) * HEAD_DIM)
-        keys = jnp.concatenate([one[:, columns], two[:, columns]], axis=0)
-        values = jnp.concatenate([one[:, value_columns], two[:, value_columns]], axis=0)
-        scores = dot_rows(queries[:, columns], keys) * HEAD_DIM ** (-0.5)
-        maxima = jnp.max(scores, axis=-1, keepdims=True)
-        weights = jnp.exp(scores - maxima).astype(BF16)
-        output = jnp.dot(
-            weights, jnp.concatenate([values, ones], axis=1), preferred_element_type=F32
-        )
-        old = highest[head]
-        new = jnp.maximum(old, maxima)
-        keep_old, keep_new = jnp.exp(old - new), jnp.exp(maxima - new)
-        highest[head] = new
-        for part in range(2):
-            lanes = slice(part * HEAD_DIM, (part + 1) * HEAD_DIM)
-            total[head, :, lanes] = total[head, :, lanes] * keep_old + output[:, lanes] * keep_new
-
-
-def own_attend_kernel(queries, a0, a1, total, highest):
-    total[...] = jnp.zeros_like(total)
-    highest[...] = jnp.full_like(highest, -1e30)
-    attend_group(queries, a0, a1, (total, highest))
-
-
-def next_attend_kernel(which, queries, one, two, total_in, highest_in, total, highest):
-    total[...] = total_in[...]
-    highest[...] = highest_in[...]
-    pl.when(here()[which] == 1)(lambda: attend_group(queries, one, two, (total, highest)))
-
-
-def last_attend_kernel(
-    queries, d0, d1, total_in, highest_in, o3, o2, o1, o0, total, highest, result
-):
-    line, _, _, chip = here()
-    total[...] = total_in[...]
-    highest[...] = highest_in[...]
-    pl.when(chip == 1)(lambda: attend_group(queries, d0, d1, (total, highest)))
-    for head in range(2):
-        columns = slice(head * HEAD_DIM, (head + 1) * HEAD_DIM)
-        result[:, columns] = (total[head, :, :HEAD_DIM] / total[head, :, HEAD_DIM:]).astype(BF16)
+        result[:, columns] = (total[:, :HEAD_DIM] / total[:, HEAD_DIM:]).astype(BF16)
     for step, out in enumerate((o0, o1, o2, o3)):
         at = pl.multiple_of(jnp.bitwise_xor(line, step) * TOK_DEV, 16)
         out[...] = result[pl.ds(at, TOK_DEV), :]
@@ -359,23 +356,18 @@
 
 
 def finish_kernel(
-    r3, r2, r1, w_out, base, vectors, w_head, levels, latents_in, stream_out, latents_out,
+    r3, r2, r1, w_out, base, vectors, w_head, size, latents_in, stream_out, latents_out,
     latents, arrived,
 ):
     copies = load((latents_in,), (latents,), arrived)
     projected = times_w_out(r3, w_out, 3) + times_w_out(r2, w_out, 2) + times_w_out(r1, w_out, 1)
     updated = base[...] + vectors[0:1] * projected
-    stream_out[...] = updated.astype(BF16)
+    stream_out[...] = updated
     head_in = (layer_norm(updated) * vectors[1:2] + vectors[2:3]).astype(BF16)
     velocity = dot_rows(head_in, w_head[...])
 
-    def sigma(level):
-        fraction = level.astype(F32) / LEVELS
-        return 5.0 * fraction / (1.0 + 4.0 * fraction)
-
-    level = levels[...]
     copies[0].wait()
-    latents_out[...] = latents[...] + (sigma(level - 1) - sigma(level)) * velocity
+    latents_out[...] = latents[...] + size[0:1, :CHAN] * velocity
 
 
 def lines(
@@ -393,9 +385,16 @@
     def cores(value):
         return lax.ppermute(value, "slab", [(i, i ^ 1) for i in range(4)])
 
-    def chips(value, flip):
+    def chips(value):
+        return lax.ppermute(value, "slab", [(i, i ^ 2) for i in range(4)])
+
+    def chips_and_sides(value):
         count = 2 * LINE
-        pairs = [(s * count + i, (s + 2) * count + (i ^ flip)) for s in range(2) for i in range(count)]
+        pairs = [
+            (s * count + i, (s ^ 2) * count + (i ^ 1 if s < 2 else i))
+            for s in range(4)
+            for i in range(count)
+        ]
         return lax.ppermute(value, ("slab", "seq"), pairs)
 
     rows = stream[0]
@@ -411,43 +410,38 @@
     cosines = jnp.concatenate([cosines, cosines], axis=1)
     sines = jnp.concatenate([-sines, sines], axis=1)
 
+    w_second = cores(w_first)
     width = w_qkv.shape[1]
-    modded, own = vmem_call(
-        own_kernel, [((2 * TOK_DEV, D), BF16), ((2 * TOK_DEV, width), BF16)], "own", 1 << 28
-    )(x1, x2, time_rows, block_mod, w_qkv)
-    w_second = cores(w_first)
+    modded, own, other = vmem_call(
+        first_kernel, [((ROWS, D), BF16), ((ROWS, width), BF16), ((ROWS, width), F32)],
+        "first", 1 << 28,
+    )(x2, x1, x3, rows, time_rows, block_mod, w_qkv, w_first)
     message = (ROWS + 16, PAIR)
     far, near, keep, sums = vmem_call(
         project_kernel,
         [(message, BF16), (message, BF16), ((ROWS, PAIR), BF16), ((16, PAIR), BF16)],
-        "project", 1 << 28,
-        [pltpu.VMEM((ROWS, D), BF16), pltpu.VMEM((ROWS, 3 * PAIR), BF16)],
-    )(x3, rows, time_rows, block_mod, w_qkv, w_first, w_second, modded, own)
+        "project", 1 << 28, [pltpu.VMEM((ROWS, 3 * PAIR), BF16)],
+    )(w_second, modded, own, other)
     far, last_sums, near = along(2, far), along(3, sums), along(1, near)
-    queries, pairs = vmem_call(
+    queries, pairs, size = vmem_call(
         rope_kernel,
-        [((ROWS, PAIR), BF16), ((ROWS, 2 * PAIR), BF16)],
+        [((ROWS, PAIR), BF16), ((ROWS, 2 * PAIR), BF16), ((1, HEAD_DIM), F32)],
         "rope", 1 << 22, [pltpu.VMEM((3, ROWS, PAIR), BF16)],
-    )(far, last_sums, near, keep, sums, qk_gain, cosines, sines)
-    chip_pairs, both_pairs = chips(pairs, 0), chips(pairs, 1)
-    side_pairs, core_pairs = across(pairs), cores(pairs)
+    )(far, last_sums, near, keep, sums, qk_gain, cosines, sines, noise_level[None])
+    chip_pairs, side_pairs = chips(pairs), across(pairs)
+    both_pairs = chips_and_sides(pairs)
+    chip_pairs, side_pairs = lax.optimization_barrier((chip_pairs, side_pairs))
     state = [((2, ROWS, PAIR), F32), ((2, ROWS, HEAD_DIM), F32)]
-    held = [pltpu.VMEM(shape, dtype) for shape, dtype in state]
-    now = vmem_call(own_attend_kernel, state, "attend_own", 1 << 27)(queries, pairs, side_pairs)
-    now, chip_pairs, both_pairs, side_pairs = lax.optimization_barrier(
-        (now, chip_pairs, both_pairs, side_pairs)
-    )
+    now = vmem_call(first_attend_kernel, state, "attend_first", 1 << 27)(
+        queries, chip_pairs, both_pairs, pairs, side_pairs
+    )
+    _, late_pairs = lax.optimization_barrier((side_pairs, pairs))
+    core_pairs = cores(late_pairs)
     core_side, core_chip, core_both = cores(side_pairs), cores(chip_pairs), cores(both_pairs)
-    for name, which, blocks in (
-        ("attend_core", 2, (core_pairs, core_side)),
-        ("attend_chip", 3, (chip_pairs, both_pairs)),
-    ):
-        kernel = functools.partial(next_attend_kernel, which)
-        now = vmem_call(kernel, state, name, 1 << 27)(queries, *blocks, *now)
     part3, part2, part1, part0 = vmem_call(
         last_attend_kernel, [((TOK_DEV, PAIR), BF16)] * 4, "attend_last", 1 << 27,
-        held + [pltpu.VMEM((ROWS, PAIR), BF16)],
-    )(queries, core_chip, core_both, *now)
+        [pltpu.VMEM((ROWS, PAIR), BF16)],
+    )(queries, core_pairs, core_side, core_chip, core_both, *now)
     late = [along(3, part3), along(2, part2), along(1, part1)]
     loaded = (rows, time_rows, block_mod, head_mod[0])
     base, vectors = vmem_call(
@@ -455,12 +449,11 @@
         [pltpu.VMEM(v.shape, v.dtype) for v in loaded] + [pltpu.SemaphoreType.DMA((len(loaded),))],
         placed=len(loaded),
     )(part0, w_out, *loaded)
-    level = jnp.broadcast_to(noise_level[:, None], (1, CHAN))
-    new_stream, stepped = vmem_call(
-        finish_kernel, [((TOK_DEV, D), BF16), ((TOK_DEV, CHAN), F32)], "finish", 1 << 28,
+    updated, stepped = vmem_call(
+        finish_kernel, [((TOK_DEV, D), F32), ((TOK_DEV, CHAN), F32)], "finish", 1 << 28,
         [pltpu.VMEM((TOK_DEV, CHAN), F32), pltpu.SemaphoreType.DMA((1,))], placed=1,
-    )(*late, w_out, base, vectors, w_head.T, level, latents[0])
-    return (new_stream[None], from_behind(stepped[None], "slab", -1))
+    )(*late, w_out, base, vectors, w_head.T, size, latents[0])
+    return (updated.astype(BF16)[None], from_behind(stepped[None], "slab", -1))
 
 
 def solution(mesh):

time: 61 us -> 57.2 us (0.938)
  starting transfers between devices: 27.7 us -> 25.2 us
  waiting for transfers between devices: 23.2 us -> 21.4 us
  other arithmetic: 0.63 us -> 1.31 us
    ppermute x2, starting transfers between devices: 4.38 us -> 2.71 us  [the longest x1 1.52 us: chips_and_sides(): return lax.ppermute(value, ('slab', 'seq'), pairs)]
    ppermute x1, waiting for transfers between devices: 4.34 us -> 2.73 us  [from_behind(): return lax.ppermute(value, axis, pairs)]
    ppermute x2, starting transfers between devices: 3.68 us -> 2.14 us  [across(): return lax.ppermute(value, 'seq', [(i, i ^ 1) for i in range(2 * LINE)])]
    ppermute x9, waiting for transfers between devices: 7.22 us -> 5.85 us  [along(): lax.ppermute(value, 'seq', [(i, i ^ 2 * step) for i in range(2 * LINE)])]
    ppermute x9, starting transfers between devices: 11.2 us -> 12.3 us  [along(): lax.ppermute(value, 'seq', [(i, i ^ 2 * step) for i in range(2 * LINE)])]
    ppermute x2, waiting for transfers between devices: 9.44 us -> 10.2 us  [across(): return lax.ppermute(value, 'seq', [(i, i ^ 1) for i in range(2 * LINE)])]
    ppermute x2, waiting for transfers between devices: 1.78 us -> 2.52 us  [the longest x1 2.52 us: chips(): return lax.ppermute(value, 'slab', [(i, i ^ 2) for i in range(4)])]
    broadcast_in_dim x0 -> x1, other arithmetic: none -> 0.68 us  [lines(): return (updated.astype(BF16)[None], from_behind(stepped[None], 'slab', -1))]
  transfers between devices with their start and end apart: 19 -> 19, of which waited for: 7 -> 10; matrix products, arithmetic and copies ran while one was open for 1% -> 2% of each run, Pallas kernels for 4% -> 4%
where the time goes in v3:
time: 57.2 us; the launch traced here: 57.1 us
  starting transfers between devices  25.2 us (44%)
  waiting for transfers between devices  21.4 us (37%)
  Pallas kernels  5.55 us (10%)
  local copies, waits for them, and re-layouts  1.95 us (3%)
  between operations  1.67 us (3%)
  other arithmetic  1.31 us (2%)
    ppermute x9, starting transfers between devices, along(): lax.ppermute(value, 'seq', [(i, i ^ 2 * step) for i in range(2 * LINE)])  12.3 us
    ppermute x2, waiting for transfers between devices, across(): return lax.ppermute(value, 'seq', [(i, i ^ 1) for i in range(2 * LINE)])  10.2 us
    ppermute x5, starting transfers between devices, cores(): return lax.ppermute(value, 'slab', [(i, i ^ 1) for i in range(4)])  6.81 us
    ppermute x9, waiting for transfers between devices, along(): lax.ppermute(value, 'seq', [(i, i ^ 2 * step) for i in range(2 * LINE)])  5.85 us
    pallas_call x7, Pallas kernels, call(): pl.pallas_call(kernel, out_shape=[jax.ShapeDtypeStruct(shape, dtype) for...  5.55 us
    ppermute x1, waiting for transfers between devices, from_behind(): return lax.ppermute(value, axis, pairs)  2.73 us
    ppermute x1, waiting for transfers between devices, chips(): return lax.ppermute(value, 'slab', [(i, i ^ 2) for i in range(4)])  2.52 us
    ppermute x2, starting transfers between devices, across(): return lax.ppermute(value, 'seq', [(i, i ^ 1) for i in range(2 * LINE)])  2.14 us
  transfers between devices with their start and end apart: 19, of which 10 were waited for; matrix products, arithmetic and copies ran while one was open for 2% of the time, Pallas kernels for 4%

profile of v3, /device:TPU:1, one launch (start us, length us, event | category | flops | bytes accessed | tf_op | source)
XLA Modules:
  0.0 57.1 jit_solution(9784234936427289134)
XLA Ops:
  0.7 1.2 %constant_dynamic-slice_fusion = bf16[768,384]{1,0:T(8,128)(2,1)S(1)} fusion(bf16[1536,384]{1,0:T(8,128)(2,1)} %w_own.1, s32[]{:T(128)S(6)} %select_n.15), kind=kLoop, calls=%fused_computation.9 | loop fusion | bytes 1179652 | tf_op jit(solution)/shard_map/dynamic_slice | solution.py:402
  1.9 2.1 %collective-permute-start = (bf16[768,384]{1,0:T(8,128)(2,1)S(1)}, bf16[768,384]{1,0:T(8,128)(2,1)S(1)}, u32[]{:S(2)}, u32[]{:S(2)}) collective-permute-start(bf16[768,384]{1,0:T(8,128)(2,1)S(1)} %constant_dynamic-slice_fusion), channel_id=1, source_target_pairs={{0,1},{1,0},{2,3},{3,2},{4,5},{5,4},{6,7},{7,6},{8,9},{9,8},{10,11... | collective-permute-start | bytes 1769480 | tf_op jit(solution)/shard_map/ppermute | solution.py:383
  4.0 2.3 %collective-permute-start.2 = (bf16[48,1536]{1,0:T(8,128)(2,1)}, bf16[48,1536]{1,0:T(8,128)(2,1)S(1)}, u32[]{:S(2)}, u32[]{:S(2)}) collective-permute-start(bf16[48,1536]{1,0:T(8,128)(2,1)} %bitcast.10), channel_id=1, source_target_pairs={{0,4},{1,5},{2,6},{3,7},{4,0},{5,1},{6,2},{7,3},{8,12},{9,13},{10,... | collective-permute-start | bytes 442376 | tf_op jit(solution)/shard_map/ppermute | solution.py:380
  6.4 1.3 %collective-permute-start.3 = (bf16[48,1536]{1,0:T(8,128)(2,1)}, bf16[48,1536]{1,0:T(8,128)(2,1)S(1)}, u32[]{:S(2)}, u32[]{:S(2)}) collective-permute-start(bf16[48,1536]{1,0:T(8,128)(2,1)} %bitcast.11), channel_id=1, source_target_pairs={{0,2},{1,3},{2,0},{3,1},{4,6},{5,7},{6,4},{7,5},{8,10},{9,11},{10,... | collective-permute-start | bytes 442376 | tf_op jit(solution)/shard_map/ppermute | solution.py:380
  7.7 9.4 %collective-permute-done.w_first = bf16[768,384]{1,0:T(8,128)(2,1)S(1)} collective-permute-done((bf16[768,384]{1,0:T(8,128)(2,1)S(1)}, bf16[768,384]{1,0:T(8,128)(2,1)S(1)}, u32[]{:S(2)}, u32[]{:S(2)}) %collective-permute-start) | collective-permute-done | bytes 589856 | tf_op jit(solution)/shard_map/ppermute | solution.py:383
  17.1 1.2 %collective-permute-start.1 = (bf16[768,384]{1,0:T(8,128)(2,1)S(1)}, bf16[768,384]{1,0:T(8,128)(2,1)S(1)}, u32[]{:S(2)}, u32[]{:S(2)}) collective-permute-start(bf16[768,384]{1,0:T(8,128)(2,1)S(1)} %collective-permute-done.w_first), channel_id=1, source_target_pairs={{0,8},{8,0},{16,24},{24,16},{1,9},{9,1},{17,25},{25,17},{2,10},{10... | collective-permute-start | bytes 1769480 | tf_op jit(solution)/shard_map/ppermute | solution.py:386
  18.5 0.4 fusion
  19.0 0.9 %first.1 = (bf16[192,1536]{1,0:T(8,128)(2,1)S(1)}, bf16[192,384]{1,0:T(8,128)(2,1)S(1)}, f32[192,384]{1,0:T(8,128)S(1)}) custom-call(bf16[48,1536]{1,0:T(8,128)(2,1)S(1)} %collective-permute-done.2.x2, bf16[48,1536]{1,0:T(8,128)(2,1)S(1)} %collective-permute-done.3.x1, bf16[48,1536]{1,0:T(8,128)(2,1)S(1)} %collective-permute-done.4.x3, ...), custom_call_target="tpu_custom_call" | custom-call | flops 268435456 | bytes 1048576 | tf_op jit(solution)/shard_map/first/pallas_call | solution.py:148
  20.0 0.7 %project.1 = (bf16[208,256]{1,0:T(8,128)(2,1)S(1)}, bf16[208,256]{1,0:T(8,128)(2,1)S(1)}, bf16[192,256]{1,0:T(8,128)(2,1)S(1)}, bf16[16,256]{1,0:T(8,128)(2,1)S(1)}) custom-call(bf16[768,384]{1,0:T(8,128)(2,1)S(1)} %collective-permute-done.1.w_second, bf16[192,1536]{1,0:T(8,128)(2,1)S(1)} %get-tuple-element.25.modded, ...), custom_call_target="tpu_custom_call" | custom-call | flops 268435456 | bytes 1048576 | tf_op jit(solution)/shard_map/project/pallas_call | solution.py:148
  20.7 3.8 %collective-permute-start.5 = (bf16[208,256]{1,0:T(8,128)(2,1)S(1)}, bf16[208,256]{1,0:T(8,128)(2,1)S(1)}, u32[]{:S(2)}, u32[]{:S(2)}) collective-permute-start(bf16[208,256]{1,0:T(8,128)(2,1)S(1)} %get-tuple-element.28), channel_id=1, source_target_pairs={{0,4},{1,5},{2,6},{3,7},{4,0},{5,1},{6,2},{7,3},{8,12},{9,13},{10,... | collective-permute-start | bytes 319496 | tf_op jit(solution)/shard_map/ppermute | solution.py:380
  24.6 1.2 %collective-permute-start.6 = (bf16[16,256]{1,0:T(8,128)(2,1)S(1)}, bf16[16,256]{1,0:T(8,128)(2,1)S(1)}, u32[]{:S(2)}, u32[]{:S(2)}) collective-permute-start(bf16[16,256]{1,0:T(8,128)(2,1)S(1)} %get-tuple-element.29.own_sums), channel_id=1, source_target_pairs={{0,6},{1,7},{2,4},{3,5},{4,2},{5,3},{6,0},{7,1},{8,14},{9,15},{10,... | collective-permute-start | bytes 24584 | tf_op jit(solution)/shard_map/ppermute | solution.py:380
  26.7 3.0 %collective-permute-done.6.last_sums = bf16[16,256]{1,0:T(8,128)(2,1)S(1)} collective-permute-done((bf16[16,256]{1,0:T(8,128)(2,1)S(1)}, bf16[16,256]{1,0:T(8,128)(2,1)S(1)}, u32[]{:S(2)}, u32[]{:S(2)}) %collective-permute-start.6) | collective-permute-done | bytes 8224 | tf_op jit(solution)/shard_map/ppermute | solution.py:380
  29.6 0.5 collective-permute-done.5.far
  30.1 0.7 %collective-permute-done.7.near = bf16[208,256]{1,0:T(8,128)(2,1)S(1)} collective-permute-done((bf16[208,256]{1,0:T(8,128)(2,1)S(1)}, bf16[208,256]{1,0:T(8,128)(2,1)S(1)}, u32[]{:S(2)}, u32[]{:S(2)}) %collective-permute-start.7) | collective-permute-done | bytes 106528 | tf_op jit(solution)/shard_map/ppermute | solution.py:380
  31.1 1.2 %collective-permute-start.8 = (bf16[192,512]{1,0:T(8,128)(2,1)S(1)}, bf16[192,512]{1,0:T(8,128)(2,1)S(1)}, u32[]{:S(2)}, u32[]{:S(2)}) collective-permute-start(bf16[192,512]{1,0:T(8,128)(2,1)S(1)} %get-tuple-element.35.a0), channel_id=1, source_target_pairs={{0,16},{8,24},{16,0},{24,8},{1,17},{9,25},{17,1},{25,9},{2,18},{10... | collective-permute-start | bytes 589832 | tf_op jit(solution)/shard_map/ppermute | solution.py:389
  32.3 1.5 %collective-permute-start.13 = (bf16[192,512]{1,0:T(8,128)(2,1)S(1)}, bf16[192,512]{1,0:T(8,128)(2,1)S(1)}, u32[]{:S(2)}, u32[]{:S(2)}) collective-permute-start(bf16[192,512]{1,0:T(8,128)(2,1)S(1)} %get-tuple-element.35.a0), channel_id=1, source_target_pairs={{0,17},{1,16},{2,19},{3,18},{4,21},{5,20},{6,23},{7,22},{8,25},{9,... | collective-permute-start | bytes 589832 | tf_op jit(solution)/shard_map/ppermute | solution.py:398
  33.8 2.5 %collective-permute-done.8.c0 = bf16[192,512]{1,0:T(8,128)(2,1)S(1)} collective-permute-done((bf16[192,512]{1,0:T(8,128)(2,1)S(1)}, bf16[192,512]{1,0:T(8,128)(2,1)S(1)}, u32[]{:S(2)}, u32[]{:S(2)}) %collective-permute-start.8) | collective-permute-done | bytes 196640 | tf_op jit(solution)/shard_map/ppermute | solution.py:389
  36.3 0.8 %collective-permute-done.9.a1 = bf16[192,512]{1,0:T(8,128)(2,1)S(1)} collective-permute-done((bf16[192,512]{1,0:T(8,128)(2,1)S(1)}, bf16[192,512]{1,0:T(8,128)(2,1)S(1)}, u32[]{:S(2)}, u32[]{:S(2)}) %collective-permute-start.9) | collective-permute-done | bytes 196640 | tf_op jit(solution)/shard_map/ppermute | solution.py:383
  37.1 3.1 %collective-permute-start.11 = (bf16[192,512]{1,0:T(8,128)(2,1)S(1)}, bf16[192,512]{1,0:T(8,128)(2,1)S(1)}, u32[]{:S(2)}, u32[]{:S(2)}) collective-permute-start(bf16[192,512]{1,0:T(8,128)(2,1)S(1)} %collective-permute-done.9.a1), channel_id=1, source_target_pairs={{0,8},{8,0},{16,24},{24,16},{1,9},{9,1},{17,25},{25,17},{2,10},{10... | collective-permute-start | bytes 589832 | tf_op jit(solution)/shard_map/ppermute | solution.py:386
  40.2 0.5 collective-permute-start.12
  40.7 1.9 %collective-permute-start.14 = (bf16[192,512]{1,0:T(8,128)(2,1)S(1)}, bf16[192,512]{1,0:T(8,128)(2,1)S(1)}, u32[]{:S(2)}, u32[]{:S(2)}) collective-permute-start(bf16[192,512]{1,0:T(8,128)(2,1)S(1)} %collective-permute-done.13.c1), channel_id=1, source_target_pairs={{0,8},{8,0},{16,24},{24,16},{1,9},{9,1},{17,25},{25,17},{2,10},{10... | collective-permute-start | bytes 589832 | tf_op jit(solution)/shard_map/ppermute | solution.py:386
  42.7 1.0 %attend_first.1 = (f32[2,192,256]{2,1,0:T(8,128)S(1)}, f32[2,192,128]{2,1,0:T(8,128)S(1)}) custom-call(bf16[192,256]{1,0:T(8,128)(2,1)S(1)} %get-tuple-element.32.queries, bf16[192,512]{1,0:T(8,128)(2,1)S(1)} %collective-permute-done.8.c0, bf16[192,512]{1,0:T(8,128)(2,1)S(1)} %collective-permute-done.13.c1, bf16[192,512]{1,0:T(8,128)(2,1)S(1)} %get-tuple-element.35.a0, ...), custom_call_target="tpu_custom_call" | custom-call | flops 134217728 | bytes 1048576 | tf_op jit(solution)/shard_map/attend_first/pallas_call | solution.py:148
  43.7 1.0 %attend_last.1 = (bf16[48,256]{1,0:T(8,128)(2,1)S(1)}, bf16[48,256]{1,0:T(8,128)(2,1)S(1)}, bf16[48,256]{1,0:T(8,128)(2,1)S(1)}, bf16[48,256]{1,0:T(8,128)(2,1)S(1)}) custom-call(bf16[192,256]{1,0:T(8,128)(2,1)S(1)} %get-tuple-element.32.queries, bf16[192,512]{1,0:T(8,128)(2,1)S(1)} %collective-permute-done.10.b0, ...), custom_call_target="tpu_custom_call" | custom-call | flops 134217728 | bytes 1048576 | tf_op jit(solution)/shard_map/attend_last/pallas_call | solution.py:148
  44.8 1.9 %collective-permute-start.15 = (bf16[48,256]{1,0:T(8,128)(2,1)S(1)}, bf16[48,256]{1,0:T(8,128)(2,1)S(1)}, u32[]{:S(2)}, u32[]{:S(2)}) collective-permute-start(bf16[48,256]{1,0:T(8,128)(2,1)S(1)} %get-tuple-element.39), channel_id=1, source_target_pairs={{0,6},{1,7},{2,4},{3,5},{4,2},{5,3},{6,0},{7,1},{8,14},{9,15},{10,... | collective-permute-start | bytes 73736 | tf_op jit(solution)/shard_map/ppermute | solution.py:380
  46.6 1.8 %collective-permute-start.17 = (bf16[48,256]{1,0:T(8,128)(2,1)S(1)}, bf16[48,256]{1,0:T(8,128)(2,1)S(1)}, u32[]{:S(2)}, u32[]{:S(2)}) collective-permute-start(bf16[48,256]{1,0:T(8,128)(2,1)S(1)} %get-tuple-element.41), channel_id=1, source_target_pairs={{0,2},{1,3},{2,0},{3,1},{4,6},{5,7},{6,4},{7,5},{8,10},{9,11},{10,... | collective-permute-start | bytes 73736 | tf_op jit(solution)/shard_map/ppermute | solution.py:380
  48.4 0.6 %begin.1 = (f32[48,1536]{1,0:T(8,128)S(1)}, f32[8,1536]{1,0:T(8,128)S(1)}) custom-call(bf16[48,256]{1,0:T(8,128)(2,1)S(1)} %get-tuple-element.42.r0, bf16[1024,1536]{1,0:T(8,128)(2,1)S(1)} %copy-done, bf16[48,1536]{1,0:T(8,128)(2,1)S(1)} %bitcast.14, f32[3,1,1536]{2,1,0:T(1,128)S(1)} %bitcast.17, f32[3,1536]{1,0:T(4,128)S(1)} %copy-done.4, ...), custom_call_target="tpu_custom_call" | custom-call | flops 268435456 | bytes 1048576 | tf_op jit(solution)/shard_map/begin/pallas_call | solution.py:148
  49.3 1.5 %collective-permute-done.16.r2 = bf16[48,256]{1,0:T(8,128)(2,1)S(1)} collective-permute-done((bf16[48,256]{1,0:T(8,128)(2,1)S(1)}, bf16[48,256]{1,0:T(8,128)(2,1)S(1)}, u32[]{:S(2)}, u32[]{:S(2)}) %collective-permute-start.16) | collective-permute-done | bytes 24608 | tf_op jit(solution)/shard_map/ppermute | solution.py:380
  50.8 1.0 %finish.1 = (f32[48,1536]{1,0:T(8,128)S(1)}, f32[48,64]{1,0:T(8,128)S(1)}) custom-call(bf16[48,256]{1,0:T(8,128)(2,1)S(1)} %collective-permute-done.15.r3, bf16[48,256]{1,0:T(8,128)(2,1)S(1)} %collective-permute-done.16.r2, bf16[48,256]{1,0:T(8,128)(2,1)S(1)} %collective-permute-done.17.r1, bf16[1024,1536]{1,0:T(8,128)(2,1)S(1)} %copy-done, ...), custom_call_target="tpu_custom_call" | custom-call | flops 268435456 | bytes 1048576 | tf_op jit(solution)/shard_map/finish/pallas_call | solution.py:148
  51.8 1.3 %collective-permute-start.18 = (f32[1,48,64]{2,1,0:T(8,128)S(1)}, f32[1,48,64]{2,1,0:T(8,128)S(1)}, u32[]{:S(2)}, u32[]{:S(2)}) collective-permute-start(f32[1,48,64]{2,1,0:T(8,128)S(1)} %bitcast.20), channel_id=1, source_target_pairs={{0,24},{8,0},{16,8},{24,16},{1,25},{9,1},{17,9},{25,17},{2,26},{10... | collective-permute-start | bytes 36872 | tf_op jit(solution)/shard_map/ppermute | solution.py:28
  53.1 0.7 %convert_bitcast_fusion = bf16[1,48,1536]{2,1,0:T(8,128)(2,1)} fusion(f32[48,1536]{1,0:T(8,128)S(1)} %get-tuple-element.46), kind=kLoop, calls=%fused_computation | loop fusion | flops 73728 | bytes 442368 | tf_op jit(solution)/shard_map/broadcast_in_dim | solution.py:456
  53.8 2.7 %collective-permute-done.18 = f32[1,48,64]{2,1,0:T(8,128)S(1)} collective-permute-done((f32[1,48,64]{2,1,0:T(8,128)S(1)}, f32[1,48,64]{2,1,0:T(8,128)S(1)}, u32[]{:S(2)}, u32[]{:S(2)}) %collective-permute-start.18) | collective-permute-done | bytes 12320 | tf_op jit(solution)/shard_map/ppermute | solution.py:28
  56.5 0.6 %copy.14 = f32[1,48,64]{2,1,0:T(8,128)} copy(f32[1,48,64]{2,1,0:T(8,128)S(1)} %collective-permute-done.18) | data formatting | bytes 24576
  (40 shorter events, 1.1 us)
Async XLA Ops:
  0.6 18.3 %copy-start.1 = (bf16[1536,384]{1,0:T(8,128)(2,1)S(1)}, bf16[1536,384]{1,0:T(8,128)(2,1)}, u32[]{:S(2)}) copy-start(bf16[1536,384]{1,0:T(8,128)(2,1)} %w_own.1) | copy-start | bytes 3538948
  0.6 18.3 %copy-start.2 = (bf16[1,48,1536]{2,1,0:T(8,128)(2,1)S(1)}, bf16[1,48,1536]{2,1,0:T(8,128)(2,1)}, u32[]{:S(2)}) copy-start(bf16[1,48,1536]{2,1,0:T(8,128)(2,1)} %param.10) | copy-start | bytes 442372
  0.7 18.3 %copy-start.5 = (f32[1,3,1536]{2,0,1:T(1,128)S(1)}, f32[1,3,1536]{2,0,1:T(1,128)}, u32[]{:S(2)}) copy-start(f32[1,3,1536]{2,0,1:T(1,128)} %param.12) | copy-start | bytes 55300
  0.7 18.3 %copy-start.4 = (f32[3,1536]{1,0:T(4,128)S(1)}, f32[3,1536]{1,0:T(4,128)}, u32[]{:S(2)}) copy-start(f32[3,1536]{1,0:T(4,128)} %block_in.1) | copy-start | bytes 55300
  1.9 15.2 %collective-permute-start = (bf16[768,384]{1,0:T(8,128)(2,1)S(1)}, bf16[768,384]{1,0:T(8,128)(2,1)S(1)}, u32[]{:S(2)}, u32[]{:S(2)}) collective-permute-start(bf16[768,384]{1,0:T(8,128)(2,1)S(1)} %constant_dynamic-slice_fusion), channel_id=1, source_target_pairs={{0,1},{1,0},{2,3},{3,2},{4,5},{5,4},{6,7},{7,6},{8,9},{9,8},{10,11... | collective-permute-start | bytes 1769480 | tf_op jit(solution)/shard_map/ppermute | solution.py:383
  4.0 14.9 %collective-permute-start.2 = (bf16[48,1536]{1,0:T(8,128)(2,1)}, bf16[48,1536]{1,0:T(8,128)(2,1)S(1)}, u32[]{:S(2)}, u32[]{:S(2)}) collective-permute-start(bf16[48,1536]{1,0:T(8,128)(2,1)} %bitcast.10), channel_id=1, source_target_pairs={{0,4},{1,5},{2,6},{3,7},{4,0},{5,1},{6,2},{7,3},{8,12},{9,13},{10,... | collective-permute-start | bytes 442376 | tf_op jit(solution)/shard_map/ppermute | solution.py:380
  6.4 12.6 %collective-permute-start.3 = (bf16[48,1536]{1,0:T(8,128)(2,1)}, bf16[48,1536]{1,0:T(8,128)(2,1)S(1)}, u32[]{:S(2)}, u32[]{:S(2)}) collective-permute-start(bf16[48,1536]{1,0:T(8,128)(2,1)} %bitcast.11), channel_id=1, source_target_pairs={{0,2},{1,3},{2,0},{3,1},{4,6},{5,7},{6,4},{7,5},{8,10},{9,11},{10,... | collective-permute-start | bytes 442376 | tf_op jit(solution)/shard_map/ppermute | solution.py:380
  7.7 11.3 %collective-permute-start.4 = (bf16[48,1536]{1,0:T(8,128)(2,1)}, bf16[48,1536]{1,0:T(8,128)(2,1)S(1)}, u32[]{:S(2)}, u32[]{:S(2)}) collective-permute-start(bf16[48,1536]{1,0:T(8,128)(2,1)} %bitcast.12), channel_id=1, source_target_pairs={{0,6},{1,7},{2,4},{3,5},{4,2},{5,3},{6,0},{7,1},{8,14},{9,15},{10,... | collective-permute-start | bytes 442376 | tf_op jit(solution)/shard_map/ppermute | solution.py:380
  17.1 2.9 %collective-permute-start.1 = (bf16[768,384]{1,0:T(8,128)(2,1)S(1)}, bf16[768,384]{1,0:T(8,128)(2,1)S(1)}, u32[]{:S(2)}, u32[]{:S(2)}) collective-permute-start(bf16[768,384]{1,0:T(8,128)(2,1)S(1)} %collective-permute-done.w_first), channel_id=1, source_target_pairs={{0,8},{8,0},{16,24},{24,16},{1,9},{9,1},{17,25},{25,17},{2,10},{10... | collective-permute-start | bytes 1769480 | tf_op jit(solution)/shard_map/ppermute | solution.py:386
  19.9 10.8 %copy-start.8 = (f32[2,1024]{1,0:T(2,128)S(1)}, f32[2,1024]{1,0:T(2,128)}, u32[]{:S(2)}) copy-start(f32[2,1024]{1,0:T(2,128)} %gains.1) | copy-start | bytes 24580
  20.7 9.4 %collective-permute-start.5 = (bf16[208,256]{1,0:T(8,128)(2,1)S(1)}, bf16[208,256]{1,0:T(8,128)(2,1)S(1)}, u32[]{:S(2)}, u32[]{:S(2)}) collective-permute-start(bf16[208,256]{1,0:T(8,128)(2,1)S(1)} %get-tuple-element.28), channel_id=1, source_target_pairs={{0,4},{1,5},{2,6},{3,7},{4,0},{5,1},{6,2},{7,3},{8,12},{9,13},{10,... | collective-permute-start | bytes 319496 | tf_op jit(solution)/shard_map/ppermute | solution.py:380
  24.5 6.3 %collective-permute-start.7 = (bf16[208,256]{1,0:T(8,128)(2,1)S(1)}, bf16[208,256]{1,0:T(8,128)(2,1)S(1)}, u32[]{:S(2)}, u32[]{:S(2)}) collective-permute-start(bf16[208,256]{1,0:T(8,128)(2,1)S(1)} %get-tuple-element.30), channel_id=1, source_target_pairs={{0,2},{1,3},{2,0},{3,1},{4,6},{5,7},{6,4},{7,5},{8,10},{9,11},{10,... | collective-permute-start | bytes 319496 | tf_op jit(solution)/shard_map/ppermute | solution.py:380
  24.6 5.0 %collective-permute-start.6 = (bf16[16,256]{1,0:T(8,128)(2,1)S(1)}, bf16[16,256]{1,0:T(8,128)(2,1)S(1)}, u32[]{:S(2)}, u32[]{:S(2)}) collective-permute-start(bf16[16,256]{1,0:T(8,128)(2,1)S(1)} %get-tuple-element.29.own_sums), channel_id=1, source_target_pairs={{0,6},{1,7},{2,4},{3,5},{4,2},{5,3},{6,0},{7,1},{8,14},{9,15},{10,... | collective-permute-start | bytes 24584 | tf_op jit(solution)/shard_map/ppermute | solution.py:380
  25.8 22.6 %copy-start = (bf16[1024,1536]{1,0:T(8,128)(2,1)S(1)}, bf16[1024,1536]{1,0:T(8,128)(2,1)}, u32[]{:S(2)}) copy-start(bf16[1024,1536]{1,0:T(8,128)(2,1)} %w_out.3) | copy-start | bytes 9437188
  31.1 5.2 %collective-permute-start.8 = (bf16[192,512]{1,0:T(8,128)(2,1)S(1)}, bf16[192,512]{1,0:T(8,128)(2,1)S(1)}, u32[]{:S(2)}, u32[]{:S(2)}) collective-permute-start(bf16[192,512]{1,0:T(8,128)(2,1)S(1)} %get-tuple-element.35.a0), channel_id=1, source_target_pairs={{0,16},{8,24},{16,0},{24,8},{1,17},{9,25},{17,1},{25,9},{2,18},{10... | collective-permute-start | bytes 589832 | tf_op jit(solution)/shard_map/ppermute | solution.py:389
  32.3 4.8 %collective-permute-start.9 = (bf16[192,512]{1,0:T(8,128)(2,1)S(1)}, bf16[192,512]{1,0:T(8,128)(2,1)S(1)}, u32[]{:S(2)}, u32[]{:S(2)}) collective-permute-start(bf16[192,512]{1,0:T(8,128)(2,1)S(1)} %get-tuple-element.35.a0), channel_id=1, source_target_pairs={{0,1},{1,0},{2,3},{3,2},{4,5},{5,4},{6,7},{7,6},{8,9},{9,8},{10,11... | collective-permute-start | bytes 589832 | tf_op jit(solution)/shard_map/ppermute | solution.py:383
  32.3 8.5 %collective-permute-start.13 = (bf16[192,512]{1,0:T(8,128)(2,1)S(1)}, bf16[192,512]{1,0:T(8,128)(2,1)S(1)}, u32[]{:S(2)}, u32[]{:S(2)}) collective-permute-start(bf16[192,512]{1,0:T(8,128)(2,1)S(1)} %get-tuple-element.35.a0), channel_id=1, source_target_pairs={{0,17},{1,16},{2,19},{3,18},{4,21},{5,20},{6,23},{7,22},{8,25},{9,... | collective-permute-start | bytes 589832 | tf_op jit(solution)/shard_map/ppermute | solution.py:398
  37.1 6.6 %collective-permute-start.11 = (bf16[192,512]{1,0:T(8,128)(2,1)S(1)}, bf16[192,512]{1,0:T(8,128)(2,1)S(1)}, u32[]{:S(2)}, u32[]{:S(2)}) collective-permute-start(bf16[192,512]{1,0:T(8,128)(2,1)S(1)} %collective-permute-done.9.a1), channel_id=1, source_target_pairs={{0,8},{8,0},{16,24},{24,16},{1,9},{9,1},{17,25},{25,17},{2,10},{10... | collective-permute-start | bytes 589832 | tf_op jit(solution)/shard_map/ppermute | solution.py:386
  40.2 3.4 %collective-permute-start.10 = (bf16[192,512]{1,0:T(8,128)(2,1)S(1)}, bf16[192,512]{1,0:T(8,128)(2,1)S(1)}, u32[]{:S(2)}, u32[]{:S(2)}) collective-permute-start(bf16[192,512]{1,0:T(8,128)(2,1)S(1)} %get-tuple-element.35.a0), channel_id=1, source_target_pairs={{0,8},{8,0},{16,24},{24,16},{1,9},{9,1},{17,25},{25,17},{2,10},{10... | collective-permute-start | bytes 589832 | tf_op jit(solution)/shard_map/ppermute | solution.py:386
  40.2 3.5 %collective-permute-start.12 = (bf16[192,512]{1,0:T(8,128)(2,1)S(1)}, bf16[192,512]{1,0:T(8,128)(2,1)S(1)}, u32[]{:S(2)}, u32[]{:S(2)}) collective-permute-start(bf16[192,512]{1,0:T(8,128)(2,1)S(1)} %collective-permute-done.8.c0), channel_id=1, source_target_pairs={{0,8},{8,0},{16,24},{24,16},{1,9},{9,1},{17,25},{25,17},{2,10},{10... | collective-permute-start | bytes 589832 | tf_op jit(solution)/shard_map/ppermute | solution.py:386
  40.7 3.0 %collective-permute-start.14 = (bf16[192,512]{1,0:T(8,128)(2,1)S(1)}, bf16[192,512]{1,0:T(8,128)(2,1)S(1)}, u32[]{:S(2)}, u32[]{:S(2)}) collective-permute-start(bf16[192,512]{1,0:T(8,128)(2,1)S(1)} %collective-permute-done.13.c1), channel_id=1, source_target_pairs={{0,8},{8,0},{16,24},{24,16},{1,9},{9,1},{17,25},{25,17},{2,10},{10... | collective-permute-start | bytes 589832 | tf_op jit(solution)/shard_map/ppermute | solution.py:386
  42.7 5.7 %copy-start.7 = (f32[1,2,1536]{2,1,0:T(2,128)S(1)}, f32[1,2,1536]{2,1,0:T(2,128)}, u32[]{:S(2)}) copy-start(f32[1,2,1536]{2,1,0:T(2,128)} %param.17) | copy-start | bytes 36868
  44.8 4.5 %collective-permute-start.15 = (bf16[48,256]{1,0:T(8,128)(2,1)S(1)}, bf16[48,256]{1,0:T(8,128)(2,1)S(1)}, u32[]{:S(2)}, u32[]{:S(2)}) collective-permute-start(bf16[48,256]{1,0:T(8,128)(2,1)S(1)} %get-tuple-element.39), channel_id=1, source_target_pairs={{0,6},{1,7},{2,4},{3,5},{4,2},{5,3},{6,0},{7,1},{8,14},{9,15},{10,... | collective-permute-start | bytes 73736 | tf_op jit(solution)/shard_map/ppermute | solution.py:380
  46.6 4.1 %collective-permute-start.16 = (bf16[48,256]{1,0:T(8,128)(2,1)S(1)}, bf16[48,256]{1,0:T(8,128)(2,1)S(1)}, u32[]{:S(2)}, u32[]{:S(2)}) collective-permute-start(bf16[48,256]{1,0:T(8,128)(2,1)S(1)} %get-tuple-element.40), channel_id=1, source_target_pairs={{0,4},{1,5},{2,6},{3,7},{4,0},{5,1},{6,2},{7,3},{8,12},{9,13},{10,... | collective-permute-start | bytes 73736 | tf_op jit(solution)/shard_map/ppermute | solution.py:380
  46.6 4.1 %collective-permute-start.17 = (bf16[48,256]{1,0:T(8,128)(2,1)S(1)}, bf16[48,256]{1,0:T(8,128)(2,1)S(1)}, u32[]{:S(2)}, u32[]{:S(2)}) collective-permute-start(bf16[48,256]{1,0:T(8,128)(2,1)S(1)} %get-tuple-element.41), channel_id=1, source_target_pairs={{0,2},{1,3},{2,0},{3,1},{4,6},{5,7},{6,4},{7,5},{8,10},{9,11},{10,... | collective-permute-start | bytes 73736 | tf_op jit(solution)/shard_map/ppermute | solution.py:380
  48.4 2.4 %copy-start.3 = (bf16[1536,64]{0,1:T(8,128)(2,1)S(1)}, bf16[1536,64]{0,1:T(8,128)(2,1)}, u32[]{:S(2)}) copy-start(bf16[1536,64]{0,1:T(8,128)(2,1)} %param.18) | copy-start | bytes 589828
  48.4 2.4 %copy-start.6 = (f32[1,48,64]{2,1,0:T(8,128)S(1)}, f32[1,48,64]{2,1,0:T(8,128)}, u32[]{:S(2)}) copy-start(f32[1,48,64]{2,1,0:T(8,128)} %param.11) | copy-start | bytes 36868
  51.8 4.7 %collective-permute-start.18 = (f32[1,48,64]{2,1,0:T(8,128)S(1)}, f32[1,48,64]{2,1,0:T(8,128)S(1)}, u32[]{:S(2)}, u32[]{:S(2)}) collective-permute-start(f32[1,48,64]{2,1,0:T(8,128)S(1)} %bitcast.20), channel_id=1, source_target_pairs={{0,24},{8,0},{16,8},{24,16},{1,25},{9,1},{17,9},{25,17},{2,26},{10... | collective-permute-start | bytes 36872 | tf_op jit(solution)/shard_map/ppermute | solution.py:28

commit v4 on v3

--- a/solution.py
+++ b/solution.py
@@ -168,32 +168,45 @@
     return lax.dot_general(left, right, (((1,), (1,)), ((), ())), preferred_element_type=F32)
 
 
-def modulated(rows, time_mod, block_mod):
-    shift = block_mod[0:1] + time_mod[0]
-    scale = 1.0 + (block_mod[1:2] + time_mod[1])
-    return (layer_norm(rows[...].astype(F32)) * scale + shift).astype(BF16)
+def modulated(rows, shift_scale):
+    return (layer_norm(rows[...].astype(F32)) * shift_scale[1:2] + shift_scale[0:1]).astype(BF16)
+
+
+def prepare_kernel(x0, time_mod, block_mod, modded, shift_scale):
+    shift_scale[0:1] = block_mod[0:1] + time_mod[0]
+    shift_scale[1:2] = 1.0 + (block_mod[1:2] + time_mod[1])
+    modded[...] = modulated(x0, shift_scale)
 
 
 def first_kernel(
-    x2, x1, x3, x0, time_mod, block_mod, w_own, w_first, modded, own, other
-):
-    for place, rows in enumerate((x2, x1, x3, x0)):
-        modded[place * TOK_DEV : (place + 1) * TOK_DEV, :] = modulated(rows, time_mod, block_mod)
-    half = D // 2
-    at = pl.multiple_of(here()[2] * half, half)
+    x1, x2, x3, modded_own, shift_scale, w_own, w_mine, w_last, w_chip, modded, own, other
+):
+    for place, rows in enumerate((x2, x1, x3)):
+        modded[place * TOK_DEV : (place + 1) * TOK_DEV, :] = modulated(rows, shift_scale)
+    modded[3 * TOK_DEV :, :] = modded_own[...]
+    _, _, core, chip = here()
     own[...] = jnp.dot(modded[...], w_own[...], preferred_element_type=F32).astype(BF16)
-    other[...] = jnp.dot(modded[:, pl.ds(at, half)], w_first[...], preferred_element_type=F32)
+    total = part_product(modded, w_mine, 2 * chip + core)
+    total += part_product(modded, w_last, 4 + core)
+    other[...] = total + part_product(modded, w_chip, 2 * (1 - chip) + core)
+
+
+def part_product(modded, weights, part):
+    depth = weights.shape[0]
+    at = pl.multiple_of(part * depth, depth)
+    return jnp.dot(modded[:, pl.ds(at, depth)], weights[...], preferred_element_type=F32)
 
 
 def project_kernel(
-    w_second, modded, own_in, other_in, far_out, near_out, keep_out, sums_out, mixed
-):
-    line, side, core, _ = here()
-    half = D // 2
-    width = w_second.shape[1]
-    at = pl.multiple_of((1 - core) * half, half)
-    other = jnp.dot(modded[:, pl.ds(at, half)], w_second[...], preferred_element_type=F32)
-    other = (other + other_in[...]).astype(BF16)
+    w_core, w_core_last, w_core_chip, modded, own_in, other_in,
+    far_out, near_out, keep_out, sums_out, mixed,
+):
+    line, side, core, chip = here()
+    width = w_core.shape[1]
+    total = other_in[...] + part_product(modded, w_core, 2 * chip + 1 - core)
+    total += part_product(modded, w_core_last, 4 + 1 - core)
+    total += part_product(modded, w_core_chip, 2 * (1 - chip) + 1 - core)
+    other = total.astype(BF16)
     mine = pl.multiple_of(side * width, width)
     there = pl.multiple_of((1 - side) * width, width)
     for place, step in enumerate((2, 1, 3, 0)):
@@ -241,7 +254,7 @@
 
 
 def rope_kernel(
-    far, last_sums, near, keep, own_sums, gains, cosines, sines, levels, q_out, kv_out, size, units
+    near, far, last_sums, keep, own_sums, gains, cosines, sines, levels, q_out, kv_out, size, units
 ):
     line, _, _, _ = here()
     upper, odd = line // 2, line % 2
@@ -399,8 +412,13 @@
 
     rows = stream[0]
     time_rows = time_mod.transpose(1, 0, 2)
-    w_first = across(lax.dynamic_slice_in_dim(w_qkv, core * (D // 2), D // 2, 0))
-    x3, x2, x1 = along(3, rows), along(2, rows), along(1, rows)
+    depth = D // 6
+    half_mine = lax.dynamic_slice_in_dim(w_qkv, (slab // 2 * 2 + core) * depth, depth, 0)
+    half_last = lax.dynamic_slice_in_dim(w_qkv, (4 + core) * depth, depth, 0)
+    w_mine, w_last = across(half_mine), across(half_last)
+    late_rows, _ = lax.optimization_barrier((rows, half_mine))
+    x1, x2, x3 = along(1, rows), along(2, rows), along(3, rows)
+
     at = (jnp.arange(LINE)[:, None] * 2 + side) * TOK_DEV + jnp.arange(TOK_DEV)[None]
     position = (slab * (2 * LINE * TOK_DEV) + at.reshape(ROWS)).astype(F32)
     halves = HEAD_DIM // 2
@@ -409,25 +427,31 @@
     cosines, sines = jnp.cos(angles), jnp.sin(angles)
     cosines = jnp.concatenate([cosines, cosines], axis=1)
     sines = jnp.concatenate([-sines, sines], axis=1)
-
-    w_second = cores(w_first)
+    modded_own, shift_scale = vmem_call(
+        prepare_kernel, [((TOK_DEV, D), BF16), ((2, D), F32)], "prepare", 1 << 20
+    )(rows, time_rows, block_mod)
+    w_chip = chips(w_mine)
+    w_last, modded_own, shift_scale = lax.optimization_barrier((w_last, modded_own, shift_scale))
+    w_core_last = cores(w_last)
+    w_mine, w_chip = lax.optimization_barrier((w_mine, w_chip))
+    w_core, w_core_chip = cores(w_mine), cores(w_chip)
     width = w_qkv.shape[1]
     modded, own, other = vmem_call(
         first_kernel, [((ROWS, D), BF16), ((ROWS, width), BF16), ((ROWS, width), F32)],
         "first", 1 << 28,
-    )(x2, x1, x3, rows, time_rows, block_mod, w_qkv, w_first)
+    )(x1, x2, x3, modded_own, shift_scale, w_qkv, w_mine, w_last, w_chip)
     message = (ROWS + 16, PAIR)
     far, near, keep, sums = vmem_call(
         project_kernel,
         [(message, BF16), (message, BF16), ((ROWS, PAIR), BF16), ((16, PAIR), BF16)],
         "project", 1 << 28, [pltpu.VMEM((ROWS, 3 * PAIR), BF16)],
-    )(w_second, modded, own, other)
+    )(w_core, w_core_last, w_core_chip, modded, own, other)
     far, last_sums, near = along(2, far), along(3, sums), along(1, near)
     queries, pairs, size = vmem_call(
         rope_kernel,
         [((ROWS, PAIR), BF16), ((ROWS, 2 * PAIR), BF16), ((1, HEAD_DIM), F32)],
         "rope", 1 << 22, [pltpu.VMEM((3, ROWS, PAIR), BF16)],
-    )(far, last_sums, near, keep, sums, qk_gain, cosines, sines, noise_level[None])
+    )(near, far, last_sums, keep, sums, qk_gain, cosines, sines, noise_level[None])
     chip_pairs, side_pairs = chips(pairs), across(pairs)
     both_pairs = chips_and_sides(pairs)
     chip_pairs, side_pairs = lax.optimization_barrier((chip_pairs, side_pairs))

time: 57.2 us -> 55.5 us (0.970)
  waiting for transfers between devices: 21.4 us -> 12.4 us
  starting transfers between devices: 25.2 us -> 29.9 us
  local copies, waits for them, and re-layouts: 1.95 us -> 4.26 us
    ppermute x2 -> x3, waiting for transfers between devices: 10.2 us -> 2.31 us  [across(): return lax.ppermute(value, 'seq', [(i, i ^ 1) for i in range(2 * LINE)])]
    unnamed x19 -> x25, local copies, waits for them, and re-layouts: 0.65 us -> 3.02 us
    ppermute x5 -> x7, starting transfers between devices: 6.81 us -> 8.89 us  [cores(): return lax.ppermute(value, 'slab', [(i, i ^ 1) for i in range(4)])]
    ppermute x1 -> x2, starting transfers between devices: 1.19 us -> 2.41 us  [chips(): return lax.ppermute(value, 'slab', [(i, i ^ 2) for i in range(4)])]
    ppermute x9, starting transfers between devices: 12.3 us -> 13.3 us  [along(): lax.ppermute(value, 'seq', [(i, i ^ 2 * step) for i in range(2 * LINE)])]
    ppermute x9, waiting for transfers between devices: 5.85 us -> 5.08 us  [along(): lax.ppermute(value, 'seq', [(i, i ^ 2 * step) for i in range(2 * LINE)])]
    ppermute x1 -> x2, waiting for transfers between devices: 2.52 us -> 1.87 us  [chips(): return lax.ppermute(value, 'slab', [(i, i ^ 2) for i in range(4)])]
    ppermute x2 -> x3, starting transfers between devices: 2.14 us -> 2.59 us  [across(): return lax.ppermute(value, 'seq', [(i, i ^ 1) for i in range(2 * LINE)])]
  transfers between devices with their start and end apart: 19 -> 23, of which waited for: 10 -> 10; matrix products, arithmetic and copies ran while one was open for 2% -> 3% of each run, Pallas kernels for 4% -> 5%
where the time goes in v4:
time: 55.5 us; the launch traced here: 55.2 us
  starting transfers between devices  29.9 us (54%)
  waiting for transfers between devices  12.4 us (22%)
  Pallas kernels  5.72 us (10%)
  local copies, waits for them, and re-layouts  4.26 us (8%)
  between operations  1.68 us (3%)
  other arithmetic  1.3 us (2%)
    ppermute x9, starting transfers between devices, along(): lax.ppermute(value, 'seq', [(i, i ^ 2 * step) for i in range(2 * LINE)])  13.3 us
    ppermute x7, starting transfers between devices, cores(): return lax.ppermute(value, 'slab', [(i, i ^ 1) for i in range(4)])  8.89 us
    pallas_call x8, Pallas kernels, call(): pl.pallas_call(kernel, out_shape=[jax.ShapeDtypeStruct(shape, dtype) for...  5.72 us
    ppermute x9, waiting for transfers between devices, along(): lax.ppermute(value, 'seq', [(i, i ^ 2 * step) for i in range(2 * LINE)])  5.08 us
    ppermute x1, waiting for transfers between devices, from_behind(): return lax.ppermute(value, axis, pairs)  3.03 us
    unnamed x25, local copies, waits for them, and re-layouts  3.02 us
    ppermute x3, starting transfers between devices, across(): return lax.ppermute(value, 'seq', [(i, i ^ 1) for i in range(2 * LINE)])  2.59 us
    ppermute x2, starting transfers between devices, chips(): return lax.ppermute(value, 'slab', [(i, i ^ 2) for i in range(4)])  2.41 us
  transfers between devices with their start and end apart: 23, of which 10 were waited for; matrix products, arithmetic and copies ran while one was open for 3% of the time, Pallas kernels for 5%

profile of v4, /device:TPU:1, one launch (start us, length us, event | category | flops | bytes accessed | tf_op | source)
XLA Modules:
  0.0 55.2 jit_solution(6336387052040521423)
XLA Ops:
  0.7 1.2 %constant_dynamic-slice_fusion = (bf16[256,384]{1,0:T(8,128)(2,1)S(1)}, bf16[256,384]{1,0:T(8,128)(2,1)S(1)}) fusion(bf16[1536,384]{1,0:T(8,128)(2,1)} %w_own.1, s32[]{:T(128)S(6)} %select_n.24, s32[]{:T(128)S(6)} %select_n.23), kind=kLoop, calls=%fused_computation.9 | loop fusion | bytes 786440 | tf_op jit(solution)/shard_map/dynamic_slice | solution.py:417
  1.8 2.1 %collective-permute-start = (bf16[256,384]{1,0:T(8,128)(2,1)S(1)}, bf16[256,384]{1,0:T(8,128)(2,1)S(1)}, u32[]{:S(2)}, u32[]{:S(2)}) collective-permute-start(bf16[256,384]{1,0:T(8,128)(2,1)S(1)} %get-tuple-element.63), channel_id=1, source_target_pairs={{0,1},{1,0},{2,3},{3,2},{4,5},{5,4},{6,7},{7,6},{8,9},{9,8},{10,11... | collective-permute-start | bytes 589832 | tf_op jit(solution)/shard_map/ppermute | solution.py:396
  4.0 1.3 %collective-permute-start.6 = (bf16[48,1536]{1,0:T(8,128)(2,1)}, bf16[48,1536]{1,0:T(8,128)(2,1)S(1)}, u32[]{:S(2)}, u32[]{:S(2)}) collective-permute-start(bf16[48,1536]{1,0:T(8,128)(2,1)} %bitcast.10), channel_id=1, source_target_pairs={{0,2},{1,3},{2,0},{3,1},{4,6},{5,7},{6,4},{7,5},{8,10},{9,11},{10,... | collective-permute-start | bytes 442376 | tf_op jit(solution)/shard_map/ppermute | solution.py:393
  5.3 2.3 %collective-permute-start.7 = (bf16[48,1536]{1,0:T(8,128)(2,1)}, bf16[48,1536]{1,0:T(8,128)(2,1)S(1)}, u32[]{:S(2)}, u32[]{:S(2)}) collective-permute-start(bf16[48,1536]{1,0:T(8,128)(2,1)} %bitcast.11), channel_id=1, source_target_pairs={{0,4},{1,5},{2,6},{3,7},{4,0},{5,1},{6,2},{7,3},{8,12},{9,13},{10,... | collective-permute-start | bytes 442376 | tf_op jit(solution)/shard_map/ppermute | solution.py:393
  7.8 0.8 %collective-permute-done.w_mine = bf16[256,384]{1,0:T(8,128)(2,1)S(1)} collective-permute-done((bf16[256,384]{1,0:T(8,128)(2,1)S(1)}, bf16[256,384]{1,0:T(8,128)(2,1)S(1)}, u32[]{:S(2)}, u32[]{:S(2)}) %collective-permute-start) | collective-permute-done | bytes 196640 | tf_op jit(solution)/shard_map/ppermute | solution.py:396
  8.6 1.1 %collective-permute-start.1 = (bf16[256,384]{1,0:T(8,128)(2,1)S(1)}, bf16[256,384]{1,0:T(8,128)(2,1)S(1)}, u32[]{:S(2)}, u32[]{:S(2)}) collective-permute-start(bf16[256,384]{1,0:T(8,128)(2,1)S(1)} %collective-permute-done.w_mine), channel_id=1, source_target_pairs={{0,16},{8,24},{16,0},{24,8},{1,17},{9,25},{17,1},{25,9},{2,18},{10... | collective-permute-start | bytes 589832 | tf_op jit(solution)/shard_map/ppermute | solution.py:402
  9.9 0.9 %copy-done.2 = bf16[1,48,1536]{2,1,0:T(8,128)(2,1)S(1)} copy-done((bf16[1,48,1536]{2,1,0:T(8,128)(2,1)S(1)}, bf16[1,48,1536]{2,1,0:T(8,128)(2,1)}, u32[]{:S(2)}) %copy-start.2) | copy-done | bytes 147480
  10.8 0.7 %copy-done.5 = f32[3,1536]{1,0:T(4,128)S(1)} copy-done((f32[3,1536]{1,0:T(4,128)S(1)}, f32[3,1536]{1,0:T(4,128)}, u32[]{:S(2)}) %copy-start.5) | copy-done | bytes 18456
  11.5 0.7 %copy-done.7 = f32[1,3,1536]{2,0,1:T(1,128)S(1)} copy-done((f32[1,3,1536]{2,0,1:T(1,128)S(1)}, f32[1,3,1536]{2,0,1:T(1,128)}, u32[]{:S(2)}) %copy-start.7) | copy-done | bytes 18456
  12.5 2.5 %collective-permute-start.4 = (bf16[256,384]{1,0:T(8,128)(2,1)S(1)}, bf16[256,384]{1,0:T(8,128)(2,1)S(1)}, u32[]{:S(2)}, u32[]{:S(2)}) collective-permute-start(bf16[256,384]{1,0:T(8,128)(2,1)S(1)} %collective-permute-done.3.w_last), channel_id=1, source_target_pairs={{0,8},{8,0},{16,24},{24,16},{1,9},{9,1},{17,25},{25,17},{2,10},{10... | collective-permute-start | bytes 589832 | tf_op jit(solution)/shard_map/ppermute | solution.py:399
  15.0 0.9 %collective-permute-start.2 = (bf16[256,384]{1,0:T(8,128)(2,1)S(1)}, bf16[256,384]{1,0:T(8,128)(2,1)S(1)}, u32[]{:S(2)}, u32[]{:S(2)}) collective-permute-start(bf16[256,384]{1,0:T(8,128)(2,1)S(1)} %collective-permute-done.w_mine), channel_id=1, source_target_pairs={{0,8},{8,0},{16,24},{24,16},{1,9},{9,1},{17,25},{25,17},{2,10},{10... | collective-permute-start | bytes 589832 | tf_op jit(solution)/shard_map/ppermute | solution.py:399
  17.0 0.9 %first.1 = (bf16[192,1536]{1,0:T(8,128)(2,1)S(1)}, bf16[192,384]{1,0:T(8,128)(2,1)S(1)}, f32[192,384]{1,0:T(8,128)S(1)}) custom-call(bf16[48,1536]{1,0:T(8,128)(2,1)S(1)} %collective-permute-done.6.x1, bf16[48,1536]{1,0:T(8,128)(2,1)S(1)} %collective-permute-done.7.x2, bf16[48,1536]{1,0:T(8,128)(2,1)S(1)} %collective-permute-done.8.x3, ...), custom_call_target="tpu_custom_call" | custom-call | flops 268435456 | bytes 1048576 | tf_op jit(solution)/shard_map/first/pallas_call | solution.py:148
  17.9 0.7 %project.1 = (bf16[208,256]{1,0:T(8,128)(2,1)S(1)}, bf16[208,256]{1,0:T(8,128)(2,1)S(1)}, bf16[192,256]{1,0:T(8,128)(2,1)S(1)}, bf16[16,256]{1,0:T(8,128)(2,1)S(1)}) custom-call(bf16[256,384]{1,0:T(8,128)(2,1)S(1)} %collective-permute-done.2.w_core, bf16[256,384]{1,0:T(8,128)(2,1)S(1)} %collective-permute-done.4.w_core_last, ...), custom_call_target="tpu_custom_call" | custom-call | flops 268435456 | bytes 1048576 | tf_op jit(solution)/shard_map/project/pallas_call | solution.py:148
  18.6 4.8 %collective-permute-start.10 = (bf16[208,256]{1,0:T(8,128)(2,1)S(1)}, bf16[208,256]{1,0:T(8,128)(2,1)S(1)}, u32[]{:S(2)}, u32[]{:S(2)}) collective-permute-start(bf16[208,256]{1,0:T(8,128)(2,1)S(1)} %get-tuple-element.43), channel_id=1, source_target_pairs={{0,4},{1,5},{2,6},{3,7},{4,0},{5,1},{6,2},{7,3},{8,12},{9,13},{10,... | collective-permute-start | bytes 319496 | tf_op jit(solution)/shard_map/ppermute | solution.py:393
  23.4 1.3 %collective-permute-start.11 = (bf16[16,256]{1,0:T(8,128)(2,1)S(1)}, bf16[16,256]{1,0:T(8,128)(2,1)S(1)}, u32[]{:S(2)}, u32[]{:S(2)}) collective-permute-start(bf16[16,256]{1,0:T(8,128)(2,1)S(1)} %get-tuple-element.44.own_sums), channel_id=1, source_target_pairs={{0,6},{1,7},{2,4},{3,5},{4,2},{5,3},{6,0},{7,1},{8,14},{9,15},{10,... | collective-permute-start | bytes 24584 | tf_op jit(solution)/shard_map/ppermute | solution.py:393
  25.6 2.3 %collective-permute-done.11.last_sums = bf16[16,256]{1,0:T(8,128)(2,1)S(1)} collective-permute-done((bf16[16,256]{1,0:T(8,128)(2,1)S(1)}, bf16[16,256]{1,0:T(8,128)(2,1)S(1)}, u32[]{:S(2)}, u32[]{:S(2)}) %collective-permute-start.11) | collective-permute-done | bytes 8224 | tf_op jit(solution)/shard_map/ppermute | solution.py:393
  27.9 1.1 %collective-permute-done.9.near = bf16[208,256]{1,0:T(8,128)(2,1)S(1)} collective-permute-done((bf16[208,256]{1,0:T(8,128)(2,1)S(1)}, bf16[208,256]{1,0:T(8,128)(2,1)S(1)}, u32[]{:S(2)}, u32[]{:S(2)}) %collective-permute-start.9) | collective-permute-done | bytes 106528 | tf_op jit(solution)/shard_map/ppermute | solution.py:393
  29.3 1.3 %collective-permute-start.12 = (bf16[192,512]{1,0:T(8,128)(2,1)S(1)}, bf16[192,512]{1,0:T(8,128)(2,1)S(1)}, u32[]{:S(2)}, u32[]{:S(2)}) collective-permute-start(bf16[192,512]{1,0:T(8,128)(2,1)S(1)} %get-tuple-element.49.a0), channel_id=1, source_target_pairs={{0,16},{8,24},{16,0},{24,8},{1,17},{9,25},{17,1},{25,9},{2,18},{10... | collective-permute-start | bytes 589832 | tf_op jit(solution)/shard_map/ppermute | solution.py:402
  30.8 1.2 %collective-permute-start.17 = (bf16[192,512]{1,0:T(8,128)(2,1)S(1)}, bf16[192,512]{1,0:T(8,128)(2,1)S(1)}, u32[]{:S(2)}, u32[]{:S(2)}) collective-permute-start(bf16[192,512]{1,0:T(8,128)(2,1)S(1)} %get-tuple-element.49.a0), channel_id=1, source_target_pairs={{0,17},{1,16},{2,19},{3,18},{4,21},{5,20},{6,23},{7,22},{8,25},{9,... | collective-permute-start | bytes 589832 | tf_op jit(solution)/shard_map/ppermute | solution.py:411
  32.0 1.9 %collective-permute-done.12.c0 = bf16[192,512]{1,0:T(8,128)(2,1)S(1)} collective-permute-done((bf16[192,512]{1,0:T(8,128)(2,1)S(1)}, bf16[192,512]{1,0:T(8,128)(2,1)S(1)}, u32[]{:S(2)}, u32[]{:S(2)}) %collective-permute-start.12) | collective-permute-done | bytes 196640 | tf_op jit(solution)/shard_map/ppermute | solution.py:402
  33.9 1.5 %collective-permute-done.13.a1 = bf16[192,512]{1,0:T(8,128)(2,1)S(1)} collective-permute-done((bf16[192,512]{1,0:T(8,128)(2,1)S(1)}, bf16[192,512]{1,0:T(8,128)(2,1)S(1)}, u32[]{:S(2)}, u32[]{:S(2)}) %collective-permute-start.13) | collective-permute-done | bytes 196640 | tf_op jit(solution)/shard_map/ppermute | solution.py:396
  35.4 3.4 %collective-permute-start.15 = (bf16[192,512]{1,0:T(8,128)(2,1)S(1)}, bf16[192,512]{1,0:T(8,128)(2,1)S(1)}, u32[]{:S(2)}, u32[]{:S(2)}) collective-permute-start(bf16[192,512]{1,0:T(8,128)(2,1)S(1)} %collective-permute-done.13.a1), channel_id=1, source_target_pairs={{0,8},{8,0},{16,24},{24,16},{1,9},{9,1},{17,25},{25,17},{2,10},{10... | collective-permute-start | bytes 589832 | tf_op jit(solution)/shard_map/ppermute | solution.py:399
  39.3 1.6 %collective-permute-start.18 = (bf16[192,512]{1,0:T(8,128)(2,1)S(1)}, bf16[192,512]{1,0:T(8,128)(2,1)S(1)}, u32[]{:S(2)}, u32[]{:S(2)}) collective-permute-start(bf16[192,512]{1,0:T(8,128)(2,1)S(1)} %collective-permute-done.17.c1), channel_id=1, source_target_pairs={{0,8},{8,0},{16,24},{24,16},{1,9},{9,1},{17,25},{25,17},{2,10},{10... | collective-permute-start | bytes 589832 | tf_op jit(solution)/shard_map/ppermute | solution.py:399
  40.9 1.0 %attend_first.1 = (f32[2,192,256]{2,1,0:T(8,128)S(1)}, f32[2,192,128]{2,1,0:T(8,128)S(1)}) custom-call(bf16[192,256]{1,0:T(8,128)(2,1)S(1)} %get-tuple-element.46.queries, bf16[192,512]{1,0:T(8,128)(2,1)S(1)} %collective-permute-done.12.c0, bf16[192,512]{1,0:T(8,128)(2,1)S(1)} %collective-permute-done.17.c1, bf16[192,512]{1,0:T(8,128)(2,1)S(1)} %get-tuple-element.49.a0, ...), custom_call_target="tpu_custom_call" | custom-call | flops 134217728 | bytes 1048576 | tf_op jit(solution)/shard_map/attend_first/pallas_call | solution.py:148
  41.9 1.0 %attend_last.1 = (bf16[48,256]{1,0:T(8,128)(2,1)S(1)}, bf16[48,256]{1,0:T(8,128)(2,1)S(1)}, bf16[48,256]{1,0:T(8,128)(2,1)S(1)}, bf16[48,256]{1,0:T(8,128)(2,1)S(1)}) custom-call(bf16[192,256]{1,0:T(8,128)(2,1)S(1)} %get-tuple-element.46.queries, bf16[192,512]{1,0:T(8,128)(2,1)S(1)} %collective-permute-done.14.b0, ...), custom_call_target="tpu_custom_call" | custom-call | flops 134217728 | bytes 1048576 | tf_op jit(solution)/shard_map/attend_last/pallas_call | solution.py:148
  43.0 1.3 %collective-permute-start.19 = (bf16[48,256]{1,0:T(8,128)(2,1)S(1)}, bf16[48,256]{1,0:T(8,128)(2,1)S(1)}, u32[]{:S(2)}, u32[]{:S(2)}) collective-permute-start(bf16[48,256]{1,0:T(8,128)(2,1)S(1)} %get-tuple-element.53), channel_id=1, source_target_pairs={{0,6},{1,7},{2,4},{3,5},{4,2},{5,3},{6,0},{7,1},{8,14},{9,15},{10,... | collective-permute-start | bytes 73736 | tf_op jit(solution)/shard_map/ppermute | solution.py:393
  44.2 2.3 %collective-permute-start.21 = (bf16[48,256]{1,0:T(8,128)(2,1)S(1)}, bf16[48,256]{1,0:T(8,128)(2,1)S(1)}, u32[]{:S(2)}, u32[]{:S(2)}) collective-permute-start(bf16[48,256]{1,0:T(8,128)(2,1)S(1)} %get-tuple-element.55), channel_id=1, source_target_pairs={{0,2},{1,3},{2,0},{3,1},{4,6},{5,7},{6,4},{7,5},{8,10},{9,11},{10,... | collective-permute-start | bytes 73736 | tf_op jit(solution)/shard_map/ppermute | solution.py:393
  47.5 0.8 %collective-permute-done.20.r2 = bf16[48,256]{1,0:T(8,128)(2,1)S(1)} collective-permute-done((bf16[48,256]{1,0:T(8,128)(2,1)S(1)}, bf16[48,256]{1,0:T(8,128)(2,1)S(1)}, u32[]{:S(2)}, u32[]{:S(2)}) %collective-permute-start.20) | collective-permute-done | bytes 24608 | tf_op jit(solution)/shard_map/ppermute | solution.py:393
  48.3 1.0 %finish.1 = (f32[48,1536]{1,0:T(8,128)S(1)}, f32[48,64]{1,0:T(8,128)S(1)}) custom-call(bf16[48,256]{1,0:T(8,128)(2,1)S(1)} %collective-permute-done.19.r3, bf16[48,256]{1,0:T(8,128)(2,1)S(1)} %collective-permute-done.20.r2, bf16[48,256]{1,0:T(8,128)(2,1)S(1)} %collective-permute-done.21.r1, bf16[1024,1536]{1,0:T(8,128)(2,1)S(1)} %copy-done, ...), custom_call_target="tpu_custom_call" | custom-call | flops 268435456 | bytes 1048576 | tf_op jit(solution)/shard_map/finish/pallas_call | solution.py:148
  49.4 1.6 %collective-permute-start.22 = (f32[1,48,64]{2,1,0:T(8,128)S(1)}, f32[1,48,64]{2,1,0:T(8,128)S(1)}, u32[]{:S(2)}, u32[]{:S(2)}) collective-permute-start(f32[1,48,64]{2,1,0:T(8,128)S(1)} %bitcast.20), channel_id=1, source_target_pairs={{0,24},{8,0},{16,8},{24,16},{1,25},{9,1},{17,9},{25,17},{2,26},{10... | collective-permute-start | bytes 36872 | tf_op jit(solution)/shard_map/ppermute | solution.py:28
  50.9 0.7 %convert_bitcast_fusion = bf16[1,48,1536]{2,1,0:T(8,128)(2,1)} fusion(f32[48,1536]{1,0:T(8,128)S(1)} %get-tuple-element.60), kind=kLoop, calls=%fused_computation | loop fusion | flops 73728 | bytes 442368 | tf_op jit(solution)/shard_map/broadcast_in_dim | solution.py:480
  51.6 3.0 %collective-permute-done.22 = f32[1,48,64]{2,1,0:T(8,128)S(1)} collective-permute-done((f32[1,48,64]{2,1,0:T(8,128)S(1)}, f32[1,48,64]{2,1,0:T(8,128)S(1)}, u32[]{:S(2)}, u32[]{:S(2)}) %collective-permute-start.22) | collective-permute-done | bytes 12320 | tf_op jit(solution)/shard_map/ppermute | solution.py:28
  (55 shorter events, 4.4 us)
Async XLA Ops:
  0.6 16.3 %copy-start.1 = (bf16[1536,384]{1,0:T(8,128)(2,1)S(1)}, bf16[1536,384]{1,0:T(8,128)(2,1)}, u32[]{:S(2)}) copy-start(bf16[1536,384]{1,0:T(8,128)(2,1)} %w_own.1) | copy-start | bytes 3538948
  1.8 6.8 %collective-permute-start = (bf16[256,384]{1,0:T(8,128)(2,1)S(1)}, bf16[256,384]{1,0:T(8,128)(2,1)S(1)}, u32[]{:S(2)}, u32[]{:S(2)}) collective-permute-start(bf16[256,384]{1,0:T(8,128)(2,1)S(1)} %get-tuple-element.63), channel_id=1, source_target_pairs={{0,1},{1,0},{2,3},{3,2},{4,5},{5,4},{6,7},{7,6},{8,9},{9,8},{10,11... | collective-permute-start | bytes 589832 | tf_op jit(solution)/shard_map/ppermute | solution.py:396
  4.0 11.9 %collective-permute-start.6 = (bf16[48,1536]{1,0:T(8,128)(2,1)}, bf16[48,1536]{1,0:T(8,128)(2,1)S(1)}, u32[]{:S(2)}, u32[]{:S(2)}) collective-permute-start(bf16[48,1536]{1,0:T(8,128)(2,1)} %bitcast.10), channel_id=1, source_target_pairs={{0,2},{1,3},{2,0},{3,1},{4,6},{5,7},{6,4},{7,5},{8,10},{9,11},{10,... | collective-permute-start | bytes 442376 | tf_op jit(solution)/shard_map/ppermute | solution.py:393
  5.3 11.1 %collective-permute-start.7 = (bf16[48,1536]{1,0:T(8,128)(2,1)}, bf16[48,1536]{1,0:T(8,128)(2,1)S(1)}, u32[]{:S(2)}, u32[]{:S(2)}) collective-permute-start(bf16[48,1536]{1,0:T(8,128)(2,1)} %bitcast.11), channel_id=1, source_target_pairs={{0,4},{1,5},{2,6},{3,7},{4,0},{5,1},{6,2},{7,3},{8,12},{9,13},{10,... | collective-permute-start | bytes 442376 | tf_op jit(solution)/shard_map/ppermute | solution.py:393
  7.6 9.4 %collective-permute-start.8 = (bf16[48,1536]{1,0:T(8,128)(2,1)}, bf16[48,1536]{1,0:T(8,128)(2,1)S(1)}, u32[]{:S(2)}, u32[]{:S(2)}) collective-permute-start(bf16[48,1536]{1,0:T(8,128)(2,1)} %bitcast.12), channel_id=1, source_target_pairs={{0,6},{1,7},{2,4},{3,5},{4,2},{5,3},{6,0},{7,1},{8,14},{9,15},{10,... | collective-permute-start | bytes 442376 | tf_op jit(solution)/shard_map/ppermute | solution.py:393
  7.6 4.9 %collective-permute-start.3 = (bf16[256,384]{1,0:T(8,128)(2,1)S(1)}, bf16[256,384]{1,0:T(8,128)(2,1)S(1)}, u32[]{:S(2)}, u32[]{:S(2)}) collective-permute-start(bf16[256,384]{1,0:T(8,128)(2,1)S(1)} %get-tuple-element.62), channel_id=1, source_target_pairs={{0,1},{1,0},{2,3},{3,2},{4,5},{5,4},{6,7},{7,6},{8,9},{9,8},{10,11... | collective-permute-start | bytes 589832 | tf_op jit(solution)/shard_map/ppermute | solution.py:396
  8.6 6.4 %collective-permute-start.1 = (bf16[256,384]{1,0:T(8,128)(2,1)S(1)}, bf16[256,384]{1,0:T(8,128)(2,1)S(1)}, u32[]{:S(2)}, u32[]{:S(2)}) collective-permute-start(bf16[256,384]{1,0:T(8,128)(2,1)S(1)} %collective-permute-done.w_mine), channel_id=1, source_target_pairs={{0,16},{8,24},{16,0},{24,8},{1,17},{9,25},{17,1},{25,9},{2,18},{10... | collective-permute-start | bytes 589832 | tf_op jit(solution)/shard_map/ppermute | solution.py:402
  12.5 5.4 %collective-permute-start.4 = (bf16[256,384]{1,0:T(8,128)(2,1)S(1)}, bf16[256,384]{1,0:T(8,128)(2,1)S(1)}, u32[]{:S(2)}, u32[]{:S(2)}) collective-permute-start(bf16[256,384]{1,0:T(8,128)(2,1)S(1)} %collective-permute-done.3.w_last), channel_id=1, source_target_pairs={{0,8},{8,0},{16,24},{24,16},{1,9},{9,1},{17,25},{25,17},{2,10},{10... | collective-permute-start | bytes 589832 | tf_op jit(solution)/shard_map/ppermute | solution.py:399
  15.0 2.9 %collective-permute-start.2 = (bf16[256,384]{1,0:T(8,128)(2,1)S(1)}, bf16[256,384]{1,0:T(8,128)(2,1)S(1)}, u32[]{:S(2)}, u32[]{:S(2)}) collective-permute-start(bf16[256,384]{1,0:T(8,128)(2,1)S(1)} %collective-permute-done.w_mine), channel_id=1, source_target_pairs={{0,8},{8,0},{16,24},{24,16},{1,9},{9,1},{17,25},{25,17},{2,10},{10... | collective-permute-start | bytes 589832 | tf_op jit(solution)/shard_map/ppermute | solution.py:399
  15.9 2.0 %collective-permute-start.5 = (bf16[256,384]{1,0:T(8,128)(2,1)S(1)}, bf16[256,384]{1,0:T(8,128)(2,1)S(1)}, u32[]{:S(2)}, u32[]{:S(2)}) collective-permute-start(bf16[256,384]{1,0:T(8,128)(2,1)S(1)} %collective-permute-done.1.w_chip), channel_id=1, source_target_pairs={{0,8},{8,0},{16,24},{24,16},{1,9},{9,1},{17,25},{25,17},{2,10},{10... | collective-permute-start | bytes 589832 | tf_op jit(solution)/shard_map/ppermute | solution.py:399
  17.9 11.1 %copy-start.11 = (f32[2,1024]{1,0:T(2,128)S(1)}, f32[2,1024]{1,0:T(2,128)}, u32[]{:S(2)}) copy-start(f32[2,1024]{1,0:T(2,128)} %gains.1) | copy-start | bytes 24580
  18.6 9.3 %collective-permute-start.10 = (bf16[208,256]{1,0:T(8,128)(2,1)S(1)}, bf16[208,256]{1,0:T(8,128)(2,1)S(1)}, u32[]{:S(2)}, u32[]{:S(2)}) collective-permute-start(bf16[208,256]{1,0:T(8,128)(2,1)S(1)} %get-tuple-element.43), channel_id=1, source_target_pairs={{0,4},{1,5},{2,6},{3,7},{4,0},{5,1},{6,2},{7,3},{8,12},{9,13},{10,... | collective-permute-start | bytes 319496 | tf_op jit(solution)/shard_map/ppermute | solution.py:393
  23.4 5.6 %collective-permute-start.9 = (bf16[208,256]{1,0:T(8,128)(2,1)S(1)}, bf16[208,256]{1,0:T(8,128)(2,1)S(1)}, u32[]{:S(2)}, u32[]{:S(2)}) collective-permute-start(bf16[208,256]{1,0:T(8,128)(2,1)S(1)} %get-tuple-element.42), channel_id=1, source_target_pairs={{0,2},{1,3},{2,0},{3,1},{4,6},{5,7},{6,4},{7,5},{8,10},{9,11},{10,... | collective-permute-start | bytes 319496 | tf_op jit(solution)/shard_map/ppermute | solution.py:393
  23.4 4.5 %collective-permute-start.11 = (bf16[16,256]{1,0:T(8,128)(2,1)S(1)}, bf16[16,256]{1,0:T(8,128)(2,1)S(1)}, u32[]{:S(2)}, u32[]{:S(2)}) collective-permute-start(bf16[16,256]{1,0:T(8,128)(2,1)S(1)} %get-tuple-element.44.own_sums), channel_id=1, source_target_pairs={{0,6},{1,7},{2,4},{3,5},{4,2},{5,3},{6,0},{7,1},{8,14},{9,15},{10,... | collective-permute-start | bytes 24584 | tf_op jit(solution)/shard_map/ppermute | solution.py:393
  24.7 21.9 %copy-start = (bf16[1024,1536]{1,0:T(8,128)(2,1)S(1)}, bf16[1024,1536]{1,0:T(8,128)(2,1)}, u32[]{:S(2)}) copy-start(bf16[1024,1536]{1,0:T(8,128)(2,1)} %w_out.3) | copy-start | bytes 9437188
  29.3 4.6 %collective-permute-start.12 = (bf16[192,512]{1,0:T(8,128)(2,1)S(1)}, bf16[192,512]{1,0:T(8,128)(2,1)S(1)}, u32[]{:S(2)}, u32[]{:S(2)}) collective-permute-start(bf16[192,512]{1,0:T(8,128)(2,1)S(1)} %get-tuple-element.49.a0), channel_id=1, source_target_pairs={{0,16},{8,24},{16,0},{24,8},{1,17},{9,25},{17,1},{25,9},{2,18},{10... | collective-permute-start | bytes 589832 | tf_op jit(solution)/shard_map/ppermute | solution.py:402
  30.6 4.8 %collective-permute-start.13 = (bf16[192,512]{1,0:T(8,128)(2,1)S(1)}, bf16[192,512]{1,0:T(8,128)(2,1)S(1)}, u32[]{:S(2)}, u32[]{:S(2)}) collective-permute-start(bf16[192,512]{1,0:T(8,128)(2,1)S(1)} %get-tuple-element.49.a0), channel_id=1, source_target_pairs={{0,1},{1,0},{2,3},{3,2},{4,5},{5,4},{6,7},{7,6},{8,9},{9,8},{10,11... | collective-permute-start | bytes 589832 | tf_op jit(solution)/shard_map/ppermute | solution.py:396
  30.8 8.5 %collective-permute-start.17 = (bf16[192,512]{1,0:T(8,128)(2,1)S(1)}, bf16[192,512]{1,0:T(8,128)(2,1)S(1)}, u32[]{:S(2)}, u32[]{:S(2)}) collective-permute-start(bf16[192,512]{1,0:T(8,128)(2,1)S(1)} %get-tuple-element.49.a0), channel_id=1, source_target_pairs={{0,17},{1,16},{2,19},{3,18},{4,21},{5,20},{6,23},{7,22},{8,25},{9,... | collective-permute-start | bytes 589832 | tf_op jit(solution)/shard_map/ppermute | solution.py:411
  35.4 6.5 %collective-permute-start.15 = (bf16[192,512]{1,0:T(8,128)(2,1)S(1)}, bf16[192,512]{1,0:T(8,128)(2,1)S(1)}, u32[]{:S(2)}, u32[]{:S(2)}) collective-permute-start(bf16[192,512]{1,0:T(8,128)(2,1)S(1)} %collective-permute-done.13.a1), channel_id=1, source_target_pairs={{0,8},{8,0},{16,24},{24,16},{1,9},{9,1},{17,25},{25,17},{2,10},{10... | collective-permute-start | bytes 589832 | tf_op jit(solution)/shard_map/ppermute | solution.py:399
  38.8 3.1 %collective-permute-start.14 = (bf16[192,512]{1,0:T(8,128)(2,1)S(1)}, bf16[192,512]{1,0:T(8,128)(2,1)S(1)}, u32[]{:S(2)}, u32[]{:S(2)}) collective-permute-start(bf16[192,512]{1,0:T(8,128)(2,1)S(1)} %get-tuple-element.49.a0), channel_id=1, source_target_pairs={{0,8},{8,0},{16,24},{24,16},{1,9},{9,1},{17,25},{25,17},{2,10},{10... | collective-permute-start | bytes 589832 | tf_op jit(solution)/shard_map/ppermute | solution.py:399
  38.8 3.1 %collective-permute-start.16 = (bf16[192,512]{1,0:T(8,128)(2,1)S(1)}, bf16[192,512]{1,0:T(8,128)(2,1)S(1)}, u32[]{:S(2)}, u32[]{:S(2)}) collective-permute-start(bf16[192,512]{1,0:T(8,128)(2,1)S(1)} %collective-permute-done.12.c0), channel_id=1, source_target_pairs={{0,8},{8,0},{16,24},{24,16},{1,9},{9,1},{17,25},{25,17},{2,10},{10... | collective-permute-start | bytes 589832 | tf_op jit(solution)/shard_map/ppermute | solution.py:399
  39.3 2.7 %collective-permute-start.18 = (bf16[192,512]{1,0:T(8,128)(2,1)S(1)}, bf16[192,512]{1,0:T(8,128)(2,1)S(1)}, u32[]{:S(2)}, u32[]{:S(2)}) collective-permute-start(bf16[192,512]{1,0:T(8,128)(2,1)S(1)} %collective-permute-done.17.c1), channel_id=1, source_target_pairs={{0,8},{8,0},{16,24},{24,16},{1,9},{9,1},{17,25},{25,17},{2,10},{10... | collective-permute-start | bytes 589832 | tf_op jit(solution)/shard_map/ppermute | solution.py:399
  40.9 5.7 %copy-start.3 = (bf16[1,48,1536]{2,1,0:T(8,128)(2,1)S(1)}, bf16[1,48,1536]{2,1,0:T(8,128)(2,1)}, u32[]{:S(2)}) copy-start(bf16[1,48,1536]{2,1,0:T(8,128)(2,1)} %param.10) | copy-start | bytes 442372
  40.9 5.7 %copy-start.6 = (f32[3,1536]{1,0:T(4,128)S(1)}, f32[3,1536]{1,0:T(4,128)}, u32[]{:S(2)}) copy-start(f32[3,1536]{1,0:T(4,128)} %block_in.1) | copy-start | bytes 55300
  40.9 5.7 %copy-start.8 = (f32[1,3,1536]{2,0,1:T(1,128)S(1)}, f32[1,3,1536]{2,0,1:T(1,128)}, u32[]{:S(2)}) copy-start(f32[1,3,1536]{2,0,1:T(1,128)} %param.12) | copy-start | bytes 55300
  40.9 5.7 %copy-start.10 = (f32[1,2,1536]{2,1,0:T(2,128)S(1)}, f32[1,2,1536]{2,1,0:T(2,128)}, u32[]{:S(2)}) copy-start(f32[1,2,1536]{2,1,0:T(2,128)} %param.17) | copy-start | bytes 36868
  43.0 4.5 %collective-permute-start.19 = (bf16[48,256]{1,0:T(8,128)(2,1)S(1)}, bf16[48,256]{1,0:T(8,128)(2,1)S(1)}, u32[]{:S(2)}, u32[]{:S(2)}) collective-permute-start(bf16[48,256]{1,0:T(8,128)(2,1)S(1)} %get-tuple-element.53), channel_id=1, source_target_pairs={{0,6},{1,7},{2,4},{3,5},{4,2},{5,3},{6,0},{7,1},{8,14},{9,15},{10,... | collective-permute-start | bytes 73736 | tf_op jit(solution)/shard_map/ppermute | solution.py:393
  44.2 4.1 %collective-permute-start.20 = (bf16[48,256]{1,0:T(8,128)(2,1)S(1)}, bf16[48,256]{1,0:T(8,128)(2,1)S(1)}, u32[]{:S(2)}, u32[]{:S(2)}) collective-permute-start(bf16[48,256]{1,0:T(8,128)(2,1)S(1)} %get-tuple-element.54), channel_id=1, source_target_pairs={{0,4},{1,5},{2,6},{3,7},{4,0},{5,1},{6,2},{7,3},{8,12},{9,13},{10,... | collective-permute-start | bytes 73736 | tf_op jit(solution)/shard_map/ppermute | solution.py:393
  44.2 4.1 %collective-permute-start.21 = (bf16[48,256]{1,0:T(8,128)(2,1)S(1)}, bf16[48,256]{1,0:T(8,128)(2,1)S(1)}, u32[]{:S(2)}, u32[]{:S(2)}) collective-permute-start(bf16[48,256]{1,0:T(8,128)(2,1)S(1)} %get-tuple-element.55), channel_id=1, source_target_pairs={{0,2},{1,3},{2,0},{3,1},{4,6},{5,7},{6,4},{7,5},{8,10},{9,11},{10,... | collective-permute-start | bytes 73736 | tf_op jit(solution)/shard_map/ppermute | solution.py:393
  46.6 1.7 %copy-start.4 = (bf16[1536,64]{0,1:T(8,128)(2,1)S(1)}, bf16[1536,64]{0,1:T(8,128)(2,1)}, u32[]{:S(2)}) copy-start(bf16[1536,64]{0,1:T(8,128)(2,1)} %param.18) | copy-start | bytes 589828
  46.6 1.7 %copy-start.9 = (f32[1,48,64]{2,1,0:T(8,128)S(1)}, f32[1,48,64]{2,1,0:T(8,128)}, u32[]{:S(2)}) copy-start(f32[1,48,64]{2,1,0:T(8,128)} %param.11) | copy-start | bytes 36868
  49.4 5.3 %collective-permute-start.22 = (f32[1,48,64]{2,1,0:T(8,128)S(1)}, f32[1,48,64]{2,1,0:T(8,128)S(1)}, u32[]{:S(2)}, u32[]{:S(2)}) collective-permute-start(f32[1,48,64]{2,1,0:T(8,128)S(1)} %bitcast.20), channel_id=1, source_target_pairs={{0,24},{8,0},{16,8},{24,16},{1,25},{9,1},{17,9},{25,17},{2,26},{10... | collective-permute-start | bytes 36872 | tf_op jit(solution)/shard_map/ppermute | solution.py:28
  (3 other events, 2.4 us)

commit v5 on v4

--- a/solution.py
+++ b/solution.py
@@ -178,19 +178,6 @@
     modded[...] = modulated(x0, shift_scale)
 
 
-def first_kernel(
-    x1, x2, x3, modded_own, shift_scale, w_own, w_mine, w_last, w_chip, modded, own, other
-):
-    for place, rows in enumerate((x2, x1, x3)):
-        modded[place * TOK_DEV : (place + 1) * TOK_DEV, :] = modulated(rows, shift_scale)
-    modded[3 * TOK_DEV :, :] = modded_own[...]
-    _, _, core, chip = here()
-    own[...] = jnp.dot(modded[...], w_own[...], preferred_element_type=F32).astype(BF16)
-    total = part_product(modded, w_mine, 2 * chip + core)
-    total += part_product(modded, w_last, 4 + core)
-    other[...] = total + part_product(modded, w_chip, 2 * (1 - chip) + core)
-
-
 def part_product(modded, weights, part):
     depth = weights.shape[0]
     at = pl.multiple_of(part * depth, depth)
@@ -198,21 +185,27 @@
 
 
 def project_kernel(
-    w_core, w_core_last, w_core_chip, modded, own_in, other_in,
-    far_out, near_out, keep_out, sums_out, mixed,
-):
+    x1, x2, x3, modded_own, shift_scale, w_own, w_mine, w_last, w_chip,
+    w_core, w_core_last, w_core_chip, far_out, near_out, keep_out, sums_out, modded, mixed,
+):
+    for place, rows in enumerate((x2, x1, x3)):
+        modded[place * TOK_DEV : (place + 1) * TOK_DEV, :] = modulated(rows, shift_scale)
+    modded[3 * TOK_DEV :, :] = modded_own[...]
     line, side, core, chip = here()
-    width = w_core.shape[1]
-    total = other_in[...] + part_product(modded, w_core, 2 * chip + 1 - core)
-    total += part_product(modded, w_core_last, 4 + 1 - core)
+    width = w_own.shape[1]
+    own = jnp.dot(modded[...], w_own[...], preferred_element_type=F32).astype(BF16)
+    total = part_product(modded, w_mine, 2 * chip + core)
+    total += part_product(modded, w_core, 2 * chip + 1 - core)
+    total += part_product(modded, w_chip, 2 * (1 - chip) + core)
     total += part_product(modded, w_core_chip, 2 * (1 - chip) + 1 - core)
-    other = total.astype(BF16)
+    total += part_product(modded, w_last, 4 + core)
+    other = (total + part_product(modded, w_core_last, 5 - core)).astype(BF16)
     mine = pl.multiple_of(side * width, width)
     there = pl.multiple_of((1 - side) * width, width)
     for place, step in enumerate((2, 1, 3, 0)):
         at = pl.multiple_of(jnp.bitwise_xor(line, step) * TOK_DEV, 16)
         rows = slice(place * TOK_DEV, (place + 1) * TOK_DEV)
-        mixed[pl.ds(at, TOK_DEV), pl.ds(mine, width)] = own_in[rows, :]
+        mixed[pl.ds(at, TOK_DEV), pl.ds(mine, width)] = own[rows]
         mixed[pl.ds(at, TOK_DEV), pl.ds(there, width)] = other[rows]
     ones = jnp.ones((16, PAIR), BF16)
     row_id = lax.broadcasted_iota(jnp.int32, (16, ROWS), 0)
@@ -369,7 +362,7 @@
 
 
 def finish_kernel(
-    r3, r2, r1, w_out, base, vectors, w_head, size, latents_in, stream_out, latents_out,
+    r2, r3, r1, w_out, base, vectors, w_head, size, latents_in, stream_out, latents_out,
     latents, arrived,
 ):
     copies = load((latents_in,), (latents,), arrived)
@@ -413,7 +406,7 @@
     rows = stream[0]
     time_rows = time_mod.transpose(1, 0, 2)
     depth = D // 6
-    half_mine = lax.dynamic_slice_in_dim(w_qkv, (slab // 2 * 2 + core) * depth, depth, 0)
+    half_mine = lax.dynamic_slice_in_dim(w_qkv, slab * depth, depth, 0)
     half_last = lax.dynamic_slice_in_dim(w_qkv, (4 + core) * depth, depth, 0)
     w_mine, w_last = across(half_mine), across(half_last)
     late_rows, _ = lax.optimization_barrier((rows, half_mine))
@@ -435,17 +428,15 @@
     w_core_last = cores(w_last)
     w_mine, w_chip = lax.optimization_barrier((w_mine, w_chip))
     w_core, w_core_chip = cores(w_mine), cores(w_chip)
-    width = w_qkv.shape[1]
-    modded, own, other = vmem_call(
-        first_kernel, [((ROWS, D), BF16), ((ROWS, width), BF16), ((ROWS, width), F32)],
-        "first", 1 << 28,
-    )(x1, x2, x3, modded_own, shift_scale, w_qkv, w_mine, w_last, w_chip)
     message = (ROWS + 16, PAIR)
     far, near, keep, sums = vmem_call(
         project_kernel,
         [(message, BF16), (message, BF16), ((ROWS, PAIR), BF16), ((16, PAIR), BF16)],
-        "project", 1 << 28, [pltpu.VMEM((ROWS, 3 * PAIR), BF16)],
-    )(w_core, w_core_last, w_core_chip, modded, own, other)
+        "project", 1 << 28, [pltpu.VMEM((ROWS, D), BF16), pltpu.VMEM((ROWS, 3 * PAIR), BF16)],
+    )(
+        x1, x2, x3, modded_own, shift_scale, w_qkv,
+        w_mine, w_last, w_chip, w_core, w_core_last, w_core_chip,
+    )
     far, last_sums, near = along(2, far), along(3, sums), along(1, near)
     queries, pairs, size = vmem_call(
         rope_kernel,
@@ -466,7 +457,7 @@
         last_attend_kernel, [((TOK_DEV, PAIR), BF16)] * 4, "attend_last", 1 << 27,
         [pltpu.VMEM((ROWS, PAIR), BF16)],
     )(queries, core_pairs, core_side, core_chip, core_both, *now)
-    late = [along(3, part3), along(2, part2), along(1, part1)]
+    late = [along(2, part2), along(3, part3), along(1, part1)]
     loaded = (rows, time_rows, block_mod, head_mod[0])
     base, vectors = vmem_call(
         begin_kernel, [((TOK_DEV, D), F32), ((8, D), F32)], "begin", 1 << 28,

time: 55.5 us -> 54.9 us (0.989)
  starting transfers between devices: 29.9 us -> 28.7 us
  waiting for transfers between devices: 12.4 us -> 13.1 us
    ppermute x9, starting transfers between devices: 13.3 us -> 12 us  [along(): lax.ppermute(value, 'seq', [(i, i ^ 2 * step) for i in range(2 * LINE)])]
    pallas_call x8 -> x7, Pallas kernels: 5.72 us -> 5.58 us  [call(): pl.pallas_call(kernel, out_shape=[jax.ShapeDtypeStruct(shape, dtype) for...]
  transfers between devices with their start and end apart: 23 -> 23, of which waited for: 10 -> 10; matrix products, arithmetic and copies ran while one was open for 3% -> 3% of each run, Pallas kernels for 5% -> 3%
where the time goes in v5:
time: 54.9 us; the launch traced here: 54.7 us
  starting transfers between devices  28.7 us (52%)
  waiting for transfers between devices  13.1 us (24%)
  Pallas kernels  5.58 us (10%)
  local copies, waits for them, and re-layouts  4.26 us (8%)
  between operations  1.65 us (3%)
  other arithmetic  1.3 us (2%)
    ppermute x9, starting transfers between devices, along(): lax.ppermute(value, 'seq', [(i, i ^ 2 * step) for i in range(2 * LINE)])  12 us
    ppermute x7, starting transfers between devices, cores(): return lax.ppermute(value, 'slab', [(i, i ^ 1) for i in range(4)])  8.91 us
    pallas_call x7, Pallas kernels, call(): pl.pallas_call(kernel, out_shape=[jax.ShapeDtypeStruct(shape, dtype) for...  5.58 us
    ppermute x9, waiting for transfers between devices, along(): lax.ppermute(value, 'seq', [(i, i ^ 2 * step) for i in range(2 * LINE)])  5.37 us
    ppermute x1, waiting for transfers between devices, from_behind(): return lax.ppermute(value, axis, pairs)  3.13 us
    unnamed x25, local copies, waits for them, and re-layouts  3.02 us
    ppermute x2, starting transfers between devices, chips(): return lax.ppermute(value, 'slab', [(i, i ^ 2) for i in range(4)])  2.39 us
    ppermute x3, starting transfers between devices, across(): return lax.ppermute(value, 'seq', [(i, i ^ 1) for i in range(2 * LINE)])  2.36 us
  transfers between devices with their start and end apart: 23, of which 10 were waited for; matrix products, arithmetic and copies ran while one was open for 3% of the time, Pallas kernels for 3%

profile of v5, /device:TPU:1, one launch (start us, length us, event | category | flops | bytes accessed | tf_op | source)
XLA Modules:
  0.0 54.7 jit_solution(1224099315724999617)
XLA Ops:
  0.7 1.2 %constant_dynamic-slice_fusion = (bf16[256,384]{1,0:T(8,128)(2,1)S(1)}, bf16[256,384]{1,0:T(8,128)(2,1)S(1)}) fusion(bf16[1536,384]{1,0:T(8,128)(2,1)} %w_own.1, s32[]{:T(128)S(6)} %select_n.19, s32[]{:T(128)S(6)} %select_n.18), kind=kLoop, calls=%fused_computation.9 | loop fusion | bytes 786440 | tf_op jit(solution)/shard_map/dynamic_slice | solution.py:409
  1.8 2.1 %collective-permute-start.4 = (bf16[256,384]{1,0:T(8,128)(2,1)S(1)}, bf16[256,384]{1,0:T(8,128)(2,1)S(1)}, u32[]{:S(2)}, u32[]{:S(2)}) collective-permute-start(bf16[256,384]{1,0:T(8,128)(2,1)S(1)} %get-tuple-element.56), channel_id=1, source_target_pairs={{0,1},{1,0},{2,3},{3,2},{4,5},{5,4},{6,7},{7,6},{8,9},{9,8},{10,11... | collective-permute-start | bytes 589832 | tf_op jit(solution)/shard_map/ppermute | solution.py:389
  3.9 1.3 %collective-permute-start = (bf16[48,1536]{1,0:T(8,128)(2,1)}, bf16[48,1536]{1,0:T(8,128)(2,1)S(1)}, u32[]{:S(2)}, u32[]{:S(2)}) collective-permute-start(bf16[48,1536]{1,0:T(8,128)(2,1)} %bitcast.10), channel_id=1, source_target_pairs={{0,2},{1,3},{2,0},{3,1},{4,6},{5,7},{6,4},{7,5},{8,10},{9,11},{10,... | collective-permute-start | bytes 442376 | tf_op jit(solution)/shard_map/ppermute | solution.py:386
  5.2 2.3 %collective-permute-start.1 = (bf16[48,1536]{1,0:T(8,128)(2,1)}, bf16[48,1536]{1,0:T(8,128)(2,1)S(1)}, u32[]{:S(2)}, u32[]{:S(2)}) collective-permute-start(bf16[48,1536]{1,0:T(8,128)(2,1)} %bitcast.11), channel_id=1, source_target_pairs={{0,4},{1,5},{2,6},{3,7},{4,0},{5,1},{6,2},{7,3},{8,12},{9,13},{10,... | collective-permute-start | bytes 442376 | tf_op jit(solution)/shard_map/ppermute | solution.py:386
  7.8 0.8 %collective-permute-done.4.w_mine = bf16[256,384]{1,0:T(8,128)(2,1)S(1)} collective-permute-done((bf16[256,384]{1,0:T(8,128)(2,1)S(1)}, bf16[256,384]{1,0:T(8,128)(2,1)S(1)}, u32[]{:S(2)}, u32[]{:S(2)}) %collective-permute-start.4) | collective-permute-done | bytes 196640 | tf_op jit(solution)/shard_map/ppermute | solution.py:389
  8.6 1.1 %collective-permute-start.5 = (bf16[256,384]{1,0:T(8,128)(2,1)S(1)}, bf16[256,384]{1,0:T(8,128)(2,1)S(1)}, u32[]{:S(2)}, u32[]{:S(2)}) collective-permute-start(bf16[256,384]{1,0:T(8,128)(2,1)S(1)} %collective-permute-done.4.w_mine), channel_id=1, source_target_pairs={{0,16},{8,24},{16,0},{24,8},{1,17},{9,25},{17,1},{25,9},{2,18},{10... | collective-permute-start | bytes 589832 | tf_op jit(solution)/shard_map/ppermute | solution.py:395
  9.9 0.9 %copy-done.2 = bf16[1,48,1536]{2,1,0:T(8,128)(2,1)S(1)} copy-done((bf16[1,48,1536]{2,1,0:T(8,128)(2,1)S(1)}, bf16[1,48,1536]{2,1,0:T(8,128)(2,1)}, u32[]{:S(2)}) %copy-start.2) | copy-done | bytes 147480
  10.8 0.7 %copy-done.5 = f32[3,1536]{1,0:T(4,128)S(1)} copy-done((f32[3,1536]{1,0:T(4,128)S(1)}, f32[3,1536]{1,0:T(4,128)}, u32[]{:S(2)}) %copy-start.5) | copy-done | bytes 18456
  11.5 0.7 %copy-done.7 = f32[1,3,1536]{2,0,1:T(1,128)S(1)} copy-done((f32[1,3,1536]{2,0,1:T(1,128)S(1)}, f32[1,3,1536]{2,0,1:T(1,128)}, u32[]{:S(2)}) %copy-start.7) | copy-done | bytes 18456
  12.5 2.5 %collective-permute-start.7 = (bf16[256,384]{1,0:T(8,128)(2,1)S(1)}, bf16[256,384]{1,0:T(8,128)(2,1)S(1)}, u32[]{:S(2)}, u32[]{:S(2)}) collective-permute-start(bf16[256,384]{1,0:T(8,128)(2,1)S(1)} %collective-permute-done.3.w_last), channel_id=1, source_target_pairs={{0,8},{8,0},{16,24},{24,16},{1,9},{9,1},{17,25},{25,17},{2,10},{10... | collective-permute-start | bytes 589832 | tf_op jit(solution)/shard_map/ppermute | solution.py:392
  15.0 0.9 %collective-permute-start.6 = (bf16[256,384]{1,0:T(8,128)(2,1)S(1)}, bf16[256,384]{1,0:T(8,128)(2,1)S(1)}, u32[]{:S(2)}, u32[]{:S(2)}) collective-permute-start(bf16[256,384]{1,0:T(8,128)(2,1)S(1)} %collective-permute-done.4.w_mine), channel_id=1, source_target_pairs={{0,8},{8,0},{16,24},{24,16},{1,9},{9,1},{17,25},{25,17},{2,10},{10... | collective-permute-start | bytes 589832 | tf_op jit(solution)/shard_map/ppermute | solution.py:392
  17.3 1.5 %project.1 = (bf16[208,256]{1,0:T(8,128)(2,1)S(1)}, bf16[208,256]{1,0:T(8,128)(2,1)S(1)}, bf16[192,256]{1,0:T(8,128)(2,1)S(1)}, bf16[16,256]{1,0:T(8,128)(2,1)S(1)}) custom-call(bf16[48,1536]{1,0:T(8,128)(2,1)S(1)} %collective-permute-done.x1, bf16[48,1536]{1,0:T(8,128)(2,1)S(1)} %collective-permute-done.1.x2, ...), custom_call_target="tpu_custom_call" | custom-call | flops 268435456 | bytes 1048576 | tf_op jit(solution)/shard_map/project/pallas_call | solution.py:148
  18.8 4.4 %collective-permute-start.10 = (bf16[208,256]{1,0:T(8,128)(2,1)S(1)}, bf16[208,256]{1,0:T(8,128)(2,1)S(1)}, u32[]{:S(2)}, u32[]{:S(2)}) collective-permute-start(bf16[208,256]{1,0:T(8,128)(2,1)S(1)} %get-tuple-element.37), channel_id=1, source_target_pairs={{0,4},{1,5},{2,6},{3,7},{4,0},{5,1},{6,2},{7,3},{8,12},{9,13},{10,... | collective-permute-start | bytes 319496 | tf_op jit(solution)/shard_map/ppermute | solution.py:386
  23.2 1.3 %collective-permute-start.11 = (bf16[16,256]{1,0:T(8,128)(2,1)S(1)}, bf16[16,256]{1,0:T(8,128)(2,1)S(1)}, u32[]{:S(2)}, u32[]{:S(2)}) collective-permute-start(bf16[16,256]{1,0:T(8,128)(2,1)S(1)} %get-tuple-element.38.own_sums), channel_id=1, source_target_pairs={{0,6},{1,7},{2,4},{3,5},{4,2},{5,3},{6,0},{7,1},{8,14},{9,15},{10,... | collective-permute-start | bytes 24584 | tf_op jit(solution)/shard_map/ppermute | solution.py:386
  25.4 2.3 %collective-permute-done.11.last_sums = bf16[16,256]{1,0:T(8,128)(2,1)S(1)} collective-permute-done((bf16[16,256]{1,0:T(8,128)(2,1)S(1)}, bf16[16,256]{1,0:T(8,128)(2,1)S(1)}, u32[]{:S(2)}, u32[]{:S(2)}) %collective-permute-start.11) | collective-permute-done | bytes 8224 | tf_op jit(solution)/shard_map/ppermute | solution.py:386
  27.7 1.1 %collective-permute-done.9.near = bf16[208,256]{1,0:T(8,128)(2,1)S(1)} collective-permute-done((bf16[208,256]{1,0:T(8,128)(2,1)S(1)}, bf16[208,256]{1,0:T(8,128)(2,1)S(1)}, u32[]{:S(2)}, u32[]{:S(2)}) %collective-permute-start.9) | collective-permute-done | bytes 106528 | tf_op jit(solution)/shard_map/ppermute | solution.py:386
  29.1 1.3 %collective-permute-start.12 = (bf16[192,512]{1,0:T(8,128)(2,1)S(1)}, bf16[192,512]{1,0:T(8,128)(2,1)S(1)}, u32[]{:S(2)}, u32[]{:S(2)}) collective-permute-start(bf16[192,512]{1,0:T(8,128)(2,1)S(1)} %get-tuple-element.43.a0), channel_id=1, source_target_pairs={{0,16},{8,24},{16,0},{24,8},{1,17},{9,25},{17,1},{25,9},{2,18},{10... | collective-permute-start | bytes 589832 | tf_op jit(solution)/shard_map/ppermute | solution.py:395
  30.4 1.4 %collective-permute-start.17 = (bf16[192,512]{1,0:T(8,128)(2,1)S(1)}, bf16[192,512]{1,0:T(8,128)(2,1)S(1)}, u32[]{:S(2)}, u32[]{:S(2)}) collective-permute-start(bf16[192,512]{1,0:T(8,128)(2,1)S(1)} %get-tuple-element.43.a0), channel_id=1, source_target_pairs={{0,17},{1,16},{2,19},{3,18},{4,21},{5,20},{6,23},{7,22},{8,25},{9,... | collective-permute-start | bytes 589832 | tf_op jit(solution)/shard_map/ppermute | solution.py:404
  31.8 1.9 %collective-permute-done.12.c0 = bf16[192,512]{1,0:T(8,128)(2,1)S(1)} collective-permute-done((bf16[192,512]{1,0:T(8,128)(2,1)S(1)}, bf16[192,512]{1,0:T(8,128)(2,1)S(1)}, u32[]{:S(2)}, u32[]{:S(2)}) %collective-permute-start.12) | collective-permute-done | bytes 196640 | tf_op jit(solution)/shard_map/ppermute | solution.py:395
  33.7 1.5 %collective-permute-done.13.a1 = bf16[192,512]{1,0:T(8,128)(2,1)S(1)} collective-permute-done((bf16[192,512]{1,0:T(8,128)(2,1)S(1)}, bf16[192,512]{1,0:T(8,128)(2,1)S(1)}, u32[]{:S(2)}, u32[]{:S(2)}) %collective-permute-start.13) | collective-permute-done | bytes 196640 | tf_op jit(solution)/shard_map/ppermute | solution.py:389
  35.2 3.4 %collective-permute-start.15 = (bf16[192,512]{1,0:T(8,128)(2,1)S(1)}, bf16[192,512]{1,0:T(8,128)(2,1)S(1)}, u32[]{:S(2)}, u32[]{:S(2)}) collective-permute-start(bf16[192,512]{1,0:T(8,128)(2,1)S(1)} %collective-permute-done.13.a1), channel_id=1, source_target_pairs={{0,8},{8,0},{16,24},{24,16},{1,9},{9,1},{17,25},{25,17},{2,10},{10... | collective-permute-start | bytes 589832 | tf_op jit(solution)/shard_map/ppermute | solution.py:392
  39.1 1.6 %collective-permute-start.18 = (bf16[192,512]{1,0:T(8,128)(2,1)S(1)}, bf16[192,512]{1,0:T(8,128)(2,1)S(1)}, u32[]{:S(2)}, u32[]{:S(2)}) collective-permute-start(bf16[192,512]{1,0:T(8,128)(2,1)S(1)} %collective-permute-done.17.c1), channel_id=1, source_target_pairs={{0,8},{8,0},{16,24},{24,16},{1,9},{9,1},{17,25},{25,17},{2,10},{10... | collective-permute-start | bytes 589832 | tf_op jit(solution)/shard_map/ppermute | solution.py:392
  40.7 1.0 %attend_first.1 = (f32[2,192,256]{2,1,0:T(8,128)S(1)}, f32[2,192,128]{2,1,0:T(8,128)S(1)}) custom-call(bf16[192,256]{1,0:T(8,128)(2,1)S(1)} %get-tuple-element.40.queries, bf16[192,512]{1,0:T(8,128)(2,1)S(1)} %collective-permute-done.12.c0, bf16[192,512]{1,0:T(8,128)(2,1)S(1)} %collective-permute-done.17.c1, bf16[192,512]{1,0:T(8,128)(2,1)S(1)} %get-tuple-element.43.a0, ...), custom_call_target="tpu_custom_call" | custom-call | flops 134217728 | bytes 1048576 | tf_op jit(solution)/shard_map/attend_first/pallas_call | solution.py:148
  41.8 1.0 %attend_last.1 = (bf16[48,256]{1,0:T(8,128)(2,1)S(1)}, bf16[48,256]{1,0:T(8,128)(2,1)S(1)}, bf16[48,256]{1,0:T(8,128)(2,1)S(1)}, bf16[48,256]{1,0:T(8,128)(2,1)S(1)}) custom-call(bf16[192,256]{1,0:T(8,128)(2,1)S(1)} %get-tuple-element.40.queries, bf16[192,512]{1,0:T(8,128)(2,1)S(1)} %collective-permute-done.14.b0, ...), custom_call_target="tpu_custom_call" | custom-call | flops 134217728 | bytes 1048576 | tf_op jit(solution)/shard_map/attend_last/pallas_call | solution.py:148
  42.9 1.5 %collective-permute-start.20 = (bf16[48,256]{1,0:T(8,128)(2,1)S(1)}, bf16[48,256]{1,0:T(8,128)(2,1)S(1)}, u32[]{:S(2)}, u32[]{:S(2)}) collective-permute-start(bf16[48,256]{1,0:T(8,128)(2,1)S(1)} %get-tuple-element.48), channel_id=1, source_target_pairs={{0,6},{1,7},{2,4},{3,5},{4,2},{5,3},{6,0},{7,1},{8,14},{9,15},{10,... | collective-permute-start | bytes 73736 | tf_op jit(solution)/shard_map/ppermute | solution.py:386
  44.4 1.1 %collective-permute-start.21 = (bf16[48,256]{1,0:T(8,128)(2,1)S(1)}, bf16[48,256]{1,0:T(8,128)(2,1)S(1)}, u32[]{:S(2)}, u32[]{:S(2)}) collective-permute-start(bf16[48,256]{1,0:T(8,128)(2,1)S(1)} %get-tuple-element.49), channel_id=1, source_target_pairs={{0,2},{1,3},{2,0},{3,1},{4,6},{5,7},{6,4},{7,5},{8,10},{9,11},{10,... | collective-permute-start | bytes 73736 | tf_op jit(solution)/shard_map/ppermute | solution.py:386
  46.7 0.9 %collective-permute-done.20.r3 = bf16[48,256]{1,0:T(8,128)(2,1)S(1)} collective-permute-done((bf16[48,256]{1,0:T(8,128)(2,1)S(1)}, bf16[48,256]{1,0:T(8,128)(2,1)S(1)}, u32[]{:S(2)}, u32[]{:S(2)}) %collective-permute-start.20) | collective-permute-done | bytes 24608 | tf_op jit(solution)/shard_map/ppermute | solution.py:386
  47.6 1.0 %finish.1 = (f32[48,1536]{1,0:T(8,128)S(1)}, f32[48,64]{1,0:T(8,128)S(1)}) custom-call(bf16[48,256]{1,0:T(8,128)(2,1)S(1)} %collective-permute-done.19.r2, bf16[48,256]{1,0:T(8,128)(2,1)S(1)} %collective-permute-done.20.r3, bf16[48,256]{1,0:T(8,128)(2,1)S(1)} %collective-permute-done.21.r1, bf16[1024,1536]{1,0:T(8,128)(2,1)S(1)} %copy-done, ...), custom_call_target="tpu_custom_call" | custom-call | flops 268435456 | bytes 1048576 | tf_op jit(solution)/shard_map/finish/pallas_call | solution.py:148
  48.6 1.7 %collective-permute-start.22 = (f32[1,48,64]{2,1,0:T(8,128)S(1)}, f32[1,48,64]{2,1,0:T(8,128)S(1)}, u32[]{:S(2)}, u32[]{:S(2)}) collective-permute-start(f32[1,48,64]{2,1,0:T(8,128)S(1)} %bitcast.20), channel_id=1, source_target_pairs={{0,24},{8,0},{16,8},{24,16},{1,25},{9,1},{17,9},{25,17},{2,26},{10... | collective-permute-start | bytes 36872 | tf_op jit(solution)/shard_map/ppermute | solution.py:28
  50.2 0.7 %convert_bitcast_fusion = bf16[1,48,1536]{2,1,0:T(8,128)(2,1)} fusion(f32[48,1536]{1,0:T(8,128)S(1)} %get-tuple-element.54), kind=kLoop, calls=%fused_computation | loop fusion | flops 73728 | bytes 442368 | tf_op jit(solution)/shard_map/broadcast_in_dim | solution.py:471
  50.9 3.1 %collective-permute-done.22 = f32[1,48,64]{2,1,0:T(8,128)S(1)} collective-permute-done((f32[1,48,64]{2,1,0:T(8,128)S(1)}, f32[1,48,64]{2,1,0:T(8,128)S(1)}, u32[]{:S(2)}, u32[]{:S(2)}) %collective-permute-start.22) | collective-permute-done | bytes 12320 | tf_op jit(solution)/shard_map/ppermute | solution.py:28
  54.0 0.6 %copy.14 = f32[1,48,64]{2,1,0:T(8,128)} copy(f32[1,48,64]{2,1,0:T(8,128)S(1)} %collective-permute-done.22) | data formatting | bytes 24576
  (54 shorter events, 4.3 us)
Async XLA Ops:
  0.6 16.7 %copy-start.1 = (bf16[1536,384]{1,0:T(8,128)(2,1)S(1)}, bf16[1536,384]{1,0:T(8,128)(2,1)}, u32[]{:S(2)}) copy-start(bf16[1536,384]{1,0:T(8,128)(2,1)} %w_own.1) | copy-start | bytes 3538948
  1.8 6.8 %collective-permute-start.4 = (bf16[256,384]{1,0:T(8,128)(2,1)S(1)}, bf16[256,384]{1,0:T(8,128)(2,1)S(1)}, u32[]{:S(2)}, u32[]{:S(2)}) collective-permute-start(bf16[256,384]{1,0:T(8,128)(2,1)S(1)} %get-tuple-element.56), channel_id=1, source_target_pairs={{0,1},{1,0},{2,3},{3,2},{4,5},{5,4},{6,7},{7,6},{8,9},{9,8},{10,11... | collective-permute-start | bytes 589832 | tf_op jit(solution)/shard_map/ppermute | solution.py:389
  3.9 11.9 %collective-permute-start = (bf16[48,1536]{1,0:T(8,128)(2,1)}, bf16[48,1536]{1,0:T(8,128)(2,1)S(1)}, u32[]{:S(2)}, u32[]{:S(2)}) collective-permute-start(bf16[48,1536]{1,0:T(8,128)(2,1)} %bitcast.10), channel_id=1, source_target_pairs={{0,2},{1,3},{2,0},{3,1},{4,6},{5,7},{6,4},{7,5},{8,10},{9,11},{10,... | collective-permute-start | bytes 442376 | tf_op jit(solution)/shard_map/ppermute | solution.py:386
  5.2 11.1 %collective-permute-start.1 = (bf16[48,1536]{1,0:T(8,128)(2,1)}, bf16[48,1536]{1,0:T(8,128)(2,1)S(1)}, u32[]{:S(2)}, u32[]{:S(2)}) collective-permute-start(bf16[48,1536]{1,0:T(8,128)(2,1)} %bitcast.11), channel_id=1, source_target_pairs={{0,4},{1,5},{2,6},{3,7},{4,0},{5,1},{6,2},{7,3},{8,12},{9,13},{10,... | collective-permute-start | bytes 442376 | tf_op jit(solution)/shard_map/ppermute | solution.py:386
  7.6 9.4 %collective-permute-start.2 = (bf16[48,1536]{1,0:T(8,128)(2,1)}, bf16[48,1536]{1,0:T(8,128)(2,1)S(1)}, u32[]{:S(2)}, u32[]{:S(2)}) collective-permute-start(bf16[48,1536]{1,0:T(8,128)(2,1)} %bitcast.12), channel_id=1, source_target_pairs={{0,6},{1,7},{2,4},{3,5},{4,2},{5,3},{6,0},{7,1},{8,14},{9,15},{10,... | collective-permute-start | bytes 442376 | tf_op jit(solution)/shard_map/ppermute | solution.py:386
  7.6 4.9 %collective-permute-start.3 = (bf16[256,384]{1,0:T(8,128)(2,1)S(1)}, bf16[256,384]{1,0:T(8,128)(2,1)S(1)}, u32[]{:S(2)}, u32[]{:S(2)}) collective-permute-start(bf16[256,384]{1,0:T(8,128)(2,1)S(1)} %get-tuple-element.57), channel_id=1, source_target_pairs={{0,1},{1,0},{2,3},{3,2},{4,5},{5,4},{6,7},{7,6},{8,9},{9,8},{10,11... | collective-permute-start | bytes 589832 | tf_op jit(solution)/shard_map/ppermute | solution.py:389
  8.6 6.4 %collective-permute-start.5 = (bf16[256,384]{1,0:T(8,128)(2,1)S(1)}, bf16[256,384]{1,0:T(8,128)(2,1)S(1)}, u32[]{:S(2)}, u32[]{:S(2)}) collective-permute-start(bf16[256,384]{1,0:T(8,128)(2,1)S(1)} %collective-permute-done.4.w_mine), channel_id=1, source_target_pairs={{0,16},{8,24},{16,0},{24,8},{1,17},{9,25},{17,1},{25,9},{2,18},{10... | collective-permute-start | bytes 589832 | tf_op jit(solution)/shard_map/ppermute | solution.py:395
  12.5 4.5 %collective-permute-start.7 = (bf16[256,384]{1,0:T(8,128)(2,1)S(1)}, bf16[256,384]{1,0:T(8,128)(2,1)S(1)}, u32[]{:S(2)}, u32[]{:S(2)}) collective-permute-start(bf16[256,384]{1,0:T(8,128)(2,1)S(1)} %collective-permute-done.3.w_last), channel_id=1, source_target_pairs={{0,8},{8,0},{16,24},{24,16},{1,9},{9,1},{17,25},{25,17},{2,10},{10... | collective-permute-start | bytes 589832 | tf_op jit(solution)/shard_map/ppermute | solution.py:392
  15.0 2.0 %collective-permute-start.6 = (bf16[256,384]{1,0:T(8,128)(2,1)S(1)}, bf16[256,384]{1,0:T(8,128)(2,1)S(1)}, u32[]{:S(2)}, u32[]{:S(2)}) collective-permute-start(bf16[256,384]{1,0:T(8,128)(2,1)S(1)} %collective-permute-done.4.w_mine), channel_id=1, source_target_pairs={{0,8},{8,0},{16,24},{24,16},{1,9},{9,1},{17,25},{25,17},{2,10},{10... | collective-permute-start | bytes 589832 | tf_op jit(solution)/shard_map/ppermute | solution.py:392
  15.9 1.4 %collective-permute-start.8 = (bf16[256,384]{1,0:T(8,128)(2,1)S(1)}, bf16[256,384]{1,0:T(8,128)(2,1)S(1)}, u32[]{:S(2)}, u32[]{:S(2)}) collective-permute-start(bf16[256,384]{1,0:T(8,128)(2,1)S(1)} %collective-permute-done.5.w_chip), channel_id=1, source_target_pairs={{0,8},{8,0},{16,24},{24,16},{1,9},{9,1},{17,25},{25,17},{2,10},{10... | collective-permute-start | bytes 589832 | tf_op jit(solution)/shard_map/ppermute | solution.py:392
  16.3 12.5 %copy-start.11 = (f32[2,1024]{1,0:T(2,128)S(1)}, f32[2,1024]{1,0:T(2,128)}, u32[]{:S(2)}) copy-start(f32[2,1024]{1,0:T(2,128)} %gains.1) | copy-start | bytes 24580
  18.8 8.9 %collective-permute-start.10 = (bf16[208,256]{1,0:T(8,128)(2,1)S(1)}, bf16[208,256]{1,0:T(8,128)(2,1)S(1)}, u32[]{:S(2)}, u32[]{:S(2)}) collective-permute-start(bf16[208,256]{1,0:T(8,128)(2,1)S(1)} %get-tuple-element.37), channel_id=1, source_target_pairs={{0,4},{1,5},{2,6},{3,7},{4,0},{5,1},{6,2},{7,3},{8,12},{9,13},{10,... | collective-permute-start | bytes 319496 | tf_op jit(solution)/shard_map/ppermute | solution.py:386
  23.2 5.5 %collective-permute-start.9 = (bf16[208,256]{1,0:T(8,128)(2,1)S(1)}, bf16[208,256]{1,0:T(8,128)(2,1)S(1)}, u32[]{:S(2)}, u32[]{:S(2)}) collective-permute-start(bf16[208,256]{1,0:T(8,128)(2,1)S(1)} %get-tuple-element.36), channel_id=1, source_target_pairs={{0,2},{1,3},{2,0},{3,1},{4,6},{5,7},{6,4},{7,5},{8,10},{9,11},{10,... | collective-permute-start | bytes 319496 | tf_op jit(solution)/shard_map/ppermute | solution.py:386
  23.2 4.5 %collective-permute-start.11 = (bf16[16,256]{1,0:T(8,128)(2,1)S(1)}, bf16[16,256]{1,0:T(8,128)(2,1)S(1)}, u32[]{:S(2)}, u32[]{:S(2)}) collective-permute-start(bf16[16,256]{1,0:T(8,128)(2,1)S(1)} %get-tuple-element.38.own_sums), channel_id=1, source_target_pairs={{0,6},{1,7},{2,4},{3,5},{4,2},{5,3},{6,0},{7,1},{8,14},{9,15},{10,... | collective-permute-start | bytes 24584 | tf_op jit(solution)/shard_map/ppermute | solution.py:386
  24.5 21.0 %copy-start = (bf16[1024,1536]{1,0:T(8,128)(2,1)S(1)}, bf16[1024,1536]{1,0:T(8,128)(2,1)}, u32[]{:S(2)}) copy-start(bf16[1024,1536]{1,0:T(8,128)(2,1)} %w_out.3) | copy-start | bytes 9437188
  29.1 4.6 %collective-permute-start.12 = (bf16[192,512]{1,0:T(8,128)(2,1)S(1)}, bf16[192,512]{1,0:T(8,128)(2,1)S(1)}, u32[]{:S(2)}, u32[]{:S(2)}) collective-permute-start(bf16[192,512]{1,0:T(8,128)(2,1)S(1)} %get-tuple-element.43.a0), channel_id=1, source_target_pairs={{0,16},{8,24},{16,0},{24,8},{1,17},{9,25},{17,1},{25,9},{2,18},{10... | collective-permute-start | bytes 589832 | tf_op jit(solution)/shard_map/ppermute | solution.py:395
  30.4 4.8 %collective-permute-start.13 = (bf16[192,512]{1,0:T(8,128)(2,1)S(1)}, bf16[192,512]{1,0:T(8,128)(2,1)S(1)}, u32[]{:S(2)}, u32[]{:S(2)}) collective-permute-start(bf16[192,512]{1,0:T(8,128)(2,1)S(1)} %get-tuple-element.43.a0), channel_id=1, source_target_pairs={{0,1},{1,0},{2,3},{3,2},{4,5},{5,4},{6,7},{7,6},{8,9},{9,8},{10,11... | collective-permute-start | bytes 589832 | tf_op jit(solution)/shard_map/ppermute | solution.py:389
  30.4 8.7 %collective-permute-start.17 = (bf16[192,512]{1,0:T(8,128)(2,1)S(1)}, bf16[192,512]{1,0:T(8,128)(2,1)S(1)}, u32[]{:S(2)}, u32[]{:S(2)}) collective-permute-start(bf16[192,512]{1,0:T(8,128)(2,1)S(1)} %get-tuple-element.43.a0), channel_id=1, source_target_pairs={{0,17},{1,16},{2,19},{3,18},{4,21},{5,20},{6,23},{7,22},{8,25},{9,... | collective-permute-start | bytes 589832 | tf_op jit(solution)/shard_map/ppermute | solution.py:404
  35.2 6.5 %collective-permute-start.15 = (bf16[192,512]{1,0:T(8,128)(2,1)S(1)}, bf16[192,512]{1,0:T(8,128)(2,1)S(1)}, u32[]{:S(2)}, u32[]{:S(2)}) collective-permute-start(bf16[192,512]{1,0:T(8,128)(2,1)S(1)} %collective-permute-done.13.a1), channel_id=1, source_target_pairs={{0,8},{8,0},{16,24},{24,16},{1,9},{9,1},{17,25},{25,17},{2,10},{10... | collective-permute-start | bytes 589832 | tf_op jit(solution)/shard_map/ppermute | solution.py:392
  38.6 3.1 %collective-permute-start.14 = (bf16[192,512]{1,0:T(8,128)(2,1)S(1)}, bf16[192,512]{1,0:T(8,128)(2,1)S(1)}, u32[]{:S(2)}, u32[]{:S(2)}) collective-permute-start(bf16[192,512]{1,0:T(8,128)(2,1)S(1)} %get-tuple-element.43.a0), channel_id=1, source_target_pairs={{0,8},{8,0},{16,24},{24,16},{1,9},{9,1},{17,25},{25,17},{2,10},{10... | collective-permute-start | bytes 589832 | tf_op jit(solution)/shard_map/ppermute | solution.py:392
  38.6 3.1 %collective-permute-start.16 = (bf16[192,512]{1,0:T(8,128)(2,1)S(1)}, bf16[192,512]{1,0:T(8,128)(2,1)S(1)}, u32[]{:S(2)}, u32[]{:S(2)}) collective-permute-start(bf16[192,512]{1,0:T(8,128)(2,1)S(1)} %collective-permute-done.12.c0), channel_id=1, source_target_pairs={{0,8},{8,0},{16,24},{24,16},{1,9},{9,1},{17,25},{25,17},{2,10},{10... | collective-permute-start | bytes 589832 | tf_op jit(solution)/shard_map/ppermute | solution.py:392
  39.1 2.7 %collective-permute-start.18 = (bf16[192,512]{1,0:T(8,128)(2,1)S(1)}, bf16[192,512]{1,0:T(8,128)(2,1)S(1)}, u32[]{:S(2)}, u32[]{:S(2)}) collective-permute-start(bf16[192,512]{1,0:T(8,128)(2,1)S(1)} %collective-permute-done.17.c1), channel_id=1, source_target_pairs={{0,8},{8,0},{16,24},{24,16},{1,9},{9,1},{17,25},{25,17},{2,10},{10... | collective-permute-start | bytes 589832 | tf_op jit(solution)/shard_map/ppermute | solution.py:392
  40.7 4.8 %copy-start.3 = (bf16[1,48,1536]{2,1,0:T(8,128)(2,1)S(1)}, bf16[1,48,1536]{2,1,0:T(8,128)(2,1)}, u32[]{:S(2)}) copy-start(bf16[1,48,1536]{2,1,0:T(8,128)(2,1)} %param.10) | copy-start | bytes 442372
  40.7 4.8 %copy-start.6 = (f32[3,1536]{1,0:T(4,128)S(1)}, f32[3,1536]{1,0:T(4,128)}, u32[]{:S(2)}) copy-start(f32[3,1536]{1,0:T(4,128)} %block_in.1) | copy-start | bytes 55300
  40.7 4.8 %copy-start.8 = (f32[1,3,1536]{2,0,1:T(1,128)S(1)}, f32[1,3,1536]{2,0,1:T(1,128)}, u32[]{:S(2)}) copy-start(f32[1,3,1536]{2,0,1:T(1,128)} %param.12) | copy-start | bytes 55300
  40.7 4.8 %copy-start.10 = (f32[1,2,1536]{2,1,0:T(2,128)S(1)}, f32[1,2,1536]{2,1,0:T(2,128)}, u32[]{:S(2)}) copy-start(f32[1,2,1536]{2,1,0:T(2,128)} %param.17) | copy-start | bytes 36868
  42.8 3.9 %collective-permute-start.19 = (bf16[48,256]{1,0:T(8,128)(2,1)S(1)}, bf16[48,256]{1,0:T(8,128)(2,1)S(1)}, u32[]{:S(2)}, u32[]{:S(2)}) collective-permute-start(bf16[48,256]{1,0:T(8,128)(2,1)S(1)} %get-tuple-element.47), channel_id=1, source_target_pairs={{0,4},{1,5},{2,6},{3,7},{4,0},{5,1},{6,2},{7,3},{8,12},{9,13},{10,... | collective-permute-start | bytes 73736 | tf_op jit(solution)/shard_map/ppermute | solution.py:386
  42.9 4.7 %collective-permute-start.20 = (bf16[48,256]{1,0:T(8,128)(2,1)S(1)}, bf16[48,256]{1,0:T(8,128)(2,1)S(1)}, u32[]{:S(2)}, u32[]{:S(2)}) collective-permute-start(bf16[48,256]{1,0:T(8,128)(2,1)S(1)} %get-tuple-element.48), channel_id=1, source_target_pairs={{0,6},{1,7},{2,4},{3,5},{4,2},{5,3},{6,0},{7,1},{8,14},{9,15},{10,... | collective-permute-start | bytes 73736 | tf_op jit(solution)/shard_map/ppermute | solution.py:386
  44.4 3.2 %collective-permute-start.21 = (bf16[48,256]{1,0:T(8,128)(2,1)S(1)}, bf16[48,256]{1,0:T(8,128)(2,1)S(1)}, u32[]{:S(2)}, u32[]{:S(2)}) collective-permute-start(bf16[48,256]{1,0:T(8,128)(2,1)S(1)} %get-tuple-element.49), channel_id=1, source_target_pairs={{0,2},{1,3},{2,0},{3,1},{4,6},{5,7},{6,4},{7,5},{8,10},{9,11},{10,... | collective-permute-start | bytes 73736 | tf_op jit(solution)/shard_map/ppermute | solution.py:386
  45.5 2.0 %copy-start.4 = (bf16[1536,64]{0,1:T(8,128)(2,1)S(1)}, bf16[1536,64]{0,1:T(8,128)(2,1)}, u32[]{:S(2)}) copy-start(bf16[1536,64]{0,1:T(8,128)(2,1)} %param.18) | copy-start | bytes 589828
  45.5 2.0 %copy-start.9 = (f32[1,48,64]{2,1,0:T(8,128)S(1)}, f32[1,48,64]{2,1,0:T(8,128)}, u32[]{:S(2)}) copy-start(f32[1,48,64]{2,1,0:T(8,128)} %param.11) | copy-start | bytes 36868
  48.6 5.5 %collective-permute-start.22 = (f32[1,48,64]{2,1,0:T(8,128)S(1)}, f32[1,48,64]{2,1,0:T(8,128)S(1)}, u32[]{:S(2)}, u32[]{:S(2)}) collective-permute-start(f32[1,48,64]{2,1,0:T(8,128)S(1)} %bitcast.20), channel_id=1, source_target_pairs={{0,24},{8,0},{16,8},{24,16},{1,25},{9,1},{17,9},{25,17},{2,26},{10... | collective-permute-start | bytes 36872 | tf_op jit(solution)/shard_map/ppermute | solution.py:28
  (3 other events, 2.4 us)

commit v6 on v5

--- a/solution.py
+++ b/solution.py
@@ -20,6 +20,7 @@
 BF16 = jnp.bfloat16
 F32 = jnp.float32
 VMEM_LIMIT = 40 * 1024 * 1024
+EXPONENT = HEAD_DIM ** (-0.5) * 1.4426950408889634
 
 
 def from_behind(value, axis, steps):
@@ -246,8 +247,25 @@
     return sigma(level - 1) - sigma(level)
 
 
-def rope_kernel(
-    near, far, last_sums, keep, own_sums, gains, cosines, sines, levels, q_out, kv_out, size, units
+def row_scale(pieces, kind):
+    wanted = lax.broadcasted_iota(jnp.int32, (16, 1), 0) // 3 == kind
+    total = jnp.zeros((1, PAIR), F32)
+    for piece in pieces:
+        total += jnp.sum(jnp.where(wanted, piece, 0.0), axis=0, keepdims=True)
+    scale = lax.rsqrt(total * (1.0 / ATT) + 1e-06)
+    return jnp.transpose(jnp.broadcast_to(scale, (HEAD_DIM, PAIR)))[:ROWS]
+
+
+def turn(values, scale, gains, kind, head, cos, sin):
+    columns = slice(head * HEAD_DIM, (head + 1) * HEAD_DIM)
+    at = pl.multiple_of(here()[0] * PAIR + head * HEAD_DIM, HEAD_DIM)
+    scaled = values[:, columns] * scale * gains[kind : kind + 1, pl.ds(at, HEAD_DIM)]
+    return (scaled * cos + pltpu.roll(scaled, HEAD_DIM // 2, axis=1) * sin).astype(BF16)
+
+
+def keys_kernel(
+    near, far, middle_sums, keep, own_sums, gains, cosines, sines, levels,
+    kv_out, q_out, sums_out, size, units,
 ):
     line, _, _, _ = here()
     upper, odd = line // 2, line % 2
@@ -259,28 +277,30 @@
     units[0] = keep[...]
     units[1] = near[:ROWS, :]
     units[2] = far[:ROWS, :]
+    inner = (line == 1) | (line == 2)
     pieces = [
-        own_sums[...].astype(F32), near[ROWS:, :].astype(F32),
-        far[ROWS:, :].astype(F32), last_sums[...].astype(F32),
+        own_sums[...].astype(F32), near[ROWS:, :].astype(F32), far[ROWS:, :].astype(F32),
+        jnp.where(inner, middle_sums[...].astype(F32), 0.0),
     ]
-    row_id = lax.broadcasted_iota(jnp.int32, (16, 1), 0)
-    cos, sin = cosines[...], sines[...]
-    for kind in range(2):
-        wanted = row_id // 3 == kind
-        total = jnp.zeros((1, PAIR), F32)
-        for piece in pieces:
-            total += jnp.sum(jnp.where(wanted, piece, 0.0), axis=0, keepdims=True)
-        scale = lax.rsqrt(total * (1.0 / ATT) + 1e-06)
-        scale = jnp.transpose(jnp.broadcast_to(scale, (HEAD_DIM, PAIR)))[:ROWS]
-        values = units[slots[kind]].astype(F32)
-        for head in range(2):
-            columns = slice(head * HEAD_DIM, (head + 1) * HEAD_DIM)
-            at = pl.multiple_of(line * PAIR + head * HEAD_DIM, HEAD_DIM)
-            scaled = values[:, columns] * scale * gains[kind : kind + 1, pl.ds(at, HEAD_DIM)]
-            turned = scaled * cos + pltpu.roll(scaled, HEAD_DIM // 2, axis=1) * sin
-            (kv_out if kind else q_out)[:, columns] = turned.astype(BF16)
+    scale = row_scale(pieces, 1)
+    values = units[slots[1]].astype(F32)
+    for head in range(2):
+        columns = slice(head * HEAD_DIM, (head + 1) * HEAD_DIM)
+        kv_out[:, columns] = turn(values, scale, gains, 1, head, cosines[...], sines[...])
     kv_out[:, PAIR:] = units[slots[2]]
     size[...] = step_size(levels)
+    q_out[...] = units[slots[0]]
+    sums_out[...] = pieces[0] + pieces[1] + pieces[2] + pieces[3]
+
+
+def queries_kernel(raw, sums, last_sums, gains, cosines, sines, q_out):
+    line = here()[0]
+    last = jnp.where(line == 3, last_sums[...].astype(F32), 0.0)
+    scale = row_scale([sums[...], last], 0)
+    values = raw[...].astype(F32)
+    for head in range(2):
+        columns = slice(head * HEAD_DIM, (head + 1) * HEAD_DIM)
+        q_out[:, columns] = turn(values, scale, gains, 0, head, cosines[...], sines[...])
 
 
 def attend_group(queries, one, two, head, counts=None):
@@ -384,6 +404,10 @@
 
     def along(step, value):
         return lax.ppermute(value, "seq", [(i, i ^ (2 * step)) for i in range(2 * LINE)])
+
+    def middle(value):
+        pairs = [(i, i ^ 6 if i in (2, 3, 4, 5) else i ^ 1) for i in range(2 * LINE)]
+        return lax.ppermute(value, "seq", pairs)
 
     def across(value):
         return lax.ppermute(value, "seq", [(i, i ^ 1) for i in range(2 * LINE)])
@@ -437,21 +461,25 @@
         x1, x2, x3, modded_own, shift_scale, w_qkv,
         w_mine, w_last, w_chip, w_core, w_core_last, w_core_chip,
     )
-    far, last_sums, near = along(2, far), along(3, sums), along(1, near)
-    queries, pairs, size = vmem_call(
-        rope_kernel,
-        [((ROWS, PAIR), BF16), ((ROWS, 2 * PAIR), BF16), ((1, HEAD_DIM), F32)],
-        "rope", 1 << 22, [pltpu.VMEM((3, ROWS, PAIR), BF16)],
-    )(near, far, last_sums, keep, sums, qk_gain, cosines, sines, noise_level[None])
-    chip_pairs, side_pairs = chips(pairs), across(pairs)
+    near, middle_sums, far = along(1, near), middle(sums), along(2, far)
+    pairs, raw_queries, some_sums, size = vmem_call(
+        keys_kernel,
+        [((ROWS, 2 * PAIR), BF16), ((ROWS, PAIR), BF16), ((16, PAIR), F32), ((1, HEAD_DIM), F32)],
+        "rope_keys", 1 << 22, [pltpu.VMEM((3, ROWS, PAIR), BF16)],
+    )(near, far, middle_sums, keep, sums, qk_gain, cosines, sines, noise_level[None])
+    _, late_sums = lax.optimization_barrier((some_sums, sums))
+    chip_pairs, side_pairs, last_sums = chips(pairs), across(pairs), along(3, late_sums)
     both_pairs = chips_and_sides(pairs)
     chip_pairs, side_pairs = lax.optimization_barrier((chip_pairs, side_pairs))
+    both_pairs, last_sums = lax.optimization_barrier((both_pairs, last_sums))
+    (queries,) = vmem_call(queries_kernel, [((ROWS, PAIR), BF16)], "rope_queries", 1 << 22)(
+        raw_queries, some_sums, last_sums, qk_gain, cosines, sines
+    )
     state = [((2, ROWS, PAIR), F32), ((2, ROWS, HEAD_DIM), F32)]
     now = vmem_call(first_attend_kernel, state, "attend_first", 1 << 27)(
         queries, chip_pairs, both_pairs, pairs, side_pairs
     )
-    _, late_pairs = lax.optimization_barrier((side_pairs, pairs))
-    core_pairs = cores(late_pairs)
+    core_pairs = cores(pairs)
     core_side, core_chip, core_both = cores(side_pairs), cores(chip_pairs), cores(both_pairs)
     part3, part2, part1, part0 = vmem_call(
         last_attend_kernel, [((TOK_DEV, PAIR), BF16)] * 4, "attend_last", 1 << 27,

time: 54.9 us -> 54.5 us (level)
  waiting for transfers between devices: 13.1 us -> 12.2 us
    ppermute x1, waiting for transfers between devices: 0.01 us -> 2.12 us  [chips_and_sides(): return lax.ppermute(value, ('slab', 'seq'), pairs)]
    ppermute x2, waiting for transfers between devices: 1.87 us -> 0.01 us  [chips(): return lax.ppermute(value, 'slab', [(i, i ^ 2) for i in range(4)])]
    ppermute x7, starting transfers between devices: 8.91 us -> 10.4 us  [cores(): return lax.ppermute(value, 'slab', [(i, i ^ 1) for i in range(4)])]
    ppermute x3, waiting for transfers between devices: 2.29 us -> 0.79 us  [across(): return lax.ppermute(value, 'seq', [(i, i ^ 1) for i in range(2 * LINE)])]
    ppermute x9, starting transfers between devices: 12 us -> 10.7 us  [along(): lax.ppermute(value, 'seq', [(i, i ^ 2 * step) for i in range(2 * LINE)])]
    ppermute x0 -> x1, waiting for transfers between devices: none -> 1.07 us  [middle(): return lax.ppermute(value, 'seq', pairs)]
    ppermute x1, waiting for transfers between devices: 3.13 us -> 2.23 us  [from_behind(): return lax.ppermute(value, axis, pairs)]
    ppermute x0 -> x1, starting transfers between devices: none -> 0.66 us  [middle(): return lax.ppermute(value, 'seq', pairs)]
  transfers between devices with their start and end apart: 23 -> 24, of which waited for: 10 -> 12; matrix products, arithmetic and copies ran while one was open for 3% -> 3% of each run, Pallas kernels for 3% -> 4%
where the time goes in v6:
time: 54.5 us; the launch traced here: 54.2 us
  starting transfers between devices  29.2 us (54%)
  waiting for transfers between devices  12.2 us (22%)
  Pallas kernels  5.74 us (11%)
  local copies, waits for them, and re-layouts  4.27 us (8%)
  between operations  1.53 us (3%)
  other arithmetic  1.3 us (2%)
    ppermute x9, starting transfers between devices, along(): lax.ppermute(value, 'seq', [(i, i ^ 2 * step) for i in range(2 * LINE)])  10.7 us
    ppermute x7, starting transfers between devices, cores(): return lax.ppermute(value, 'slab', [(i, i ^ 1) for i in range(4)])  10.4 us
    pallas_call x8, Pallas kernels, call(): pl.pallas_call(kernel, out_shape=[jax.ShapeDtypeStruct(shape, dtype) for...  5.74 us
    ppermute x9, waiting for transfers between devices, along(): lax.ppermute(value, 'seq', [(i, i ^ 2 * step) for i in range(2 * LINE)])  5.58 us
    unnamed x25, local copies, waits for them, and re-layouts  3.03 us
    ppermute x2, starting transfers between devices, chips(): return lax.ppermute(value, 'slab', [(i, i ^ 2) for i in range(4)])  2.4 us
    ppermute x3, starting transfers between devices, across(): return lax.ppermute(value, 'seq', [(i, i ^ 1) for i in range(2 * LINE)])  2.36 us
    ppermute x1, waiting for transfers between devices, from_behind(): return lax.ppermute(value, axis, pairs)  2.23 us
  transfers between devices with their start and end apart: 24, of which 12 were waited for; matrix products, arithmetic and copies ran while one was open for 3% of the time, Pallas kernels for 4%

profile of v6, /device:TPU:1, one launch (start us, length us, event | category | flops | bytes accessed | tf_op | source)
XLA Modules:
  0.0 54.2 jit_solution(14356676500480343389)
XLA Ops:
  0.7 1.2 %constant_dynamic-slice_fusion = (bf16[256,384]{1,0:T(8,128)(2,1)S(1)}, bf16[256,384]{1,0:T(8,128)(2,1)S(1)}) fusion(bf16[1536,384]{1,0:T(8,128)(2,1)} %w_own.1, s32[]{:T(128)S(6)} %select_n.19, s32[]{:T(128)S(6)} %select_n.18), kind=kLoop, calls=%fused_computation.9 | loop fusion | bytes 786440 | tf_op jit(solution)/shard_map/dynamic_slice | solution.py:433
  1.8 2.1 %collective-permute-start.4 = (bf16[256,384]{1,0:T(8,128)(2,1)S(1)}, bf16[256,384]{1,0:T(8,128)(2,1)S(1)}, u32[]{:S(2)}, u32[]{:S(2)}) collective-permute-start(bf16[256,384]{1,0:T(8,128)(2,1)S(1)} %get-tuple-element.62), channel_id=1, source_target_pairs={{0,1},{1,0},{2,3},{3,2},{4,5},{5,4},{6,7},{7,6},{8,9},{9,8},{10,11... | collective-permute-start | bytes 589832 | tf_op jit(solution)/shard_map/ppermute | solution.py:413
  3.9 1.3 %collective-permute-start = (bf16[48,1536]{1,0:T(8,128)(2,1)}, bf16[48,1536]{1,0:T(8,128)(2,1)S(1)}, u32[]{:S(2)}, u32[]{:S(2)}) collective-permute-start(bf16[48,1536]{1,0:T(8,128)(2,1)} %bitcast.10), channel_id=1, source_target_pairs={{0,2},{1,3},{2,0},{3,1},{4,6},{5,7},{6,4},{7,5},{8,10},{9,11},{10,... | collective-permute-start | bytes 442376 | tf_op jit(solution)/shard_map/ppermute | solution.py:406
  5.2 2.3 %collective-permute-start.1 = (bf16[48,1536]{1,0:T(8,128)(2,1)}, bf16[48,1536]{1,0:T(8,128)(2,1)S(1)}, u32[]{:S(2)}, u32[]{:S(2)}) collective-permute-start(bf16[48,1536]{1,0:T(8,128)(2,1)} %bitcast.11), channel_id=1, source_target_pairs={{0,4},{1,5},{2,6},{3,7},{4,0},{5,1},{6,2},{7,3},{8,12},{9,13},{10,... | collective-permute-start | bytes 442376 | tf_op jit(solution)/shard_map/ppermute | solution.py:406
  7.8 0.8 %collective-permute-done.4.w_mine = bf16[256,384]{1,0:T(8,128)(2,1)S(1)} collective-permute-done((bf16[256,384]{1,0:T(8,128)(2,1)S(1)}, bf16[256,384]{1,0:T(8,128)(2,1)S(1)}, u32[]{:S(2)}, u32[]{:S(2)}) %collective-permute-start.4) | collective-permute-done | bytes 196640 | tf_op jit(solution)/shard_map/ppermute | solution.py:413
  8.6 1.1 %collective-permute-start.5 = (bf16[256,384]{1,0:T(8,128)(2,1)S(1)}, bf16[256,384]{1,0:T(8,128)(2,1)S(1)}, u32[]{:S(2)}, u32[]{:S(2)}) collective-permute-start(bf16[256,384]{1,0:T(8,128)(2,1)S(1)} %collective-permute-done.4.w_mine), channel_id=1, source_target_pairs={{0,16},{8,24},{16,0},{24,8},{1,17},{9,25},{17,1},{25,9},{2,18},{10... | collective-permute-start | bytes 589832 | tf_op jit(solution)/shard_map/ppermute | solution.py:419
  9.9 0.9 %copy-done.2 = bf16[1,48,1536]{2,1,0:T(8,128)(2,1)S(1)} copy-done((bf16[1,48,1536]{2,1,0:T(8,128)(2,1)S(1)}, bf16[1,48,1536]{2,1,0:T(8,128)(2,1)}, u32[]{:S(2)}) %copy-start.2) | copy-done | bytes 147480
  10.8 0.7 %copy-done.5 = f32[3,1536]{1,0:T(4,128)S(1)} copy-done((f32[3,1536]{1,0:T(4,128)S(1)}, f32[3,1536]{1,0:T(4,128)}, u32[]{:S(2)}) %copy-start.5) | copy-done | bytes 18456
  11.5 0.7 %copy-done.7 = f32[1,3,1536]{2,0,1:T(1,128)S(1)} copy-done((f32[1,3,1536]{2,0,1:T(1,128)S(1)}, f32[1,3,1536]{2,0,1:T(1,128)}, u32[]{:S(2)}) %copy-start.7) | copy-done | bytes 18456
  12.5 2.5 %collective-permute-start.7 = (bf16[256,384]{1,0:T(8,128)(2,1)S(1)}, bf16[256,384]{1,0:T(8,128)(2,1)S(1)}, u32[]{:S(2)}, u32[]{:S(2)}) collective-permute-start(bf16[256,384]{1,0:T(8,128)(2,1)S(1)} %collective-permute-done.3.w_last), channel_id=1, source_target_pairs={{0,8},{8,0},{16,24},{24,16},{1,9},{9,1},{17,25},{25,17},{2,10},{10... | collective-permute-start | bytes 589832 | tf_op jit(solution)/shard_map/ppermute | solution.py:416
  15.0 0.9 %collective-permute-start.6 = (bf16[256,384]{1,0:T(8,128)(2,1)S(1)}, bf16[256,384]{1,0:T(8,128)(2,1)S(1)}, u32[]{:S(2)}, u32[]{:S(2)}) collective-permute-start(bf16[256,384]{1,0:T(8,128)(2,1)S(1)} %collective-permute-done.4.w_mine), channel_id=1, source_target_pairs={{0,8},{8,0},{16,24},{24,16},{1,9},{9,1},{17,25},{25,17},{2,10},{10... | collective-permute-start | bytes 589832 | tf_op jit(solution)/shard_map/ppermute | solution.py:416
  17.3 1.5 %project.1 = (bf16[208,256]{1,0:T(8,128)(2,1)S(1)}, bf16[208,256]{1,0:T(8,128)(2,1)S(1)}, bf16[192,256]{1,0:T(8,128)(2,1)S(1)}, bf16[16,256]{1,0:T(8,128)(2,1)S(1)}) custom-call(bf16[48,1536]{1,0:T(8,128)(2,1)S(1)} %collective-permute-done.x1, bf16[48,1536]{1,0:T(8,128)(2,1)S(1)} %collective-permute-done.1.x2, ...), custom_call_target="tpu_custom_call" | custom-call | flops 268435456 | bytes 1048576 | tf_op jit(solution)/shard_map/project/pallas_call | solution.py:149
  18.8 4.4 %collective-permute-start.10 = (bf16[208,256]{1,0:T(8,128)(2,1)S(1)}, bf16[208,256]{1,0:T(8,128)(2,1)S(1)}, u32[]{:S(2)}, u32[]{:S(2)}) collective-permute-start(bf16[208,256]{1,0:T(8,128)(2,1)S(1)} %get-tuple-element.40), channel_id=1, source_target_pairs={{0,4},{1,5},{2,6},{3,7},{4,0},{5,1},{6,2},{7,3},{8,12},{9,13},{10,... | collective-permute-start | bytes 319496 | tf_op jit(solution)/shard_map/ppermute | solution.py:406
  23.2 0.7 %collective-permute-start.11 = (bf16[16,256]{1,0:T(8,128)(2,1)S(1)}, bf16[16,256]{1,0:T(8,128)(2,1)S(1)}, u32[]{:S(2)}, u32[]{:S(2)}) collective-permute-start(bf16[16,256]{1,0:T(8,128)(2,1)S(1)} %get-tuple-element.46.own_sums), channel_id=1, source_target_pairs={{0,1},{1,0},{2,4},{3,5},{4,2},{5,3},{6,7},{7,6},{8,9},{9,8},{10,12... | collective-permute-start | bytes 24584 | tf_op jit(solution)/shard_map/ppermute | solution.py:410
  24.7 1.1 %collective-permute-done.11.middle_sums = bf16[16,256]{1,0:T(8,128)(2,1)S(1)} collective-permute-done((bf16[16,256]{1,0:T(8,128)(2,1)S(1)}, bf16[16,256]{1,0:T(8,128)(2,1)S(1)}, u32[]{:S(2)}, u32[]{:S(2)}) %collective-permute-start.11) | collective-permute-done | bytes 8224 | tf_op jit(solution)/shard_map/ppermute | solution.py:410
  25.7 1.3 %collective-permute-done.10.far = bf16[208,256]{1,0:T(8,128)(2,1)S(1)} collective-permute-done((bf16[208,256]{1,0:T(8,128)(2,1)S(1)}, bf16[208,256]{1,0:T(8,128)(2,1)S(1)}, u32[]{:S(2)}, u32[]{:S(2)}) %collective-permute-start.10) | collective-permute-done | bytes 106528 | tf_op jit(solution)/shard_map/ppermute | solution.py:406
  27.0 1.7 %collective-permute-done.9.near = bf16[208,256]{1,0:T(8,128)(2,1)S(1)} collective-permute-done((bf16[208,256]{1,0:T(8,128)(2,1)S(1)}, bf16[208,256]{1,0:T(8,128)(2,1)S(1)}, u32[]{:S(2)}, u32[]{:S(2)}) %collective-permute-start.9) | collective-permute-done | bytes 106528 | tf_op jit(solution)/shard_map/ppermute | solution.py:406
  29.0 1.3 %collective-permute-start.15 = (bf16[192,512]{1,0:T(8,128)(2,1)S(1)}, bf16[192,512]{1,0:T(8,128)(2,1)S(1)}, u32[]{:S(2)}, u32[]{:S(2)}) collective-permute-start(bf16[192,512]{1,0:T(8,128)(2,1)S(1)} %get-tuple-element.45.a0), channel_id=1, source_target_pairs={{0,16},{8,24},{16,0},{24,8},{1,17},{9,25},{17,1},{25,9},{2,18},{10... | collective-permute-start | bytes 589832 | tf_op jit(solution)/shard_map/ppermute | solution.py:419
  30.3 1.4 %collective-permute-start.12 = (bf16[192,512]{1,0:T(8,128)(2,1)S(1)}, bf16[192,512]{1,0:T(8,128)(2,1)S(1)}, u32[]{:S(2)}, u32[]{:S(2)}) collective-permute-start(bf16[192,512]{1,0:T(8,128)(2,1)S(1)} %get-tuple-element.45.a0), channel_id=1, source_target_pairs={{0,17},{1,16},{2,19},{3,18},{4,21},{5,20},{6,23},{7,22},{8,25},{9,... | collective-permute-start | bytes 589832 | tf_op jit(solution)/shard_map/ppermute | solution.py:428
  31.7 4.0 %collective-permute-start.14 = (bf16[192,512]{1,0:T(8,128)(2,1)S(1)}, bf16[192,512]{1,0:T(8,128)(2,1)S(1)}, u32[]{:S(2)}, u32[]{:S(2)}) collective-permute-start(bf16[192,512]{1,0:T(8,128)(2,1)S(1)} %get-tuple-element.45.a0), channel_id=1, source_target_pairs={{0,8},{8,0},{16,24},{24,16},{1,9},{9,1},{17,25},{25,17},{2,10},{10... | collective-permute-start | bytes 589832 | tf_op jit(solution)/shard_map/ppermute | solution.py:416
  36.0 2.1 %collective-permute-done.12.c1 = bf16[192,512]{1,0:T(8,128)(2,1)S(1)} collective-permute-done((bf16[192,512]{1,0:T(8,128)(2,1)S(1)}, bf16[192,512]{1,0:T(8,128)(2,1)S(1)}, u32[]{:S(2)}, u32[]{:S(2)}) %collective-permute-start.12) | collective-permute-done | bytes 196640 | tf_op jit(solution)/shard_map/ppermute | solution.py:428
  38.1 2.5 %collective-permute-start.17 = (bf16[192,512]{1,0:T(8,128)(2,1)S(1)}, bf16[192,512]{1,0:T(8,128)(2,1)S(1)}, u32[]{:S(2)}, u32[]{:S(2)}) collective-permute-start(bf16[192,512]{1,0:T(8,128)(2,1)S(1)} %collective-permute-done.16.a1), channel_id=1, source_target_pairs={{0,8},{8,0},{16,24},{24,16},{1,9},{9,1},{17,25},{25,17},{2,10},{10... | collective-permute-start | bytes 589832 | tf_op jit(solution)/shard_map/ppermute | solution.py:416
  41.3 1.0 %attend_first.1 = (f32[2,192,256]{2,1,0:T(8,128)S(1)}, f32[2,192,128]{2,1,0:T(8,128)S(1)}) custom-call(bf16[192,256]{1,0:T(8,128)(2,1)S(1)} %rope_queries.1.queries, bf16[192,512]{1,0:T(8,128)(2,1)S(1)} %collective-permute-done.15.c0, bf16[192,512]{1,0:T(8,128)(2,1)S(1)} %collective-permute-done.12.c1, bf16[192,512]{1,0:T(8,128)(2,1)S(1)} %get-tuple-element.45.a0, ...), custom_call_target="tpu_custom_call" | custom-call | flops 134217728 | bytes 1048576 | tf_op jit(solution)/shard_map/attend_first/pallas_call | solution.py:149
  42.4 1.0 %attend_last.1 = (bf16[48,256]{1,0:T(8,128)(2,1)S(1)}, bf16[48,256]{1,0:T(8,128)(2,1)S(1)}, bf16[48,256]{1,0:T(8,128)(2,1)S(1)}, bf16[48,256]{1,0:T(8,128)(2,1)S(1)}) custom-call(bf16[192,256]{1,0:T(8,128)(2,1)S(1)} %rope_queries.1.queries, bf16[192,512]{1,0:T(8,128)(2,1)S(1)} %collective-permute-done.14.b0, ...), custom_call_target="tpu_custom_call" | custom-call | flops 134217728 | bytes 1048576 | tf_op jit(solution)/shard_map/attend_last/pallas_call | solution.py:149
  43.5 1.6 %collective-permute-start.21 = (bf16[48,256]{1,0:T(8,128)(2,1)S(1)}, bf16[48,256]{1,0:T(8,128)(2,1)S(1)}, u32[]{:S(2)}, u32[]{:S(2)}) collective-permute-start(bf16[48,256]{1,0:T(8,128)(2,1)S(1)} %get-tuple-element.54), channel_id=1, source_target_pairs={{0,6},{1,7},{2,4},{3,5},{4,2},{5,3},{6,0},{7,1},{8,14},{9,15},{10,... | collective-permute-start | bytes 73736 | tf_op jit(solution)/shard_map/ppermute | solution.py:406
  45.1 1.1 %collective-permute-start.22 = (bf16[48,256]{1,0:T(8,128)(2,1)S(1)}, bf16[48,256]{1,0:T(8,128)(2,1)S(1)}, u32[]{:S(2)}, u32[]{:S(2)}) collective-permute-start(bf16[48,256]{1,0:T(8,128)(2,1)S(1)} %get-tuple-element.55), channel_id=1, source_target_pairs={{0,2},{1,3},{2,0},{3,1},{4,6},{5,7},{6,4},{7,5},{8,10},{9,11},{10,... | collective-permute-start | bytes 73736 | tf_op jit(solution)/shard_map/ppermute | solution.py:406
  47.2 0.9 %collective-permute-done.21.r3 = bf16[48,256]{1,0:T(8,128)(2,1)S(1)} collective-permute-done((bf16[48,256]{1,0:T(8,128)(2,1)S(1)}, bf16[48,256]{1,0:T(8,128)(2,1)S(1)}, u32[]{:S(2)}, u32[]{:S(2)}) %collective-permute-start.21) | collective-permute-done | bytes 24608 | tf_op jit(solution)/shard_map/ppermute | solution.py:406
  48.5 1.0 %finish.1 = (f32[48,1536]{1,0:T(8,128)S(1)}, f32[48,64]{1,0:T(8,128)S(1)}) custom-call(bf16[48,256]{1,0:T(8,128)(2,1)S(1)} %collective-permute-done.20.r2, bf16[48,256]{1,0:T(8,128)(2,1)S(1)} %collective-permute-done.21.r3, bf16[48,256]{1,0:T(8,128)(2,1)S(1)} %collective-permute-done.22.r1, bf16[1024,1536]{1,0:T(8,128)(2,1)S(1)} %copy-done, ...), custom_call_target="tpu_custom_call" | custom-call | flops 268435456 | bytes 1048576 | tf_op jit(solution)/shard_map/finish/pallas_call | solution.py:149
  49.5 1.2 %collective-permute-start.23 = (f32[1,48,64]{2,1,0:T(8,128)S(1)}, f32[1,48,64]{2,1,0:T(8,128)S(1)}, u32[]{:S(2)}, u32[]{:S(2)}) collective-permute-start(f32[1,48,64]{2,1,0:T(8,128)S(1)} %bitcast.20), channel_id=1, source_target_pairs={{0,24},{8,0},{16,8},{24,16},{1,25},{9,1},{17,9},{25,17},{2,26},{10... | collective-permute-start | bytes 36872 | tf_op jit(solution)/shard_map/ppermute | solution.py:29
  50.7 0.7 %convert_bitcast_fusion = bf16[1,48,1536]{2,1,0:T(8,128)(2,1)} fusion(f32[48,1536]{1,0:T(8,128)S(1)} %get-tuple-element.60), kind=kLoop, calls=%fused_computation | loop fusion | flops 73728 | bytes 442368 | tf_op jit(solution)/shard_map/broadcast_in_dim | solution.py:499
  51.4 2.2 %collective-permute-done.23 = f32[1,48,64]{2,1,0:T(8,128)S(1)} collective-permute-done((f32[1,48,64]{2,1,0:T(8,128)S(1)}, f32[1,48,64]{2,1,0:T(8,128)S(1)}, u32[]{:S(2)}, u32[]{:S(2)}) %collective-permute-start.23) | collective-permute-done | bytes 12320 | tf_op jit(solution)/shard_map/ppermute | solution.py:29
  53.6 0.6 %copy.14 = f32[1,48,64]{2,1,0:T(8,128)} copy(f32[1,48,64]{2,1,0:T(8,128)S(1)} %collective-permute-done.23) | data formatting | bytes 24576
  (57 shorter events, 5.0 us)
Async XLA Ops:
  0.6 16.7 %copy-start.1 = (bf16[1536,384]{1,0:T(8,128)(2,1)S(1)}, bf16[1536,384]{1,0:T(8,128)(2,1)}, u32[]{:S(2)}) copy-start(bf16[1536,384]{1,0:T(8,128)(2,1)} %w_own.1) | copy-start | bytes 3538948
  1.8 6.8 %collective-permute-start.4 = (bf16[256,384]{1,0:T(8,128)(2,1)S(1)}, bf16[256,384]{1,0:T(8,128)(2,1)S(1)}, u32[]{:S(2)}, u32[]{:S(2)}) collective-permute-start(bf16[256,384]{1,0:T(8,128)(2,1)S(1)} %get-tuple-element.62), channel_id=1, source_target_pairs={{0,1},{1,0},{2,3},{3,2},{4,5},{5,4},{6,7},{7,6},{8,9},{9,8},{10,11... | collective-permute-start | bytes 589832 | tf_op jit(solution)/shard_map/ppermute | solution.py:413
  3.9 11.9 %collective-permute-start = (bf16[48,1536]{1,0:T(8,128)(2,1)}, bf16[48,1536]{1,0:T(8,128)(2,1)S(1)}, u32[]{:S(2)}, u32[]{:S(2)}) collective-permute-start(bf16[48,1536]{1,0:T(8,128)(2,1)} %bitcast.10), channel_id=1, source_target_pairs={{0,2},{1,3},{2,0},{3,1},{4,6},{5,7},{6,4},{7,5},{8,10},{9,11},{10,... | collective-permute-start | bytes 442376 | tf_op jit(solution)/shard_map/ppermute | solution.py:406
  5.2 11.1 %collective-permute-start.1 = (bf16[48,1536]{1,0:T(8,128)(2,1)}, bf16[48,1536]{1,0:T(8,128)(2,1)S(1)}, u32[]{:S(2)}, u32[]{:S(2)}) collective-permute-start(bf16[48,1536]{1,0:T(8,128)(2,1)} %bitcast.11), channel_id=1, source_target_pairs={{0,4},{1,5},{2,6},{3,7},{4,0},{5,1},{6,2},{7,3},{8,12},{9,13},{10,... | collective-permute-start | bytes 442376 | tf_op jit(solution)/shard_map/ppermute | solution.py:406
  7.6 9.4 %collective-permute-start.2 = (bf16[48,1536]{1,0:T(8,128)(2,1)}, bf16[48,1536]{1,0:T(8,128)(2,1)S(1)}, u32[]{:S(2)}, u32[]{:S(2)}) collective-permute-start(bf16[48,1536]{1,0:T(8,128)(2,1)} %bitcast.12), channel_id=1, source_target_pairs={{0,6},{1,7},{2,4},{3,5},{4,2},{5,3},{6,0},{7,1},{8,14},{9,15},{10,... | collective-permute-start | bytes 442376 | tf_op jit(solution)/shard_map/ppermute | solution.py:406
  7.6 4.9 %collective-permute-start.3 = (bf16[256,384]{1,0:T(8,128)(2,1)S(1)}, bf16[256,384]{1,0:T(8,128)(2,1)S(1)}, u32[]{:S(2)}, u32[]{:S(2)}) collective-permute-start(bf16[256,384]{1,0:T(8,128)(2,1)S(1)} %get-tuple-element.63), channel_id=1, source_target_pairs={{0,1},{1,0},{2,3},{3,2},{4,5},{5,4},{6,7},{7,6},{8,9},{9,8},{10,11... | collective-permute-start | bytes 589832 | tf_op jit(solution)/shard_map/ppermute | solution.py:413
  8.6 6.4 %collective-permute-start.5 = (bf16[256,384]{1,0:T(8,128)(2,1)S(1)}, bf16[256,384]{1,0:T(8,128)(2,1)S(1)}, u32[]{:S(2)}, u32[]{:S(2)}) collective-permute-start(bf16[256,384]{1,0:T(8,128)(2,1)S(1)} %collective-permute-done.4.w_mine), channel_id=1, source_target_pairs={{0,16},{8,24},{16,0},{24,8},{1,17},{9,25},{17,1},{25,9},{2,18},{10... | collective-permute-start | bytes 589832 | tf_op jit(solution)/shard_map/ppermute | solution.py:419
  12.5 4.5 %collective-permute-start.7 = (bf16[256,384]{1,0:T(8,128)(2,1)S(1)}, bf16[256,384]{1,0:T(8,128)(2,1)S(1)}, u32[]{:S(2)}, u32[]{:S(2)}) collective-permute-start(bf16[256,384]{1,0:T(8,128)(2,1)S(1)} %collective-permute-done.3.w_last), channel_id=1, source_target_pairs={{0,8},{8,0},{16,24},{24,16},{1,9},{9,1},{17,25},{25,17},{2,10},{10... | collective-permute-start | bytes 589832 | tf_op jit(solution)/shard_map/ppermute | solution.py:416
  15.0 2.0 %collective-permute-start.6 = (bf16[256,384]{1,0:T(8,128)(2,1)S(1)}, bf16[256,384]{1,0:T(8,128)(2,1)S(1)}, u32[]{:S(2)}, u32[]{:S(2)}) collective-permute-start(bf16[256,384]{1,0:T(8,128)(2,1)S(1)} %collective-permute-done.4.w_mine), channel_id=1, source_target_pairs={{0,8},{8,0},{16,24},{24,16},{1,9},{9,1},{17,25},{25,17},{2,10},{10... | collective-permute-start | bytes 589832 | tf_op jit(solution)/shard_map/ppermute | solution.py:416
  15.9 1.4 %collective-permute-start.8 = (bf16[256,384]{1,0:T(8,128)(2,1)S(1)}, bf16[256,384]{1,0:T(8,128)(2,1)S(1)}, u32[]{:S(2)}, u32[]{:S(2)}) collective-permute-start(bf16[256,384]{1,0:T(8,128)(2,1)S(1)} %collective-permute-done.5.w_chip), channel_id=1, source_target_pairs={{0,8},{8,0},{16,24},{24,16},{1,9},{9,1},{17,25},{25,17},{2,10},{10... | collective-permute-start | bytes 589832 | tf_op jit(solution)/shard_map/ppermute | solution.py:416
  16.3 12.4 %copy-start.9 = (f32[2,1024]{1,0:T(2,128)S(1)}, f32[2,1024]{1,0:T(2,128)}, u32[]{:S(2)}) copy-start(f32[2,1024]{1,0:T(2,128)} %gains.3) | copy-start | bytes 24580
  18.8 8.2 %collective-permute-start.10 = (bf16[208,256]{1,0:T(8,128)(2,1)S(1)}, bf16[208,256]{1,0:T(8,128)(2,1)S(1)}, u32[]{:S(2)}, u32[]{:S(2)}) collective-permute-start(bf16[208,256]{1,0:T(8,128)(2,1)S(1)} %get-tuple-element.40), channel_id=1, source_target_pairs={{0,4},{1,5},{2,6},{3,7},{4,0},{5,1},{6,2},{7,3},{8,12},{9,13},{10,... | collective-permute-start | bytes 319496 | tf_op jit(solution)/shard_map/ppermute | solution.py:406
  23.2 5.5 %collective-permute-start.9 = (bf16[208,256]{1,0:T(8,128)(2,1)S(1)}, bf16[208,256]{1,0:T(8,128)(2,1)S(1)}, u32[]{:S(2)}, u32[]{:S(2)}) collective-permute-start(bf16[208,256]{1,0:T(8,128)(2,1)S(1)} %get-tuple-element.39), channel_id=1, source_target_pairs={{0,2},{1,3},{2,0},{3,1},{4,6},{5,7},{6,4},{7,5},{8,10},{9,11},{10,... | collective-permute-start | bytes 319496 | tf_op jit(solution)/shard_map/ppermute | solution.py:406
  23.2 2.5 %collective-permute-start.11 = (bf16[16,256]{1,0:T(8,128)(2,1)S(1)}, bf16[16,256]{1,0:T(8,128)(2,1)S(1)}, u32[]{:S(2)}, u32[]{:S(2)}) collective-permute-start(bf16[16,256]{1,0:T(8,128)(2,1)S(1)} %get-tuple-element.46.own_sums), channel_id=1, source_target_pairs={{0,1},{1,0},{2,4},{3,5},{4,2},{5,3},{6,7},{7,6},{8,9},{9,8},{10,12... | collective-permute-start | bytes 24584 | tf_op jit(solution)/shard_map/ppermute | solution.py:410
  23.9 22.2 %copy-start.11 = (f32[1,2,1536]{2,1,0:T(2,128)S(1)}, f32[1,2,1536]{2,1,0:T(2,128)}, u32[]{:S(2)}) copy-start(f32[1,2,1536]{2,1,0:T(2,128)} %param.17) | copy-start | bytes 36868
  28.7 17.4 %copy-start = (bf16[1024,1536]{1,0:T(8,128)(2,1)S(1)}, bf16[1024,1536]{1,0:T(8,128)(2,1)}, u32[]{:S(2)}) copy-start(bf16[1024,1536]{1,0:T(8,128)(2,1)} %w_out.3) | copy-start | bytes 9437188
  29.0 6.8 %collective-permute-start.15 = (bf16[192,512]{1,0:T(8,128)(2,1)S(1)}, bf16[192,512]{1,0:T(8,128)(2,1)S(1)}, u32[]{:S(2)}, u32[]{:S(2)}) collective-permute-start(bf16[192,512]{1,0:T(8,128)(2,1)S(1)} %get-tuple-element.45.a0), channel_id=1, source_target_pairs={{0,16},{8,24},{16,0},{24,8},{1,17},{9,25},{17,1},{25,9},{2,18},{10... | collective-permute-start | bytes 589832 | tf_op jit(solution)/shard_map/ppermute | solution.py:419
  30.3 5.5 %collective-permute-start.16 = (bf16[192,512]{1,0:T(8,128)(2,1)S(1)}, bf16[192,512]{1,0:T(8,128)(2,1)S(1)}, u32[]{:S(2)}, u32[]{:S(2)}) collective-permute-start(bf16[192,512]{1,0:T(8,128)(2,1)S(1)} %get-tuple-element.45.a0), channel_id=1, source_target_pairs={{0,1},{1,0},{2,3},{3,2},{4,5},{5,4},{6,7},{7,6},{8,9},{9,8},{10,11... | collective-permute-start | bytes 589832 | tf_op jit(solution)/shard_map/ppermute | solution.py:413
  30.3 7.8 %collective-permute-start.12 = (bf16[192,512]{1,0:T(8,128)(2,1)S(1)}, bf16[192,512]{1,0:T(8,128)(2,1)S(1)}, u32[]{:S(2)}, u32[]{:S(2)}) collective-permute-start(bf16[192,512]{1,0:T(8,128)(2,1)S(1)} %get-tuple-element.45.a0), channel_id=1, source_target_pairs={{0,17},{1,16},{2,19},{3,18},{4,21},{5,20},{6,23},{7,22},{8,25},{9,... | collective-permute-start | bytes 589832 | tf_op jit(solution)/shard_map/ppermute | solution.py:428
  31.7 4.3 %collective-permute-start.13 = (bf16[16,256]{1,0:T(8,128)(2,1)S(1)}, bf16[16,256]{1,0:T(8,128)(2,1)S(1)}, u32[]{:S(2)}, u32[]{:S(2)}) collective-permute-start(bf16[16,256]{1,0:T(8,128)(2,1)S(1)} %get-tuple-element.46.own_sums), channel_id=1, source_target_pairs={{0,6},{1,7},{2,4},{3,5},{4,2},{5,3},{6,0},{7,1},{8,14},{9,15},{10,... | collective-permute-start | bytes 24584 | tf_op jit(solution)/shard_map/ppermute | solution.py:406
  31.7 10.6 %collective-permute-start.14 = (bf16[192,512]{1,0:T(8,128)(2,1)S(1)}, bf16[192,512]{1,0:T(8,128)(2,1)S(1)}, u32[]{:S(2)}, u32[]{:S(2)}) collective-permute-start(bf16[192,512]{1,0:T(8,128)(2,1)S(1)} %get-tuple-element.45.a0), channel_id=1, source_target_pairs={{0,8},{8,0},{16,24},{24,16},{1,9},{9,1},{17,25},{25,17},{2,10},{10... | collective-permute-start | bytes 589832 | tf_op jit(solution)/shard_map/ppermute | solution.py:416
  38.1 4.2 %collective-permute-start.17 = (bf16[192,512]{1,0:T(8,128)(2,1)S(1)}, bf16[192,512]{1,0:T(8,128)(2,1)S(1)}, u32[]{:S(2)}, u32[]{:S(2)}) collective-permute-start(bf16[192,512]{1,0:T(8,128)(2,1)S(1)} %collective-permute-done.16.a1), channel_id=1, source_target_pairs={{0,8},{8,0},{16,24},{24,16},{1,9},{9,1},{17,25},{25,17},{2,10},{10... | collective-permute-start | bytes 589832 | tf_op jit(solution)/shard_map/ppermute | solution.py:416
  40.6 1.8 %collective-permute-start.18 = (bf16[192,512]{1,0:T(8,128)(2,1)S(1)}, bf16[192,512]{1,0:T(8,128)(2,1)S(1)}, u32[]{:S(2)}, u32[]{:S(2)}) collective-permute-start(bf16[192,512]{1,0:T(8,128)(2,1)S(1)} %collective-permute-done.15.c0), channel_id=1, source_target_pairs={{0,8},{8,0},{16,24},{24,16},{1,9},{9,1},{17,25},{25,17},{2,10},{10... | collective-permute-start | bytes 589832 | tf_op jit(solution)/shard_map/ppermute | solution.py:416
  40.6 1.8 %collective-permute-start.19 = (bf16[192,512]{1,0:T(8,128)(2,1)S(1)}, bf16[192,512]{1,0:T(8,128)(2,1)S(1)}, u32[]{:S(2)}, u32[]{:S(2)}) collective-permute-start(bf16[192,512]{1,0:T(8,128)(2,1)S(1)} %collective-permute-done.12.c1), channel_id=1, source_target_pairs={{0,8},{8,0},{16,24},{24,16},{1,9},{9,1},{17,25},{25,17},{2,10},{10... | collective-permute-start | bytes 589832 | tf_op jit(solution)/shard_map/ppermute | solution.py:416
  41.3 4.8 %copy-start.3 = (bf16[1,48,1536]{2,1,0:T(8,128)(2,1)S(1)}, bf16[1,48,1536]{2,1,0:T(8,128)(2,1)}, u32[]{:S(2)}) copy-start(bf16[1,48,1536]{2,1,0:T(8,128)(2,1)} %param.10) | copy-start | bytes 442372
  41.3 4.8 %copy-start.6 = (f32[3,1536]{1,0:T(4,128)S(1)}, f32[3,1536]{1,0:T(4,128)}, u32[]{:S(2)}) copy-start(f32[3,1536]{1,0:T(4,128)} %block_in.1) | copy-start | bytes 55300
  41.3 4.8 %copy-start.8 = (f32[1,3,1536]{2,0,1:T(1,128)S(1)}, f32[1,3,1536]{2,0,1:T(1,128)}, u32[]{:S(2)}) copy-start(f32[1,3,1536]{2,0,1:T(1,128)} %param.12) | copy-start | bytes 55300
  43.4 3.8 %collective-permute-start.20 = (bf16[48,256]{1,0:T(8,128)(2,1)S(1)}, bf16[48,256]{1,0:T(8,128)(2,1)S(1)}, u32[]{:S(2)}, u32[]{:S(2)}) collective-permute-start(bf16[48,256]{1,0:T(8,128)(2,1)S(1)} %get-tuple-element.53), channel_id=1, source_target_pairs={{0,4},{1,5},{2,6},{3,7},{4,0},{5,1},{6,2},{7,3},{8,12},{9,13},{10,... | collective-permute-start | bytes 73736 | tf_op jit(solution)/shard_map/ppermute | solution.py:406
  43.5 4.7 %collective-permute-start.21 = (bf16[48,256]{1,0:T(8,128)(2,1)S(1)}, bf16[48,256]{1,0:T(8,128)(2,1)S(1)}, u32[]{:S(2)}, u32[]{:S(2)}) collective-permute-start(bf16[48,256]{1,0:T(8,128)(2,1)S(1)} %get-tuple-element.54), channel_id=1, source_target_pairs={{0,6},{1,7},{2,4},{3,5},{4,2},{5,3},{6,0},{7,1},{8,14},{9,15},{10,... | collective-permute-start | bytes 73736 | tf_op jit(solution)/shard_map/ppermute | solution.py:406
  45.1 3.5 %collective-permute-start.22 = (bf16[48,256]{1,0:T(8,128)(2,1)S(1)}, bf16[48,256]{1,0:T(8,128)(2,1)S(1)}, u32[]{:S(2)}, u32[]{:S(2)}) collective-permute-start(bf16[48,256]{1,0:T(8,128)(2,1)S(1)} %get-tuple-element.55), channel_id=1, source_target_pairs={{0,2},{1,3},{2,0},{3,1},{4,6},{5,7},{6,4},{7,5},{8,10},{9,11},{10,... | collective-permute-start | bytes 73736 | tf_op jit(solution)/shard_map/ppermute | solution.py:406
  46.1 2.4 %copy-start.4 = (bf16[1536,64]{0,1:T(8,128)(2,1)S(1)}, bf16[1536,64]{0,1:T(8,128)(2,1)}, u32[]{:S(2)}) copy-start(bf16[1536,64]{0,1:T(8,128)(2,1)} %param.18) | copy-start | bytes 589828
  49.5 4.1 %collective-permute-start.23 = (f32[1,48,64]{2,1,0:T(8,128)S(1)}, f32[1,48,64]{2,1,0:T(8,128)S(1)}, u32[]{:S(2)}, u32[]{:S(2)}) collective-permute-start(f32[1,48,64]{2,1,0:T(8,128)S(1)} %bitcast.20), channel_id=1, source_target_pairs={{0,24},{8,0},{16,8},{24,16},{1,25},{9,1},{17,9},{25,17},{2,26},{10... | collective-permute-start | bytes 36872 | tf_op jit(solution)/shard_map/ppermute | solution.py:29
  (4 other events, 4.8 us)

commit v7 on v6

--- a/solution.py
+++ b/solution.py
@@ -185,16 +185,24 @@
     return jnp.dot(modded[:, pl.ds(at, depth)], weights[...], preferred_element_type=F32)
 
 
+def early_kernel(x1, modded_own, shift_scale, w_own, modded, own):
+    modded[:TOK_DEV, :] = modulated(x1, shift_scale)
+    modded[TOK_DEV:, :] = modded_own[...]
+    own[...] = jnp.dot(modded[...], w_own[...], preferred_element_type=F32).astype(BF16)
+
+
 def project_kernel(
-    x1, x2, x3, modded_own, shift_scale, w_own, w_mine, w_last, w_chip,
+    x2, x3, modded_early, own_early, shift_scale, w_own, w_mine, w_last, w_chip,
     w_core, w_core_last, w_core_chip, far_out, near_out, keep_out, sums_out, modded, mixed,
 ):
-    for place, rows in enumerate((x2, x1, x3)):
+    for place, rows in enumerate((x2, x3)):
         modded[place * TOK_DEV : (place + 1) * TOK_DEV, :] = modulated(rows, shift_scale)
-    modded[3 * TOK_DEV :, :] = modded_own[...]
+    late = 2 * TOK_DEV
+    modded[late:, :] = modded_early[...]
     line, side, core, chip = here()
     width = w_own.shape[1]
-    own = jnp.dot(modded[...], w_own[...], preferred_element_type=F32).astype(BF16)
+    own = jnp.dot(modded[:late, :], w_own[...], preferred_element_type=F32).astype(BF16)
+    own = jnp.concatenate([own, own_early[...]], axis=0)
     total = part_product(modded, w_mine, 2 * chip + core)
     total += part_product(modded, w_core, 2 * chip + 1 - core)
     total += part_product(modded, w_chip, 2 * (1 - chip) + core)
@@ -203,7 +211,7 @@
     other = (total + part_product(modded, w_core_last, 5 - core)).astype(BF16)
     mine = pl.multiple_of(side * width, width)
     there = pl.multiple_of((1 - side) * width, width)
-    for place, step in enumerate((2, 1, 3, 0)):
+    for place, step in enumerate((2, 3, 1, 0)):
         at = pl.multiple_of(jnp.bitwise_xor(line, step) * TOK_DEV, 16)
         rows = slice(place * TOK_DEV, (place + 1) * TOK_DEV)
         mixed[pl.ds(at, TOK_DEV), pl.ds(mine, width)] = own[rows]
@@ -452,13 +460,17 @@
     w_core_last = cores(w_last)
     w_mine, w_chip = lax.optimization_barrier((w_mine, w_chip))
     w_core, w_core_chip = cores(w_mine), cores(w_chip)
+    modded_early, own_early = vmem_call(
+        early_kernel,
+        [((2 * TOK_DEV, D), BF16), ((2 * TOK_DEV, w_qkv.shape[1]), BF16)], "early", 1 << 26,
+    )(x1, modded_own, shift_scale, w_qkv)
     message = (ROWS + 16, PAIR)
     far, near, keep, sums = vmem_call(
         project_kernel,
         [(message, BF16), (message, BF16), ((ROWS, PAIR), BF16), ((16, PAIR), BF16)],
         "project", 1 << 28, [pltpu.VMEM((ROWS, D), BF16), pltpu.VMEM((ROWS, 3 * PAIR), BF16)],
     )(
-        x1, x2, x3, modded_own, shift_scale, w_qkv,
+        x2, x3, modded_early, own_early, shift_scale, w_qkv,
         w_mine, w_last, w_chip, w_core, w_core_last, w_core_chip,
     )
     near, middle_sums, far = along(1, near), middle(sums), along(2, far)

time: 54.5 us -> 54.4 us (level)
    pallas_call x8 -> x9, Pallas kernels: 5.74 us -> 6.1 us  [call(): pl.pallas_call(kernel, out_shape=[jax.ShapeDtypeStruct(shape, dtype) for...]
  transfers between devices with their start and end apart: 24 -> 24, of which waited for: 12 -> 12; matrix products, arithmetic and copies ran while one was open for 3% -> 3% of each run, Pallas kernels for 4% -> 5%
where the time goes in v7:
time: 54.4 us; the launch traced here: 54.1 us
  starting transfers between devices  29.2 us (54%)
  waiting for transfers between devices  11.7 us (22%)
  Pallas kernels  6.1 us (11%)
  local copies, waits for them, and re-layouts  4.27 us (8%)
  between operations  1.53 us (3%)
  other arithmetic  1.3 us (2%)
    ppermute x9, starting transfers between devices, along(): lax.ppermute(value, 'seq', [(i, i ^ 2 * step) for i in range(2 * LINE)])  10.7 us
    ppermute x7, starting transfers between devices, cores(): return lax.ppermute(value, 'slab', [(i, i ^ 1) for i in range(4)])  10.4 us
    pallas_call x9, Pallas kernels, call(): pl.pallas_call(kernel, out_shape=[jax.ShapeDtypeStruct(shape, dtype) for...  6.1 us
    ppermute x9, waiting for transfers between devices, along(): lax.ppermute(value, 'seq', [(i, i ^ 2 * step) for i in range(2 * LINE)])  5.04 us
    unnamed x25, local copies, waits for them, and re-layouts  3.02 us
    ppermute x2, starting transfers between devices, chips(): return lax.ppermute(value, 'slab', [(i, i ^ 2) for i in range(4)])  2.39 us
    ppermute x3, starting transfers between devices, across(): return lax.ppermute(value, 'seq', [(i, i ^ 1) for i in range(2 * LINE)])  2.36 us
    ppermute x1, waiting for transfers between devices, from_behind(): return lax.ppermute(value, axis, pairs)  2.25 us
  transfers between devices with their start and end apart: 24, of which 12 were waited for; matrix products, arithmetic and copies ran while one was open for 3% of the time, Pallas kernels for 5%

profile of v7, /device:TPU:1, one launch (start us, length us, event | category | flops | bytes accessed | tf_op | source)
XLA Modules:
  0.0 54.1 jit_solution(15224226295266615409)
XLA Ops:
  0.7 1.2 %constant_dynamic-slice_fusion = (bf16[256,384]{1,0:T(8,128)(2,1)S(1)}, bf16[256,384]{1,0:T(8,128)(2,1)S(1)}) fusion(bf16[1536,384]{1,0:T(8,128)(2,1)} %w_own.3, s32[]{:T(128)S(6)} %select_n.19, s32[]{:T(128)S(6)} %select_n.18), kind=kLoop, calls=%fused_computation.9 | loop fusion | bytes 786440 | tf_op jit(solution)/shard_map/dynamic_slice | solution.py:441
  1.8 2.1 %collective-permute-start.4 = (bf16[256,384]{1,0:T(8,128)(2,1)S(1)}, bf16[256,384]{1,0:T(8,128)(2,1)S(1)}, u32[]{:S(2)}, u32[]{:S(2)}) collective-permute-start(bf16[256,384]{1,0:T(8,128)(2,1)S(1)} %get-tuple-element.66), channel_id=1, source_target_pairs={{0,1},{1,0},{2,3},{3,2},{4,5},{5,4},{6,7},{7,6},{8,9},{9,8},{10,11... | collective-permute-start | bytes 589832 | tf_op jit(solution)/shard_map/ppermute | solution.py:421
  3.9 1.3 %collective-permute-start.2 = (bf16[48,1536]{1,0:T(8,128)(2,1)}, bf16[48,1536]{1,0:T(8,128)(2,1)S(1)}, u32[]{:S(2)}, u32[]{:S(2)}) collective-permute-start(bf16[48,1536]{1,0:T(8,128)(2,1)} %bitcast.10), channel_id=1, source_target_pairs={{0,2},{1,3},{2,0},{3,1},{4,6},{5,7},{6,4},{7,5},{8,10},{9,11},{10,... | collective-permute-start | bytes 442376 | tf_op jit(solution)/shard_map/ppermute | solution.py:414
  5.2 2.3 %collective-permute-start = (bf16[48,1536]{1,0:T(8,128)(2,1)}, bf16[48,1536]{1,0:T(8,128)(2,1)S(1)}, u32[]{:S(2)}, u32[]{:S(2)}) collective-permute-start(bf16[48,1536]{1,0:T(8,128)(2,1)} %bitcast.11), channel_id=1, source_target_pairs={{0,4},{1,5},{2,6},{3,7},{4,0},{5,1},{6,2},{7,3},{8,12},{9,13},{10,... | collective-permute-start | bytes 442376 | tf_op jit(solution)/shard_map/ppermute | solution.py:414
  7.8 0.8 %collective-permute-done.4.w_mine = bf16[256,384]{1,0:T(8,128)(2,1)S(1)} collective-permute-done((bf16[256,384]{1,0:T(8,128)(2,1)S(1)}, bf16[256,384]{1,0:T(8,128)(2,1)S(1)}, u32[]{:S(2)}, u32[]{:S(2)}) %collective-permute-start.4) | collective-permute-done | bytes 196640 | tf_op jit(solution)/shard_map/ppermute | solution.py:421
  8.6 1.1 %collective-permute-start.5 = (bf16[256,384]{1,0:T(8,128)(2,1)S(1)}, bf16[256,384]{1,0:T(8,128)(2,1)S(1)}, u32[]{:S(2)}, u32[]{:S(2)}) collective-permute-start(bf16[256,384]{1,0:T(8,128)(2,1)S(1)} %collective-permute-done.4.w_mine), channel_id=1, source_target_pairs={{0,16},{8,24},{16,0},{24,8},{1,17},{9,25},{17,1},{25,9},{2,18},{10... | collective-permute-start | bytes 589832 | tf_op jit(solution)/shard_map/ppermute | solution.py:427
  9.9 0.9 %copy-done.2 = bf16[1,48,1536]{2,1,0:T(8,128)(2,1)S(1)} copy-done((bf16[1,48,1536]{2,1,0:T(8,128)(2,1)S(1)}, bf16[1,48,1536]{2,1,0:T(8,128)(2,1)}, u32[]{:S(2)}) %copy-start.2) | copy-done | bytes 147480
  10.8 0.7 %copy-done.5 = f32[3,1536]{1,0:T(4,128)S(1)} copy-done((f32[3,1536]{1,0:T(4,128)S(1)}, f32[3,1536]{1,0:T(4,128)}, u32[]{:S(2)}) %copy-start.5) | copy-done | bytes 18456
  11.5 0.7 %copy-done.7 = f32[1,3,1536]{2,0,1:T(1,128)S(1)} copy-done((f32[1,3,1536]{2,0,1:T(1,128)S(1)}, f32[1,3,1536]{2,0,1:T(1,128)}, u32[]{:S(2)}) %copy-start.7) | copy-done | bytes 18456
  12.5 2.5 %collective-permute-start.7 = (bf16[256,384]{1,0:T(8,128)(2,1)S(1)}, bf16[256,384]{1,0:T(8,128)(2,1)S(1)}, u32[]{:S(2)}, u32[]{:S(2)}) collective-permute-start(bf16[256,384]{1,0:T(8,128)(2,1)S(1)} %collective-permute-done.3.w_last), channel_id=1, source_target_pairs={{0,8},{8,0},{16,24},{24,16},{1,9},{9,1},{17,25},{25,17},{2,10},{10... | collective-permute-start | bytes 589832 | tf_op jit(solution)/shard_map/ppermute | solution.py:424
  15.0 0.9 %collective-permute-start.6 = (bf16[256,384]{1,0:T(8,128)(2,1)S(1)}, bf16[256,384]{1,0:T(8,128)(2,1)S(1)}, u32[]{:S(2)}, u32[]{:S(2)}) collective-permute-start(bf16[256,384]{1,0:T(8,128)(2,1)S(1)} %collective-permute-done.4.w_mine), channel_id=1, source_target_pairs={{0,8},{8,0},{16,24},{24,16},{1,9},{9,1},{17,25},{25,17},{2,10},{10... | collective-permute-start | bytes 589832 | tf_op jit(solution)/shard_map/ppermute | solution.py:424
  17.3 1.3 %project.1 = (bf16[208,256]{1,0:T(8,128)(2,1)S(1)}, bf16[208,256]{1,0:T(8,128)(2,1)S(1)}, bf16[192,256]{1,0:T(8,128)(2,1)S(1)}, bf16[16,256]{1,0:T(8,128)(2,1)S(1)}) custom-call(bf16[48,1536]{1,0:T(8,128)(2,1)S(1)} %collective-permute-done.x2, bf16[48,1536]{1,0:T(8,128)(2,1)S(1)} %collective-permute-done.1.x3, ...), custom_call_target="tpu_custom_call" | custom-call | flops 268435456 | bytes 1048576 | tf_op jit(solution)/shard_map/project/pallas_call | solution.py:149
  18.6 4.4 %collective-permute-start.10 = (bf16[208,256]{1,0:T(8,128)(2,1)S(1)}, bf16[208,256]{1,0:T(8,128)(2,1)S(1)}, u32[]{:S(2)}, u32[]{:S(2)}) collective-permute-start(bf16[208,256]{1,0:T(8,128)(2,1)S(1)} %get-tuple-element.44), channel_id=1, source_target_pairs={{0,4},{1,5},{2,6},{3,7},{4,0},{5,1},{6,2},{7,3},{8,12},{9,13},{10,... | collective-permute-start | bytes 319496 | tf_op jit(solution)/shard_map/ppermute | solution.py:414
  23.1 0.7 %collective-permute-start.11 = (bf16[16,256]{1,0:T(8,128)(2,1)S(1)}, bf16[16,256]{1,0:T(8,128)(2,1)S(1)}, u32[]{:S(2)}, u32[]{:S(2)}) collective-permute-start(bf16[16,256]{1,0:T(8,128)(2,1)S(1)} %get-tuple-element.50.own_sums), channel_id=1, source_target_pairs={{0,1},{1,0},{2,4},{3,5},{4,2},{5,3},{6,7},{7,6},{8,9},{9,8},{10,12... | collective-permute-start | bytes 24584 | tf_op jit(solution)/shard_map/ppermute | solution.py:418
  24.5 1.1 %collective-permute-done.11.middle_sums = bf16[16,256]{1,0:T(8,128)(2,1)S(1)} collective-permute-done((bf16[16,256]{1,0:T(8,128)(2,1)S(1)}, bf16[16,256]{1,0:T(8,128)(2,1)S(1)}, u32[]{:S(2)}, u32[]{:S(2)}) %collective-permute-start.11) | collective-permute-done | bytes 8224 | tf_op jit(solution)/shard_map/ppermute | solution.py:418
  25.6 1.3 %collective-permute-done.10.far = bf16[208,256]{1,0:T(8,128)(2,1)S(1)} collective-permute-done((bf16[208,256]{1,0:T(8,128)(2,1)S(1)}, bf16[208,256]{1,0:T(8,128)(2,1)S(1)}, u32[]{:S(2)}, u32[]{:S(2)}) %collective-permute-start.10) | collective-permute-done | bytes 106528 | tf_op jit(solution)/shard_map/ppermute | solution.py:414
  26.9 1.7 %collective-permute-done.9.near = bf16[208,256]{1,0:T(8,128)(2,1)S(1)} collective-permute-done((bf16[208,256]{1,0:T(8,128)(2,1)S(1)}, bf16[208,256]{1,0:T(8,128)(2,1)S(1)}, u32[]{:S(2)}, u32[]{:S(2)}) %collective-permute-start.9) | collective-permute-done | bytes 106528 | tf_op jit(solution)/shard_map/ppermute | solution.py:414
  28.8 1.3 %collective-permute-start.15 = (bf16[192,512]{1,0:T(8,128)(2,1)S(1)}, bf16[192,512]{1,0:T(8,128)(2,1)S(1)}, u32[]{:S(2)}, u32[]{:S(2)}) collective-permute-start(bf16[192,512]{1,0:T(8,128)(2,1)S(1)} %get-tuple-element.49.a0), channel_id=1, source_target_pairs={{0,16},{8,24},{16,0},{24,8},{1,17},{9,25},{17,1},{25,9},{2,18},{10... | collective-permute-start | bytes 589832 | tf_op jit(solution)/shard_map/ppermute | solution.py:427
  30.1 1.4 %collective-permute-start.12 = (bf16[192,512]{1,0:T(8,128)(2,1)S(1)}, bf16[192,512]{1,0:T(8,128)(2,1)S(1)}, u32[]{:S(2)}, u32[]{:S(2)}) collective-permute-start(bf16[192,512]{1,0:T(8,128)(2,1)S(1)} %get-tuple-element.49.a0), channel_id=1, source_target_pairs={{0,17},{1,16},{2,19},{3,18},{4,21},{5,20},{6,23},{7,22},{8,25},{9,... | collective-permute-start | bytes 589832 | tf_op jit(solution)/shard_map/ppermute | solution.py:436
  31.5 4.1 %collective-permute-start.14 = (bf16[192,512]{1,0:T(8,128)(2,1)S(1)}, bf16[192,512]{1,0:T(8,128)(2,1)S(1)}, u32[]{:S(2)}, u32[]{:S(2)}) collective-permute-start(bf16[192,512]{1,0:T(8,128)(2,1)S(1)} %get-tuple-element.49.a0), channel_id=1, source_target_pairs={{0,8},{8,0},{16,24},{24,16},{1,9},{9,1},{17,25},{25,17},{2,10},{10... | collective-permute-start | bytes 589832 | tf_op jit(solution)/shard_map/ppermute | solution.py:424
  35.8 2.1 %collective-permute-done.12.c1 = bf16[192,512]{1,0:T(8,128)(2,1)S(1)} collective-permute-done((bf16[192,512]{1,0:T(8,128)(2,1)S(1)}, bf16[192,512]{1,0:T(8,128)(2,1)S(1)}, u32[]{:S(2)}, u32[]{:S(2)}) %collective-permute-start.12) | collective-permute-done | bytes 196640 | tf_op jit(solution)/shard_map/ppermute | solution.py:436
  37.9 2.5 %collective-permute-start.17 = (bf16[192,512]{1,0:T(8,128)(2,1)S(1)}, bf16[192,512]{1,0:T(8,128)(2,1)S(1)}, u32[]{:S(2)}, u32[]{:S(2)}) collective-permute-start(bf16[192,512]{1,0:T(8,128)(2,1)S(1)} %collective-permute-done.16.a1), channel_id=1, source_target_pairs={{0,8},{8,0},{16,24},{24,16},{1,9},{9,1},{17,25},{25,17},{2,10},{10... | collective-permute-start | bytes 589832 | tf_op jit(solution)/shard_map/ppermute | solution.py:424
  41.2 1.0 %attend_first.1 = (f32[2,192,256]{2,1,0:T(8,128)S(1)}, f32[2,192,128]{2,1,0:T(8,128)S(1)}) custom-call(bf16[192,256]{1,0:T(8,128)(2,1)S(1)} %rope_queries.1.queries, bf16[192,512]{1,0:T(8,128)(2,1)S(1)} %collective-permute-done.15.c0, bf16[192,512]{1,0:T(8,128)(2,1)S(1)} %collective-permute-done.12.c1, bf16[192,512]{1,0:T(8,128)(2,1)S(1)} %get-tuple-element.49.a0, ...), custom_call_target="tpu_custom_call" | custom-call | flops 134217728 | bytes 1048576 | tf_op jit(solution)/shard_map/attend_first/pallas_call | solution.py:149
  42.2 1.0 %attend_last.1 = (bf16[48,256]{1,0:T(8,128)(2,1)S(1)}, bf16[48,256]{1,0:T(8,128)(2,1)S(1)}, bf16[48,256]{1,0:T(8,128)(2,1)S(1)}, bf16[48,256]{1,0:T(8,128)(2,1)S(1)}) custom-call(bf16[192,256]{1,0:T(8,128)(2,1)S(1)} %rope_queries.1.queries, bf16[192,512]{1,0:T(8,128)(2,1)S(1)} %collective-permute-done.14.b0, ...), custom_call_target="tpu_custom_call" | custom-call | flops 134217728 | bytes 1048576 | tf_op jit(solution)/shard_map/attend_last/pallas_call | solution.py:149
  43.3 1.6 %collective-permute-start.21 = (bf16[48,256]{1,0:T(8,128)(2,1)S(1)}, bf16[48,256]{1,0:T(8,128)(2,1)S(1)}, u32[]{:S(2)}, u32[]{:S(2)}) collective-permute-start(bf16[48,256]{1,0:T(8,128)(2,1)S(1)} %get-tuple-element.58), channel_id=1, source_target_pairs={{0,6},{1,7},{2,4},{3,5},{4,2},{5,3},{6,0},{7,1},{8,14},{9,15},{10,... | collective-permute-start | bytes 73736 | tf_op jit(solution)/shard_map/ppermute | solution.py:414
  44.9 1.0 %collective-permute-start.22 = (bf16[48,256]{1,0:T(8,128)(2,1)S(1)}, bf16[48,256]{1,0:T(8,128)(2,1)S(1)}, u32[]{:S(2)}, u32[]{:S(2)}) collective-permute-start(bf16[48,256]{1,0:T(8,128)(2,1)S(1)} %get-tuple-element.59), channel_id=1, source_target_pairs={{0,2},{1,3},{2,0},{3,1},{4,6},{5,7},{6,4},{7,5},{8,10},{9,11},{10,... | collective-permute-start | bytes 73736 | tf_op jit(solution)/shard_map/ppermute | solution.py:414
  47.0 0.9 %collective-permute-done.21.r3 = bf16[48,256]{1,0:T(8,128)(2,1)S(1)} collective-permute-done((bf16[48,256]{1,0:T(8,128)(2,1)S(1)}, bf16[48,256]{1,0:T(8,128)(2,1)S(1)}, u32[]{:S(2)}, u32[]{:S(2)}) %collective-permute-start.21) | collective-permute-done | bytes 24608 | tf_op jit(solution)/shard_map/ppermute | solution.py:414
  48.4 1.0 %finish.1 = (f32[48,1536]{1,0:T(8,128)S(1)}, f32[48,64]{1,0:T(8,128)S(1)}) custom-call(bf16[48,256]{1,0:T(8,128)(2,1)S(1)} %collective-permute-done.20.r2, bf16[48,256]{1,0:T(8,128)(2,1)S(1)} %collective-permute-done.21.r3, bf16[48,256]{1,0:T(8,128)(2,1)S(1)} %collective-permute-done.22.r1, bf16[1024,1536]{1,0:T(8,128)(2,1)S(1)} %copy-done, ...), custom_call_target="tpu_custom_call" | custom-call | flops 268435456 | bytes 1048576 | tf_op jit(solution)/shard_map/finish/pallas_call | solution.py:149
  49.4 1.2 %collective-permute-start.23 = (f32[1,48,64]{2,1,0:T(8,128)S(1)}, f32[1,48,64]{2,1,0:T(8,128)S(1)}, u32[]{:S(2)}, u32[]{:S(2)}) collective-permute-start(f32[1,48,64]{2,1,0:T(8,128)S(1)} %bitcast.20), channel_id=1, source_target_pairs={{0,24},{8,0},{16,8},{24,16},{1,25},{9,1},{17,9},{25,17},{2,26},{10... | collective-permute-start | bytes 36872 | tf_op jit(solution)/shard_map/ppermute | solution.py:29
  50.5 0.7 %convert_bitcast_fusion = bf16[1,48,1536]{2,1,0:T(8,128)(2,1)} fusion(f32[48,1536]{1,0:T(8,128)S(1)} %get-tuple-element.64), kind=kLoop, calls=%fused_computation | loop fusion | flops 73728 | bytes 442368 | tf_op jit(solution)/shard_map/broadcast_in_dim | solution.py:511
  51.2 2.3 %collective-permute-done.23 = f32[1,48,64]{2,1,0:T(8,128)S(1)} collective-permute-done((f32[1,48,64]{2,1,0:T(8,128)S(1)}, f32[1,48,64]{2,1,0:T(8,128)S(1)}, u32[]{:S(2)}, u32[]{:S(2)}) %collective-permute-start.23) | collective-permute-done | bytes 12320 | tf_op jit(solution)/shard_map/ppermute | solution.py:29
  53.5 0.6 %copy.14 = f32[1,48,64]{2,1,0:T(8,128)} copy(f32[1,48,64]{2,1,0:T(8,128)S(1)} %collective-permute-done.23) | data formatting | bytes 24576
  (58 shorter events, 4.9 us)
Async XLA Ops:
  0.6 15.7 %copy-start.1 = (bf16[1536,384]{1,0:T(8,128)(2,1)S(1)}, bf16[1536,384]{1,0:T(8,128)(2,1)}, u32[]{:S(2)}) copy-start(bf16[1536,384]{1,0:T(8,128)(2,1)} %w_own.3) | copy-start | bytes 3538948
  1.8 6.8 %collective-permute-start.4 = (bf16[256,384]{1,0:T(8,128)(2,1)S(1)}, bf16[256,384]{1,0:T(8,128)(2,1)S(1)}, u32[]{:S(2)}, u32[]{:S(2)}) collective-permute-start(bf16[256,384]{1,0:T(8,128)(2,1)S(1)} %get-tuple-element.66), channel_id=1, source_target_pairs={{0,1},{1,0},{2,3},{3,2},{4,5},{5,4},{6,7},{7,6},{8,9},{9,8},{10,11... | collective-permute-start | bytes 589832 | tf_op jit(solution)/shard_map/ppermute | solution.py:421
  3.9 11.9 %collective-permute-start.2 = (bf16[48,1536]{1,0:T(8,128)(2,1)}, bf16[48,1536]{1,0:T(8,128)(2,1)S(1)}, u32[]{:S(2)}, u32[]{:S(2)}) collective-permute-start(bf16[48,1536]{1,0:T(8,128)(2,1)} %bitcast.10), channel_id=1, source_target_pairs={{0,2},{1,3},{2,0},{3,1},{4,6},{5,7},{6,4},{7,5},{8,10},{9,11},{10,... | collective-permute-start | bytes 442376 | tf_op jit(solution)/shard_map/ppermute | solution.py:414
  5.2 11.6 %collective-permute-start = (bf16[48,1536]{1,0:T(8,128)(2,1)}, bf16[48,1536]{1,0:T(8,128)(2,1)S(1)}, u32[]{:S(2)}, u32[]{:S(2)}) collective-permute-start(bf16[48,1536]{1,0:T(8,128)(2,1)} %bitcast.11), channel_id=1, source_target_pairs={{0,4},{1,5},{2,6},{3,7},{4,0},{5,1},{6,2},{7,3},{8,12},{9,13},{10,... | collective-permute-start | bytes 442376 | tf_op jit(solution)/shard_map/ppermute | solution.py:414
  7.6 9.4 %collective-permute-start.1 = (bf16[48,1536]{1,0:T(8,128)(2,1)}, bf16[48,1536]{1,0:T(8,128)(2,1)S(1)}, u32[]{:S(2)}, u32[]{:S(2)}) collective-permute-start(bf16[48,1536]{1,0:T(8,128)(2,1)} %bitcast.12), channel_id=1, source_target_pairs={{0,6},{1,7},{2,4},{3,5},{4,2},{5,3},{6,0},{7,1},{8,14},{9,15},{10,... | collective-permute-start | bytes 442376 | tf_op jit(solution)/shard_map/ppermute | solution.py:414
  7.6 4.9 %collective-permute-start.3 = (bf16[256,384]{1,0:T(8,128)(2,1)S(1)}, bf16[256,384]{1,0:T(8,128)(2,1)S(1)}, u32[]{:S(2)}, u32[]{:S(2)}) collective-permute-start(bf16[256,384]{1,0:T(8,128)(2,1)S(1)} %get-tuple-element.67), channel_id=1, source_target_pairs={{0,1},{1,0},{2,3},{3,2},{4,5},{5,4},{6,7},{7,6},{8,9},{9,8},{10,11... | collective-permute-start | bytes 589832 | tf_op jit(solution)/shard_map/ppermute | solution.py:421
  8.6 6.4 %collective-permute-start.5 = (bf16[256,384]{1,0:T(8,128)(2,1)S(1)}, bf16[256,384]{1,0:T(8,128)(2,1)S(1)}, u32[]{:S(2)}, u32[]{:S(2)}) collective-permute-start(bf16[256,384]{1,0:T(8,128)(2,1)S(1)} %collective-permute-done.4.w_mine), channel_id=1, source_target_pairs={{0,16},{8,24},{16,0},{24,8},{1,17},{9,25},{17,1},{25,9},{2,18},{10... | collective-permute-start | bytes 589832 | tf_op jit(solution)/shard_map/ppermute | solution.py:427
  12.5 4.5 %collective-permute-start.7 = (bf16[256,384]{1,0:T(8,128)(2,1)S(1)}, bf16[256,384]{1,0:T(8,128)(2,1)S(1)}, u32[]{:S(2)}, u32[]{:S(2)}) collective-permute-start(bf16[256,384]{1,0:T(8,128)(2,1)S(1)} %collective-permute-done.3.w_last), channel_id=1, source_target_pairs={{0,8},{8,0},{16,24},{24,16},{1,9},{9,1},{17,25},{25,17},{2,10},{10... | collective-permute-start | bytes 589832 | tf_op jit(solution)/shard_map/ppermute | solution.py:424
  15.0 2.0 %collective-permute-start.6 = (bf16[256,384]{1,0:T(8,128)(2,1)S(1)}, bf16[256,384]{1,0:T(8,128)(2,1)S(1)}, u32[]{:S(2)}, u32[]{:S(2)}) collective-permute-start(bf16[256,384]{1,0:T(8,128)(2,1)S(1)} %collective-permute-done.4.w_mine), channel_id=1, source_target_pairs={{0,8},{8,0},{16,24},{24,16},{1,9},{9,1},{17,25},{25,17},{2,10},{10... | collective-permute-start | bytes 589832 | tf_op jit(solution)/shard_map/ppermute | solution.py:424
  15.9 1.4 %collective-permute-start.8 = (bf16[256,384]{1,0:T(8,128)(2,1)S(1)}, bf16[256,384]{1,0:T(8,128)(2,1)S(1)}, u32[]{:S(2)}, u32[]{:S(2)}) collective-permute-start(bf16[256,384]{1,0:T(8,128)(2,1)S(1)} %collective-permute-done.5.w_chip), channel_id=1, source_target_pairs={{0,8},{8,0},{16,24},{24,16},{1,9},{9,1},{17,25},{25,17},{2,10},{10... | collective-permute-start | bytes 589832 | tf_op jit(solution)/shard_map/ppermute | solution.py:424
  17.3 11.2 %copy-start.9 = (f32[2,1024]{1,0:T(2,128)S(1)}, f32[2,1024]{1,0:T(2,128)}, u32[]{:S(2)}) copy-start(f32[2,1024]{1,0:T(2,128)} %gains.3) | copy-start | bytes 24580
  18.6 8.2 %collective-permute-start.10 = (bf16[208,256]{1,0:T(8,128)(2,1)S(1)}, bf16[208,256]{1,0:T(8,128)(2,1)S(1)}, u32[]{:S(2)}, u32[]{:S(2)}) collective-permute-start(bf16[208,256]{1,0:T(8,128)(2,1)S(1)} %get-tuple-element.44), channel_id=1, source_target_pairs={{0,4},{1,5},{2,6},{3,7},{4,0},{5,1},{6,2},{7,3},{8,12},{9,13},{10,... | collective-permute-start | bytes 319496 | tf_op jit(solution)/shard_map/ppermute | solution.py:414
  23.1 5.5 %collective-permute-start.9 = (bf16[208,256]{1,0:T(8,128)(2,1)S(1)}, bf16[208,256]{1,0:T(8,128)(2,1)S(1)}, u32[]{:S(2)}, u32[]{:S(2)}) collective-permute-start(bf16[208,256]{1,0:T(8,128)(2,1)S(1)} %get-tuple-element.43), channel_id=1, source_target_pairs={{0,2},{1,3},{2,0},{3,1},{4,6},{5,7},{6,4},{7,5},{8,10},{9,11},{10,... | collective-permute-start | bytes 319496 | tf_op jit(solution)/shard_map/ppermute | solution.py:414
  23.1 2.5 %collective-permute-start.11 = (bf16[16,256]{1,0:T(8,128)(2,1)S(1)}, bf16[16,256]{1,0:T(8,128)(2,1)S(1)}, u32[]{:S(2)}, u32[]{:S(2)}) collective-permute-start(bf16[16,256]{1,0:T(8,128)(2,1)S(1)} %get-tuple-element.50.own_sums), channel_id=1, source_target_pairs={{0,1},{1,0},{2,4},{3,5},{4,2},{5,3},{6,7},{7,6},{8,9},{9,8},{10,12... | collective-permute-start | bytes 24584 | tf_op jit(solution)/shard_map/ppermute | solution.py:418
  23.7 22.2 %copy-start.11 = (f32[1,2,1536]{2,1,0:T(2,128)S(1)}, f32[1,2,1536]{2,1,0:T(2,128)}, u32[]{:S(2)}) copy-start(f32[1,2,1536]{2,1,0:T(2,128)} %param.17) | copy-start | bytes 36868
  28.5 17.4 %copy-start = (bf16[1024,1536]{1,0:T(8,128)(2,1)S(1)}, bf16[1024,1536]{1,0:T(8,128)(2,1)}, u32[]{:S(2)}) copy-start(bf16[1024,1536]{1,0:T(8,128)(2,1)} %w_out.3) | copy-start | bytes 9437188
  28.8 6.8 %collective-permute-start.15 = (bf16[192,512]{1,0:T(8,128)(2,1)S(1)}, bf16[192,512]{1,0:T(8,128)(2,1)S(1)}, u32[]{:S(2)}, u32[]{:S(2)}) collective-permute-start(bf16[192,512]{1,0:T(8,128)(2,1)S(1)} %get-tuple-element.49.a0), channel_id=1, source_target_pairs={{0,16},{8,24},{16,0},{24,8},{1,17},{9,25},{17,1},{25,9},{2,18},{10... | collective-permute-start | bytes 589832 | tf_op jit(solution)/shard_map/ppermute | solution.py:427
  30.1 5.5 %collective-permute-start.16 = (bf16[192,512]{1,0:T(8,128)(2,1)S(1)}, bf16[192,512]{1,0:T(8,128)(2,1)S(1)}, u32[]{:S(2)}, u32[]{:S(2)}) collective-permute-start(bf16[192,512]{1,0:T(8,128)(2,1)S(1)} %get-tuple-element.49.a0), channel_id=1, source_target_pairs={{0,1},{1,0},{2,3},{3,2},{4,5},{5,4},{6,7},{7,6},{8,9},{9,8},{10,11... | collective-permute-start | bytes 589832 | tf_op jit(solution)/shard_map/ppermute | solution.py:421
  30.1 7.8 %collective-permute-start.12 = (bf16[192,512]{1,0:T(8,128)(2,1)S(1)}, bf16[192,512]{1,0:T(8,128)(2,1)S(1)}, u32[]{:S(2)}, u32[]{:S(2)}) collective-permute-start(bf16[192,512]{1,0:T(8,128)(2,1)S(1)} %get-tuple-element.49.a0), channel_id=1, source_target_pairs={{0,17},{1,16},{2,19},{3,18},{4,21},{5,20},{6,23},{7,22},{8,25},{9,... | collective-permute-start | bytes 589832 | tf_op jit(solution)/shard_map/ppermute | solution.py:436
  31.5 4.3 %collective-permute-start.13 = (bf16[16,256]{1,0:T(8,128)(2,1)S(1)}, bf16[16,256]{1,0:T(8,128)(2,1)S(1)}, u32[]{:S(2)}, u32[]{:S(2)}) collective-permute-start(bf16[16,256]{1,0:T(8,128)(2,1)S(1)} %get-tuple-element.50.own_sums), channel_id=1, source_target_pairs={{0,6},{1,7},{2,4},{3,5},{4,2},{5,3},{6,0},{7,1},{8,14},{9,15},{10,... | collective-permute-start | bytes 24584 | tf_op jit(solution)/shard_map/ppermute | solution.py:414
  31.5 10.6 %collective-permute-start.14 = (bf16[192,512]{1,0:T(8,128)(2,1)S(1)}, bf16[192,512]{1,0:T(8,128)(2,1)S(1)}, u32[]{:S(2)}, u32[]{:S(2)}) collective-permute-start(bf16[192,512]{1,0:T(8,128)(2,1)S(1)} %get-tuple-element.49.a0), channel_id=1, source_target_pairs={{0,8},{8,0},{16,24},{24,16},{1,9},{9,1},{17,25},{25,17},{2,10},{10... | collective-permute-start | bytes 589832 | tf_op jit(solution)/shard_map/ppermute | solution.py:424
  37.9 4.2 %collective-permute-start.17 = (bf16[192,512]{1,0:T(8,128)(2,1)S(1)}, bf16[192,512]{1,0:T(8,128)(2,1)S(1)}, u32[]{:S(2)}, u32[]{:S(2)}) collective-permute-start(bf16[192,512]{1,0:T(8,128)(2,1)S(1)} %collective-permute-done.16.a1), channel_id=1, source_target_pairs={{0,8},{8,0},{16,24},{24,16},{1,9},{9,1},{17,25},{25,17},{2,10},{10... | collective-permute-start | bytes 589832 | tf_op jit(solution)/shard_map/ppermute | solution.py:424
  40.4 1.8 %collective-permute-start.18 = (bf16[192,512]{1,0:T(8,128)(2,1)S(1)}, bf16[192,512]{1,0:T(8,128)(2,1)S(1)}, u32[]{:S(2)}, u32[]{:S(2)}) collective-permute-start(bf16[192,512]{1,0:T(8,128)(2,1)S(1)} %collective-permute-done.15.c0), channel_id=1, source_target_pairs={{0,8},{8,0},{16,24},{24,16},{1,9},{9,1},{17,25},{25,17},{2,10},{10... | collective-permute-start | bytes 589832 | tf_op jit(solution)/shard_map/ppermute | solution.py:424
  40.4 1.8 %collective-permute-start.19 = (bf16[192,512]{1,0:T(8,128)(2,1)S(1)}, bf16[192,512]{1,0:T(8,128)(2,1)S(1)}, u32[]{:S(2)}, u32[]{:S(2)}) collective-permute-start(bf16[192,512]{1,0:T(8,128)(2,1)S(1)} %collective-permute-done.12.c1), channel_id=1, source_target_pairs={{0,8},{8,0},{16,24},{24,16},{1,9},{9,1},{17,25},{25,17},{2,10},{10... | collective-permute-start | bytes 589832 | tf_op jit(solution)/shard_map/ppermute | solution.py:424
  41.1 4.8 %copy-start.3 = (bf16[1,48,1536]{2,1,0:T(8,128)(2,1)S(1)}, bf16[1,48,1536]{2,1,0:T(8,128)(2,1)}, u32[]{:S(2)}) copy-start(bf16[1,48,1536]{2,1,0:T(8,128)(2,1)} %param.10) | copy-start | bytes 442372
  41.1 4.8 %copy-start.6 = (f32[3,1536]{1,0:T(4,128)S(1)}, f32[3,1536]{1,0:T(4,128)}, u32[]{:S(2)}) copy-start(f32[3,1536]{1,0:T(4,128)} %block_in.1) | copy-start | bytes 55300
  41.2 4.8 %copy-start.8 = (f32[1,3,1536]{2,0,1:T(1,128)S(1)}, f32[1,3,1536]{2,0,1:T(1,128)}, u32[]{:S(2)}) copy-start(f32[1,3,1536]{2,0,1:T(1,128)} %param.12) | copy-start | bytes 55300
  43.2 3.8 %collective-permute-start.20 = (bf16[48,256]{1,0:T(8,128)(2,1)S(1)}, bf16[48,256]{1,0:T(8,128)(2,1)S(1)}, u32[]{:S(2)}, u32[]{:S(2)}) collective-permute-start(bf16[48,256]{1,0:T(8,128)(2,1)S(1)} %get-tuple-element.57), channel_id=1, source_target_pairs={{0,4},{1,5},{2,6},{3,7},{4,0},{5,1},{6,2},{7,3},{8,12},{9,13},{10,... | collective-permute-start | bytes 73736 | tf_op jit(solution)/shard_map/ppermute | solution.py:414
  43.3 4.7 %collective-permute-start.21 = (bf16[48,256]{1,0:T(8,128)(2,1)S(1)}, bf16[48,256]{1,0:T(8,128)(2,1)S(1)}, u32[]{:S(2)}, u32[]{:S(2)}) collective-permute-start(bf16[48,256]{1,0:T(8,128)(2,1)S(1)} %get-tuple-element.58), channel_id=1, source_target_pairs={{0,6},{1,7},{2,4},{3,5},{4,2},{5,3},{6,0},{7,1},{8,14},{9,15},{10,... | collective-permute-start | bytes 73736 | tf_op jit(solution)/shard_map/ppermute | solution.py:414
  44.9 3.5 %collective-permute-start.22 = (bf16[48,256]{1,0:T(8,128)(2,1)S(1)}, bf16[48,256]{1,0:T(8,128)(2,1)S(1)}, u32[]{:S(2)}, u32[]{:S(2)}) collective-permute-start(bf16[48,256]{1,0:T(8,128)(2,1)S(1)} %get-tuple-element.59), channel_id=1, source_target_pairs={{0,2},{1,3},{2,0},{3,1},{4,6},{5,7},{6,4},{7,5},{8,10},{9,11},{10,... | collective-permute-start | bytes 73736 | tf_op jit(solution)/shard_map/ppermute | solution.py:414
  46.0 2.4 %copy-start.4 = (bf16[1536,64]{0,1:T(8,128)(2,1)S(1)}, bf16[1536,64]{0,1:T(8,128)(2,1)}, u32[]{:S(2)}) copy-start(bf16[1536,64]{0,1:T(8,128)(2,1)} %param.18) | copy-start | bytes 589828
  49.4 4.1 %collective-permute-start.23 = (f32[1,48,64]{2,1,0:T(8,128)S(1)}, f32[1,48,64]{2,1,0:T(8,128)S(1)}, u32[]{:S(2)}, u32[]{:S(2)}) collective-permute-start(f32[1,48,64]{2,1,0:T(8,128)S(1)} %bitcast.20), channel_id=1, source_target_pairs={{0,24},{8,0},{16,8},{24,16},{1,25},{9,1},{17,9},{25,17},{2,26},{10... | collective-permute-start | bytes 36872 | tf_op jit(solution)/shard_map/ppermute | solution.py:29
  (4 other events, 4.8 us)
